TPU v7x, 32 devices: a whole 2x2x4 slice. The times are simulated.
32 devices in a mesh: depth: 2 (over core), pos: 16 (over z, y, x).
Axes of the slice: x: 2, y: 2, z: 4, core: 2. Of those that a mesh axis runs over, the one named last changes fastest.
Arguments:
- object_field: bfloat16 [2, 2, 2048, 4096], P('depth', None, None, 'pos'), may hold values from -4.1875 to 4.1875
- probe: bfloat16 [4, 2, 256, 256], replicated, may hold values from -4.1875 to 4.1875
- prop_phase: float32 [256, 256], replicated, may hold values from -3.140625 to 3.140625
- measured: float32 [32, 256, 256], P('pos'), may hold values from 0 to 8
- positions: int32 [32, 2], replicated, may hold values from 0 to 3840, as said below
Outputs:
- object_grad: bfloat16 [2, 2, 2048, 4096], P('depth', None, None, 'pos')
Inputs may be any that keep to these rules, and one draw needn't show every extreme that they name: `positions`: row r holds (row offset, column offset). For the block b = r // 2, column offsets lie from b * 256 to b * 256 + 255; in the last block they equal b * 256. Row offsets lie from 0 to 1792. Row 0 is (0, 0).
All inputs are finite; a program needn't handle non-finite values.
Results may differ from a plain program's by a relative error of at most 0.019.
Values may be sent and summed in bfloat16 or wider, within the bound.
No kernel may reach another device: no remote copies, remote signals or barrier semaphores. Data moves between devices by JAX's collectives and lax.ppermute only.
A program may use at most 64 MiB of HBM per device.

v0:
```python
import math

import jax
import jax.numpy as jnp
from jax import lax
from jax.sharding import PartitionSpec as P


def shifted(shard, axis, by):
    devices = lax.axis_size(axis)
    pairs = [(i, i + by) for i in range(devices) if 0 <= i + by < devices]
    return lax.ppermute(shard, axis, pairs)


def dft_tables(frame):
    ramp = jnp.arange(frame, dtype=jnp.int32)
    phases = ramp[:, None] * ramp[None, :] % frame
    angles = phases.astype(jnp.float32) * (2.0 * math.pi / frame)
    factor = 1.0 / math.sqrt(frame)
    return (
        (jnp.cos(angles) * factor).astype(jnp.bfloat16),
        (-jnp.sin(angles) * factor).astype(jnp.bfloat16),
    )


def left_mult(table, values):
    return jnp.einsum("ab,nmbc->nmac", table, values, preferred_element_type=jnp.float32)


def right_mult(values, table):
    return jnp.einsum("nmab,bc->nmac", values, table, preferred_element_type=jnp.float32)


def transform(real_in, imag_in, fourier_table_real, fourier_table_imaginary):
    in_r = real_in.astype(jnp.bfloat16)
    in_i = imag_in.astype(jnp.bfloat16)
    mid_r = (left_mult(fourier_table_real, in_r) - left_mult(fourier_table_imaginary, in_i)).astype(
        jnp.bfloat16
    )
    mid_i = (left_mult(fourier_table_real, in_i) + left_mult(fourier_table_imaginary, in_r)).astype(
        jnp.bfloat16
    )
    out_r = right_mult(mid_r, fourier_table_real) - right_mult(mid_i, fourier_table_imaginary)
    out_i = right_mult(mid_r, fourier_table_imaginary) + right_mult(mid_i, fourier_table_real)
    return (out_r, out_i)


def forward_front(
    patch_r, patch_i, probe, kern_r, kern_i, fourier_table_real, fourier_table_imaginary
):
    obj_r = patch_r.astype(jnp.float32)[:, None]
    obj_i = patch_i.astype(jnp.float32)[:, None]
    probe_r = probe[:, 0].astype(jnp.float32)[None]
    probe_i = probe[:, 1].astype(jnp.float32)[None]
    wave_r = probe_r * obj_r - probe_i * obj_i
    wave_i = probe_r * obj_i + probe_i * obj_r
    spectrum_real, spectrum_imaginary = transform(
        wave_r, wave_i, fourier_table_real, fourier_table_imaginary
    )
    return jnp.stack(
        [
            (spectrum_real * kern_r - spectrum_imaginary * kern_i).astype(jnp.bfloat16),
            (spectrum_real * kern_i + spectrum_imaginary * kern_r).astype(jnp.bfloat16),
        ]
    )


def backward_tail(spectra, patch_r, patch_i, measured, fourier_table_real, fourier_table_imaginary):
    conj_i = -fourier_table_imaginary
    wave_r, wave_i = transform(spectra[0], spectra[1], fourier_table_real, conj_i)
    obj_r = patch_r.astype(jnp.float32)[:, None]
    obj_i = patch_i.astype(jnp.float32)[:, None]
    exit_r = wave_r * obj_r - wave_i * obj_i
    exit_i = wave_r * obj_i + wave_i * obj_r
    far_r, far_i = transform(exit_r, exit_i, fourier_table_real, fourier_table_imaginary)
    intensity = jnp.sum(far_r * far_r + far_i * far_i, axis=1)
    weight = ((intensity - measured) * 0.125)[:, None]
    back_r, back_i = transform(weight * far_r, weight * far_i, fourier_table_real, conj_i)
    grad_r = jnp.sum(wave_r * back_r + wave_i * back_i, axis=1)
    grad_i = jnp.sum(wave_r * back_i - wave_i * back_r, axis=1)
    adj_r = obj_r * back_r + obj_i * back_i
    adj_i = obj_r * back_i - obj_i * back_r
    out_r, out_i = transform(adj_r, adj_i, fourier_table_real, fourier_table_imaginary)
    return (
        jnp.stack([out_r.astype(jnp.bfloat16), out_i.astype(jnp.bfloat16)]),
        jnp.stack([grad_r, grad_i]),
    )


def back_front(adjoint, probe, kern_r, kern_i, fourier_table_real, fourier_table_imaginary):
    cot_r = adjoint[0].astype(jnp.float32)
    cot_i = adjoint[1].astype(jnp.float32)
    turn_r = kern_r * cot_r + kern_i * cot_i
    turn_i = kern_r * cot_i - kern_i * cot_r
    wave_r, wave_i = transform(turn_r, turn_i, fourier_table_real, -fourier_table_imaginary)
    probe_r = probe[:, 0].astype(jnp.float32)[None]
    probe_i = probe[:, 1].astype(jnp.float32)[None]
    grad_r = jnp.sum(probe_r * wave_r + probe_i * wave_i, axis=1)
    grad_i = jnp.sum(probe_r * wave_i - probe_i * wave_r, axis=1)
    return jnp.stack([grad_r, grad_i])


def local(object_field, probe, prop_phase, measured, positions):
    frame = probe.shape[-1]
    n_modes = probe.shape[0]
    count = measured.shape[0]
    fourier_table_real, fourier_table_imaginary = dft_tables(frame)
    kern_r = jnp.cos(prop_phase)
    kern_i = jnp.sin(prop_phase)
    section_idx = lax.axis_index("depth")
    pos_index = lax.axis_index("pos")
    my_positions = lax.dynamic_slice_in_dim(positions, pos_index * count, count, 0)
    left_index = jnp.maximum(pos_index - 1, 0)
    left_positions = lax.dynamic_slice_in_dim(positions, left_index * count, count, 0)
    rows_mine = my_positions[:, 0]
    cols_mine = my_positions[:, 1] - pos_index * frame
    my_band = object_field[0]
    height = my_band.shape[1]
    outgoing = jnp.stack(
        [
            lax.dynamic_slice(my_band, (0, left_positions[which_pos, 0], 0), (2, frame, frame))
            for which_pos in range(count)
        ]
    )
    incoming = shifted(outgoing, "pos", -1)
    pieces = []
    for which_pos in range(count):
        own_rows = lax.dynamic_slice(my_band, (0, rows_mine[which_pos], 0), (2, frame, frame))
        joined = jnp.concatenate([own_rows, incoming[which_pos]], axis=2)
        pieces.append(lax.dynamic_slice(joined, (0, 0, cols_mine[which_pos]), (2, frame, frame)))
    patches = jnp.stack(pieces)
    patch_r = patches[:, 0]
    patch_i = patches[:, 1]

    def spec_zeros(rows_n):
        return jnp.zeros((2, rows_n, n_modes, frame, frame), jnp.bfloat16)

    def grad_zeros(rows_n):
        return jnp.zeros((2, rows_n, frame, frame), jnp.float32)

    def front_pass():
        return forward_front(
            patch_r, patch_i, probe, kern_r, kern_i, fourier_table_real, fourier_table_imaginary
        )

    spectra = lax.cond(section_idx == 0, front_pass, lambda: spec_zeros(count))
    arrived = shifted(spectra, "depth", 1)

    def end_pass():
        return backward_tail(
            arrived, patch_r, patch_i, measured, fourier_table_real, fourier_table_imaginary
        )

    adjoint, grad_end = lax.cond(
        section_idx == 1, end_pass, lambda: (spec_zeros(count), grad_zeros(count))
    )
    returned = shifted(adjoint, "depth", -1)

    def front_back():
        return back_front(
            returned, probe, kern_r, kern_i, fourier_table_real, fourier_table_imaginary
        )

    grads = lax.cond(section_idx == 0, front_back, lambda: grad_end)
    total = jnp.zeros((2, height, frame), jnp.float32)
    spill = []
    for which_pos in range(count):
        padded = jnp.zeros((2, frame, 2 * frame), jnp.float32)
        padded = lax.dynamic_update_slice(padded, grads[:, which_pos], (0, 0, cols_mine[which_pos]))
        corner = (0, rows_mine[which_pos], 0)
        current = lax.dynamic_slice(total, corner, (2, frame, frame))
        total = lax.dynamic_update_slice(total, current + padded[:, :, :frame], corner)
        spill.append(padded[:, :, frame:])
    from_left = shifted(jnp.stack(spill), "pos", 1)
    for which_pos in range(count):
        corner = (0, left_positions[which_pos, 0], 0)
        current = lax.dynamic_slice(total, corner, (2, frame, frame))
        total = lax.dynamic_update_slice(total, current + from_left[which_pos], corner)
    return total.astype(jnp.bfloat16)[None]


def solution(mesh):
    placed = (P("depth", None, None, "pos"), P(), P(), P("pos", None, None), P())
    return jax.shard_map(
        local, mesh=mesh, in_specs=placed, out_specs=P("depth", None, None, "pos"), check_vma=False
    )
```

profile of v0, /device:TPU:24, one launch (start us, length us, event | category | flops | bytes accessed | tf_op | source)
XLA Modules:
  0.0 144.3 jit_solution(4184718272255313668)
XLA Ops:
  0.0 0.8 constant_dynamic-slice_fusion.2
  0.8 0.6 fusion.152
  9.0 1.5 %dynamic-slice_bitcast_fusion = (bf16[2,256,256]{2,1,0:T(8,128)(2,1)S(1)}, bf16[1,2,256,256]{3,2,1,0:T(8,128)(2,1)S(1)}, bf16[2,256,256]{2,1,0:T(8,128)(2,1)S(1)}, bf16[1,2,256,256]{3,2,1,0:T(8,128)(2,1)S(1)}) fusion(bf16[1,2,2048,256]{3,2,1,0:T(8,128)(2,1)} %param.11, s32[]{:T(128)S(6)} %select_n.140, s32[]{:T(128)S(6)} %select_n.137, s32[]{:T(128)S(6)} %select_n.135, ...), kind=kLoop, calls=%fused_computation.222 | loop fusion | bytes 2097168 | tf_op jit(solution)/shard_map/dynamic_slice | solution.py:128
  10.6 4.2 %collective-permute-start = (bf16[2,2,256,256]{3,2,1,0:T(8,128)(2,1)S(1)}, bf16[2,2,256,256]{3,2,1,0:T(8,128)(2,1)S(1)}, u32[]{:S(2)}, u32[]{:S(2)}) collective-permute-start(bf16[2,2,256,256]{3,2,1,0:T(8,128)(2,1)S(1)} %pad_maximum_fusion.5), channel_id=1, source_target_pairs={{1,0},{2,1},{3,2},{4,3},{5,4},{6,5},{7,6},{8,7},{9,8},{10,9},{11,1... | collective-permute-start | bytes 1572872 | tf_op jit(solution)/shard_map/ppermute | solution.py:12
  19.4 1.1 multiply_convert_fusion.6
  20.5 1.0 fusion.151
  21.5 4.6 %collective-permute-done = bf16[2,2,256,256]{3,2,1,0:T(8,128)(2,1)S(1)} collective-permute-done((bf16[2,2,256,256]{3,2,1,0:T(8,128)(2,1)S(1)}, bf16[2,2,256,256]{3,2,1,0:T(8,128)(2,1)S(1)}, u32[]{:S(2)}, u32[]{:S(2)}) %collective-permute-start) | collective-permute-done | bytes 524320 | tf_op jit(solution)/shard_map/ppermute | solution.py:12
  26.7 0.8 fusion.147
  27.5 19.5 %conditional.3 = (bf16[2,2,4,256,256]{4,3,2,1,0:T(8,128)(2,1)S(1)}) conditional(s32[]{:T(128)} %convert_element_type.399, () %tuple.48, (bf16[4,2,256,256]{3,2,1,0:T(8,128)(2,1)}, bf16[2,256,256]{2,1,0:T(8,128)(2,1)}, bf16[2,256,256]{2,1,0:T(8,128)(2,1)}, bf16[256,256]{1,0:T(8,128)(2,1)S(1)}, bf16[256,256]{1,0:T(8,128)(2,1)S(1)}, ...), branch_computations={%region_0.1_spmd, %region_1.2_spmd} | conditional | flops 2165047296 | bytes 65011776 | solution.py:146
  27.5 2.3 %copy.45 = bf16[4,2,256,256]{2,3,0,1:T(8,128)(2,1)} copy(bf16[4,2,256,256]{3,2,1,0:T(8,128)(2,1)} %get-tuple-element.194) | data formatting | bytes 2097152 | tf_op jit(solution)/shard_map
  29.8 1.4 fusion.23
  31.2 1.8 %copy.46 = bf16[2,256,256]{1,2,0:T(8,128)(2,1)} copy(bf16[2,256,256]{2,1,0:T(8,128)(2,1)} %get-tuple-element.195) | data formatting | bytes 524288 | tf_op jit(solution)/shard_map
  32.9 1.0 convert_element_type.95
  33.9 1.8 %copy.47 = bf16[2,256,256]{1,2,0:T(8,128)(2,1)} copy(bf16[2,256,256]{2,1,0:T(8,128)(2,1)} %get-tuple-element.196) | data formatting | bytes 524288 | tf_op jit(solution)/shard_map
  35.7 1.0 convert_element_type.98
  37.3 0.6 fusion.1
  38.5 0.7 fusion
  39.8 1.8 %convolution_add_fusion = f32[2,4,256,256]{3,2,1,0:T(8,128)} fusion(f32[2,4,256,256]{3,2,1,0:T(8,128)S(1)} %fusion.25, bf16[2,4,256,256]{2,3,1,0:T(8,128)(2,1)S(1)} %fusion.1, bf16[256,256]{1,0:T(8,128)(2,1)S(1)} %get-tuple-element.138), kind=kOutput, calls=%fused_computation.7 | convolution fusion | flops 268959744 | bytes 5373952 | tf_op jit(solution)/shard_map/cond/branch_1_fun/nmab,bc->nmac/dot_general | solution.py:31
  41.6 1.8 %fusion.30 = f32[2,4,256,256]{3,2,1,0:T(8,128)} fusion(bf16[2,4,256,256]{2,3,1,0:T(8,128)(2,1)S(1)} %fusion, bf16[256,256]{1,0:T(8,128)(2,1)S(1)} %get-tuple-element.138), kind=kOutput, calls=%fused_computation.41 | convolution fusion | flops 268435456 | bytes 3276800 | tf_op jit(solution)/shard_map/cond/branch_1_fun/nmab,bc->nmac/dot_general | solution.py:31
  43.7 3.1 %fusion.4 = (bf16[1,2,4,256,256]{4,3,2,1,0:T(8,128)(2,1)S(1)}, bf16[1,2,4,256,256]{4,3,2,1,0:T(8,128)(2,1)S(1)}) fusion(f32[2,4,256,256]{3,2,1,0:T(8,128)} %convolution_add_fusion, f32[256,256]{1,0:T(8,128)S(1)} %copy.49, f32[256,256]{1,0:T(8,128)S(1)} %copy.48, f32[2,4,256,256]{3,2,1,0:T(8,128)} %fusion.30, bf16[2,4,256,256]{2,3,1,0:T(8,128)(2,1)S(1)} %copy-done.1, ...), kind=kOutput, calls=%fused_computation.13 | convolution fusion | flops 273154048 | bytes 7995392 | tf_op jit(solution)/shard_map/cond/branch_1_fun/nmab,bc->nmac/dot_general | solution.py:31
  47.0 2.3 %copy.50 = bf16[2,2,4,256,256]{3,4,2,1,0:T(8,128)(2,1)} copy(bf16[2,2,4,256,256]{4,3,2,1,0:T(8,128)(2,1)S(1)} %get-tuple-element.270) | data formatting | bytes 4194304 | tf_op jit(solution)/shard_map/cond | solution.py:146
  49.4 1.4 collective-permute-start.1
  50.8 3.8 %collective-permute-done.1 = bf16[2,2,4,256,256]{3,4,2,1,0:T(8,128)(2,1)S(1)} collective-permute-done((bf16[2,2,4,256,256]{3,4,2,1,0:T(8,128)(2,1)}, bf16[2,2,4,256,256]{3,4,2,1,0:T(8,128)(2,1)S(1)}, u32[]{:S(2)}, u32[]{:S(2)}) %collective-permute-start.1) | collective-permute-done | bytes 2097184 | tf_op jit(solution)/shard_map/ppermute | solution.py:12
  54.6 1.8 %conditional.4 = (bf16[2,2,4,256,256]{4,3,2,1,0:T(8,128)(2,1)}, f32[2,2,256,256]{3,2,1,0:T(8,128)S(1)}) conditional(s32[]{:T(128)} %convert_element_type.400, () %tuple.47, (bf16[2,256,256]{2,1,0:T(8,128)(2,1)}, bf16[2,2,4,256,256]{3,4,2,1,0:T(8,128)(2,1)S(1)}, bf16[256,256]{1,0:T(8,128)(2,1)S(1)}, bf16[256,256]{1,0:T(8,128)(2,1)S(1)}, ...), branch_computations={%region_2.3_spmd, %region_3.7_spmd} | conditional | flops 8624406528 | bytes 162005040 | solution.py:154
  54.6 1.5 %broadcast.29 = bf16[2,2,4,256,256]{4,3,2,1,0:T(8,128)(2,1)} broadcast(bf16[]{:T(256)} %constant.23.clone), dimensions={} | broadcast | bytes 2097154 | tf_op jit(solution)/shard_map/broadcast.9
  56.5 1.0 copy-done.3
  57.4 4.3 %copy.51 = bf16[2,2,4,256,256]{3,4,2,1,0:T(8,128)(2,1)} copy(bf16[2,2,4,256,256]{4,3,2,1,0:T(8,128)(2,1)} %get-tuple-element.191) | data formatting | bytes 4194304 | tf_op jit(solution)/shard_map/cond | solution.py:154
  61.7 1.3 collective-permute-start.2
  63.0 23.2 %collective-permute-done.2 = bf16[2,2,4,256,256]{3,4,2,1,0:T(8,128)(2,1)S(1)} collective-permute-done((bf16[2,2,4,256,256]{3,4,2,1,0:T(8,128)(2,1)}, bf16[2,2,4,256,256]{3,4,2,1,0:T(8,128)(2,1)S(1)}, u32[]{:S(2)}, u32[]{:S(2)}) %collective-permute-start.2) | collective-permute-done | bytes 2097184 | tf_op jit(solution)/shard_map/ppermute | solution.py:12
  86.2 5.6 %conditional.5 = (f32[2,2,256,256]{3,2,1,0:T(8,128)S(1)}) conditional(s32[]{:T(128)} %convert_element_type.399, f32[2,2,256,256]{3,2,1,0:T(8,128)S(1)} %copy-done.4, (bf16[4,2,256,256]{3,2,1,0:T(8,128)(2,1)S(1)}, f32[256,256]{0,1:T(8,128)S(1)}, bf16[2,2,4,256,256]{3,4,2,1,0:T(8,128)(2,1)S(1)}, f32[256,256]{0,1:T(8,128)S(1)}, ...), branch_computations={%region_7.8_spmd, %region_8.11_spmd} | conditional | flops 2168193024 | bytes 47185928 | solution.py:164
  86.2 0.6 fusion.126
  86.8 0.7 fusion.112
  88.0 0.6 fusion.121
  88.7 0.7 fusion.113
  90.5 1.2 add_reduce_fusion.2
  92.0 3.7 %dynamic_update_slice.18 = f32[2,256,512]{2,1,0:T(8,128)S(1)} dynamic-update-slice(f32[2,256,512]{2,1,0:T(8,128)S(1)} %broadcast.35.clone, f32[2,256,256]{2,1,0:T(8,128)S(1)} %get-tuple-element.247, s32[]{:T(128)} %constant.50.clone.1, s32[]{:T(128)} %constant.50.clone.1, s32[]{:T(128)S(6)} %select_n.139) | dynamic-update-slice | bytes 1048580 | tf_op jit(solution)/shard_map/dynamic_update_slice | solution.py:169
  95.8 2.2 %broadcast_in_dim.4 = f32[2,2048,256]{2,1,0:T(8,128)} broadcast(f32[]{:T(128)} %constant.47.clone.1), dimensions={} | broadcast | bytes 4194308 | tf_op jit(solution)/shard_map/broadcast_in_dim | solution.py:165
  98.0 3.5 %dynamic_update_slice.19 = f32[2,2048,256]{2,1,0:T(8,128)} dynamic-update-slice(f32[2,2048,256]{2,1,0:T(8,128)} %broadcast_in_dim.4, f32[2,256,256]{2,1,0:T(8,128)S(1)} %get-tuple-element.243, s32[]{:T(128)} %constant.50.clone.1, s32[]{:T(128)S(6)} %select_n.135, s32[]{:T(128)} %constant.50.clone.1) | dynamic-update-slice | bytes 1048580 | tf_op jit(solution)/shard_map/dynamic_update_slice | solution.py:172
  101.7 3.7 %dynamic_update_slice.20 = f32[2,256,512]{2,1,0:T(8,128)S(1)} dynamic-update-slice(f32[2,256,512]{2,1,0:T(8,128)S(1)} %broadcast.35.clone.1, f32[2,256,256]{2,1,0:T(8,128)S(1)} %get-tuple-element.246, s32[]{:T(128)} %constant.50.clone.1, s32[]{:T(128)} %constant.50.clone.1, s32[]{:T(128)S(6)} %select_n.141) | dynamic-update-slice | bytes 1048580 | tf_op jit(solution)/shard_map/dynamic_update_slice | solution.py:169
  105.3 1.2 slice_bitcast_fusion.6
  106.6 5.1 %collective-permute-start.3 = (f32[2,2,256,256]{3,2,1,0:T(8,128)S(1)}, f32[2,2,256,256]{3,2,1,0:T(8,128)S(1)}, u32[]{:S(2)}, u32[]{:S(2)}) collective-permute-start(f32[2,2,256,256]{3,2,1,0:T(8,128)S(1)} %pad_maximum_fusion.4), channel_id=1, source_target_pairs={{0,1},{1,2},{2,3},{3,4},{4,5},{5,6},{6,7},{7,8},{8,9},{9,10},{10,1... | collective-permute-start | bytes 3145736 | tf_op jit(solution)/shard_map/ppermute | solution.py:12
  111.7 3.5 %dynamic_update_slice.21 = f32[2,2048,256]{2,1,0:T(8,128)} dynamic-update-slice(f32[2,2048,256]{2,1,0:T(8,128)} %dynamic_update_slice.19, f32[2,256,256]{2,1,0:T(8,128)S(1)} %get-tuple-element.245, s32[]{:T(128)} %constant.50.clone.1, s32[]{:T(128)S(6)} %select_n.140, s32[]{:T(128)} %constant.50.clone.1) | dynamic-update-slice | bytes 1048580 | tf_op jit(solution)/shard_map/dynamic_update_slice | solution.py:172
  115.2 16.2 %collective-permute-done.3 = f32[2,2,256,256]{3,2,1,0:T(8,128)S(1)} collective-permute-done((f32[2,2,256,256]{3,2,1,0:T(8,128)S(1)}, f32[2,2,256,256]{3,2,1,0:T(8,128)S(1)}, u32[]{:S(2)}, u32[]{:S(2)}) %collective-permute-start.3) | collective-permute-done | bytes 1048608 | tf_op jit(solution)/shard_map/ppermute | solution.py:12
  131.3 1.1 fusion.137
  132.4 3.5 %dynamic_update_slice.22 = f32[2,2048,256]{2,1,0:T(8,128)} dynamic-update-slice(f32[2,2048,256]{2,1,0:T(8,128)} %dynamic_update_slice.21, f32[2,256,256]{2,1,0:T(8,128)S(1)} %fusion.137, s32[]{:T(128)} %constant.50.clone.1, s32[]{:T(128)S(6)} %select_n.137, s32[]{:T(128)} %constant.50.clone.1) | dynamic-update-slice | bytes 1048580 | tf_op jit(solution)/shard_map/dynamic_update_slice | solution.py:178
  136.0 1.1 fusion.136
  137.1 3.5 %dynamic_update_slice.23 = f32[2,2048,256]{2,1,0:T(8,128)} dynamic-update-slice(f32[2,2048,256]{2,1,0:T(8,128)} %dynamic_update_slice.22, f32[2,256,256]{2,1,0:T(8,128)S(1)} %fusion.136, s32[]{:T(128)} %constant.50.clone.1, s32[]{:T(128)S(6)} %select_n.138, s32[]{:T(128)} %constant.50.clone.1) | dynamic-update-slice | bytes 1048580 | tf_op jit(solution)/shard_map/dynamic_update_slice | solution.py:178
  140.6 3.7 %convert_bitcast_fusion = bf16[1,2,2048,256]{3,2,1,0:T(8,128)(2,1)} fusion(f32[2,2048,256]{2,1,0:T(8,128)} %dynamic_update_slice.23), kind=kLoop, calls=%fused_computation.184 | loop fusion | flops 1048576 | bytes 6291456 | tf_op jit(solution)/shard_map/broadcast_in_dim | solution.py:179
  (37 shorter events, 5.8 us)
Async XLA Ops:
  0.0 18.0 %copy-start.7 = (f32[256,256]{1,0:T(8,128)S(1)}, f32[256,256]{1,0:T(8,128)}, u32[]{:S(2)}) copy-start(f32[256,256]{1,0:T(8,128)} %param.13) | copy-start | bytes 786436
  10.6 15.6 %collective-permute-start = (bf16[2,2,256,256]{3,2,1,0:T(8,128)(2,1)S(1)}, bf16[2,2,256,256]{3,2,1,0:T(8,128)(2,1)S(1)}, u32[]{:S(2)}, u32[]{:S(2)}) collective-permute-start(bf16[2,2,256,256]{3,2,1,0:T(8,128)(2,1)S(1)} %pad_maximum_fusion.5), channel_id=1, source_target_pairs={{1,0},{2,1},{3,2},{4,3},{5,4},{6,5},{7,6},{8,7},{9,8},{10,9},{11,1... | collective-permute-start | bytes 1572872 | tf_op jit(solution)/shard_map/ppermute | solution.py:12
  37.9 1.8 %copy-start = (bf16[2,4,256,256]{2,3,1,0:T(8,128)(2,1)}, bf16[2,4,256,256]{2,3,1,0:T(8,128)(2,1)S(1)}, u32[]{:S(2)}) copy-start(bf16[2,4,256,256]{2,3,1,0:T(8,128)(2,1)S(1)} %fusion.1) | copy-start | bytes 3145732 | tf_op jit(solution)/shard_map/cond
  41.6 2.1 %copy-start.1 = (bf16[2,4,256,256]{2,3,1,0:T(8,128)(2,1)S(1)}, bf16[2,4,256,256]{2,3,1,0:T(8,128)(2,1)}, u32[]{:S(2)}) copy-start(bf16[2,4,256,256]{2,3,1,0:T(8,128)(2,1)} %copy-done) | copy-start | bytes 3145732 | tf_op jit(solution)/shard_map/cond
  47.0 7.6 %copy-start.5 = (bf16[2,256,256]{2,1,0:T(8,128)(2,1)S(1)}, bf16[2,256,256]{2,1,0:T(8,128)(2,1)}, u32[]{:S(2)}) copy-start(bf16[2,256,256]{2,1,0:T(8,128)(2,1)} %get-tuple-element.248) | copy-start | bytes 786436
  49.4 5.3 %collective-permute-start.1 = (bf16[2,2,4,256,256]{3,4,2,1,0:T(8,128)(2,1)}, bf16[2,2,4,256,256]{3,4,2,1,0:T(8,128)(2,1)S(1)}, u32[]{:S(2)}, u32[]{:S(2)}) collective-permute-start(bf16[2,2,4,256,256]{3,4,2,1,0:T(8,128)(2,1)} %copy.50), channel_id=1, source_target_pairs={{0,16},{1,17},{2,18},{3,19},{4,20},{5,21},{6,22},{7,23},{8,24},{9,... | collective-permute-start | bytes 6291464 | tf_op jit(solution)/shard_map/ppermute | solution.py:12
  56.5 1.0 copy-start.3
  57.4 28.8 %copy-start.2 = (bf16[4,2,256,256]{3,2,1,0:T(8,128)(2,1)S(1)}, bf16[4,2,256,256]{3,2,1,0:T(8,128)(2,1)}, u32[]{:S(2)}) copy-start(bf16[4,2,256,256]{3,2,1,0:T(8,128)(2,1)} %param.12) | copy-start | bytes 3145732
  57.4 28.8 %copy-start.4 = (f32[2,2,256,256]{3,2,1,0:T(8,128)S(1)}, f32[2,2,256,256]{3,2,1,0:T(8,128)}, u32[]{:S(2)}) copy-start(f32[2,2,256,256]{3,2,1,0:T(8,128)} %copy-done.3) | copy-start | bytes 3145732
  61.7 24.5 %collective-permute-start.2 = (bf16[2,2,4,256,256]{3,4,2,1,0:T(8,128)(2,1)}, bf16[2,2,4,256,256]{3,4,2,1,0:T(8,128)(2,1)S(1)}, u32[]{:S(2)}, u32[]{:S(2)}) collective-permute-start(bf16[2,2,4,256,256]{3,4,2,1,0:T(8,128)(2,1)} %copy.51), channel_id=1, source_target_pairs={{16,0},{17,1},{18,2},{19,3},{20,4},{21,5},{22,6},{23,7},{24,8},{25... | collective-permute-start | bytes 6291464 | tf_op jit(solution)/shard_map/ppermute | solution.py:12
  106.6 24.7 %collective-permute-start.3 = (f32[2,2,256,256]{3,2,1,0:T(8,128)S(1)}, f32[2,2,256,256]{3,2,1,0:T(8,128)S(1)}, u32[]{:S(2)}, u32[]{:S(2)}) collective-permute-start(f32[2,2,256,256]{3,2,1,0:T(8,128)S(1)} %pad_maximum_fusion.4), channel_id=1, source_target_pairs={{0,1},{1,2},{2,3},{3,4},{4,5},{5,6},{6,7},{7,8},{8,9},{9,10},{10,1... | collective-permute-start | bytes 3145736 | tf_op jit(solution)/shard_map/ppermute | solution.py:12
where the time goes:
time: 145 us; the launch traced here: 144 us
  waiting for transfers between devices  47.8 us (33%)
  local copies, waits for them, and re-layouts  44 us (30%)
  matrix products  15 us (10%)
  other arithmetic  13.5 us (9%)
  starting transfers between devices  12 us (8%)
  between operations  11.6 us (8%)
    ppermute x4, waiting for transfers between devices, shifted(): return lax.ppermute(shard, axis, pairs)  47.8 us
    ppermute x4, starting transfers between devices, shifted(): return lax.ppermute(shard, axis, pairs)  12 us
    dot_general x8, matrix products, right_mult(): jnp.einsum('nmab,bc->nmac', values, table, preferred_element_type=jnp.flo...  9.9 us
    another operation x9, local copies, waits for them, and re-layouts  7.93 us
    dynamic_update_slice x2, local copies, waits for them, and re-layouts, local(): lax.dynamic_update_slice(padded, grads[:, which_pos], (0, 0, cols_mine[wh...  7.37 us
    dynamic_update_slice x2, local copies, waits for them, and re-layouts, local(): lax.dynamic_update_slice(total, current + from_left[which_pos], corner)  7.03 us
    dynamic_update_slice x2, local copies, waits for them, and re-layouts, local(): lax.dynamic_update_slice(total, current + padded[:, :, :frame], corner)  6.97 us
    dot_general x8, matrix products, left_mult(): jnp.einsum('ab,nmbc->nmac', table, values, preferred_element_type=jnp.flo...  5.13 us
  transfers between devices with their start and end apart: 4, of which 4 were waited for; matrix products, arithmetic and copies ran while one was open for 4% of the time, Pallas kernels for 0%

commit v1 on v0

v1 whole, which is shorter than its diff:
```python
import functools
import math

import jax
import jax.numpy as jnp
import ml_dtypes
import numpy as np
from jax import lax
from jax.experimental import pallas as pl
from jax.experimental.pallas import tpu as pltpu
from jax.sharding import PartitionSpec as P

BF = jnp.bfloat16
F32 = jnp.float32
ROWS = 16
VMEM_BYTES = 48 << 20


def split_tables(frame):
    half = frame // 2
    n = np.arange(half)[:, None]
    k = np.arange(half)[None, :]
    factor = 1.0 / math.sqrt(frame)
    mats = []
    for odd in (0, 1):
        angle = (n * (2 * k + odd) % frame) * (2.0 * math.pi / frame)
        re = (np.cos(angle) * factor).astype(ml_dtypes.bfloat16)
        im = (-np.sin(angle) * factor).astype(ml_dtypes.bfloat16)
        mats.append(np.block([[re, im], [-im, re]]))
    return np.stack([mats[0], mats[1], mats[0].T, mats[1].T])


def order_table(frame):
    half = frame // 2
    q = np.arange(frame)
    source = np.where(q < half, 2 * q, 2 * (q - half) + 1)
    return (source[:, None] == np.arange(frame)[None, :]).astype(ml_dtypes.bfloat16)


def dot(a, b):
    return jnp.dot(a, b, preferred_element_type=F32)


def fwd_rows(r, i, t):
    h = r.shape[0] // 2
    up = jnp.concatenate([r[:h] + r[h:], i[:h] + i[h:]], 0).astype(BF)
    um = jnp.concatenate([r[:h] - r[h:], i[:h] - i[h:]], 0).astype(BF)
    e, o = dot(t[2], up), dot(t[3], um)
    return jnp.concatenate([e[:h], o[:h]], 0), jnp.concatenate([e[h:], o[h:]], 0)


def fwd_cols(r, i, t):
    h = r.shape[1] // 2
    up = jnp.concatenate([r[:, :h] + r[:, h:], i[:, :h] + i[:, h:]], 1).astype(BF)
    um = jnp.concatenate([r[:, :h] - r[:, h:], i[:, :h] - i[:, h:]], 1).astype(BF)
    e, o = dot(up, t[0]), dot(um, t[1])
    return jnp.concatenate([e[:, :h], o[:, :h]], 1), jnp.concatenate([e[:, h:], o[:, h:]], 1)


def inv_rows(r, i, t):
    h = r.shape[0] // 2
    e = dot(t[0], jnp.concatenate([r[:h], i[:h]], 0).astype(BF))
    o = dot(t[1], jnp.concatenate([r[h:], i[h:]], 0).astype(BF))
    s, d = e + o, e - o
    return jnp.concatenate([s[:h], d[:h]], 0), jnp.concatenate([s[h:], d[h:]], 0)


def inv_cols(r, i, t):
    h = r.shape[1] // 2
    e = dot(jnp.concatenate([r[:, :h], i[:, :h]], 1).astype(BF), t[2])
    o = dot(jnp.concatenate([r[:, h:], i[:, h:]], 1).astype(BF), t[3])
    s, d = e + o, e - o
    return jnp.concatenate([s[:, :h], d[:, :h]], 1), jnp.concatenate([s[:, h:], d[:, h:]], 1)


def fwd(r, i, t):
    return fwd_cols(*fwd_rows(r, i, t), t)


def inv(r, i, t):
    return inv_cols(*inv_rows(r, i, t), t)


def place(pos_ref, j, height, frame):
    y = pos_ref[j, 0]
    base = jnp.minimum((y >> 4) << 4, height - frame - ROWS)
    return pl.multiple_of(base, ROWS), y - base, pos_ref[j, 1] & (frame - 1)


def indices():
    depth, pos = lax.axis_index("depth"), lax.axis_index("pos")
    left = jnp.maximum(pos - 1, 0)
    return depth, pos, left


def columns(shape):
    return lax.broadcasted_iota(jnp.int32, shape, len(shape) - 1)


def rows(shape):
    return lax.broadcasted_iota(jnp.int32, shape, len(shape) - 2)


def extract_kernel(pos_ref, obj_ref, left_a, left_b, mine, other, head, tail, sems):
    _, _, height, frame = obj_ref.shape
    depth, pos, left = indices()
    jobs = [(left_a, 2 * left), (left_b, 2 * left + 1), (mine, 2 * pos + depth), (other, 2 * pos + 1 - depth)]
    started = []
    for w, (out, j) in enumerate(jobs):
        base, shift, _ = place(pos_ref, j, height, frame)
        src = obj_ref.at[0]
        copies = [
            pltpu.make_async_copy(src.at[:, pl.ds(base, ROWS)], head.at[w], sems.at[w, 0]),
            pltpu.make_async_copy(src.at[:, pl.ds(base + frame, ROWS)], tail.at[w], sems.at[w, 1]),
            pltpu.make_async_copy(
                src.at[:, pl.ds(base + ROWS, frame - ROWS)], out.at[:, ROWS:frame], sems.at[w, 2]
            ),
        ]
        for copy in copies:
            copy.start()
        started.append((copies, shift))
    for w, (out, _) in enumerate(jobs):
        copies, shift = started[w]
        copies[0].wait()
        copies[1].wait()
        first = head[w].astype(F32)
        last = tail[w].astype(F32)
        out[:, 0:ROWS] = jnp.where(rows(first.shape) >= shift, first, last).astype(BF)
    for copies, _ in started:
        copies[2].wait()


def prep_body(height, pos_ref, probe_ref, phase_ref, measured_ref, order_ref, probe_out, kern_out, measured_out):
    modes, _, frame, _ = probe_ref.shape
    depth, pos, _ = indices()
    _, row_shift, col_shift = place(pos_ref, 2 * pos + depth, height, frame)
    for m in range(modes):
        for c in range(2):
            plane = pltpu.roll(probe_ref[m, c].astype(F32), row_shift, 0)
            probe_out[m, c] = pltpu.roll(plane, col_shift, 1).astype(BF)
    order = order_ref[...]

    def reorder(x):
        for axis in (0, 1):
            total = None
            for _ in range(3):
                piece = x.astype(BF)
                x = x - piece.astype(F32)
                if axis == 0:
                    part = dot(order, piece)
                else:
                    part = lax.dot_general(
                        piece, order, (((1,), (1,)), ((), ())), preferred_element_type=F32
                    )
                total = part if total is None else total + part
            x = total
        return x

    phase = reorder(phase_ref[...])
    kern_out[0] = jnp.cos(phase)
    kern_out[1] = jnp.sin(phase)
    measured_out[...] = reorder(measured_ref[depth])


def joined(pos_ref, own_when_0, own_when_1, halo):
    frame = halo.shape[-1]
    depth, pos, _ = indices()
    shift = pos_ref[2 * pos + depth, 1] & (frame - 1)
    out = []
    for c in range(2):
        own = jnp.where(depth == 0, own_when_0[c].astype(F32), own_when_1[c].astype(F32))
        out.append(jnp.where(columns(own.shape) >= shift, own, halo[c].astype(F32)))
    return out


def front_kernel(pos_ref, own_0, own_1, halo, probe, kern, t, psi):
    obj_r, obj_i = joined(pos_ref, own_0, own_1, halo)
    for m in range(probe.shape[0]):
        pr, pi = probe[m, 0].astype(F32), probe[m, 1].astype(F32)
        r, i = fwd(pr * obj_r - pi * obj_i, pr * obj_i + pi * obj_r, t)
        kr, ki = kern[0], kern[1]
        r, i = inv(r * kr - i * ki, r * ki + i * kr, t)
        psi[m, 0] = r
        psi[m, 1] = i


def tail_kernel(pos_ref, own_0, own_1, halo, psi, measured, t, g1, adj, far):
    obj_r, obj_i = joined(pos_ref, own_0, own_1, halo)
    modes = psi.shape[0]
    inten = None
    for m in range(modes):
        pr, pi = psi[m, 0], psi[m, 1]
        r, i = fwd(pr * obj_r - pi * obj_i, pr * obj_i + pi * obj_r, t)
        far[m, 0] = r
        far[m, 1] = i
        power = r * r + i * i
        inten = power if inten is None else inten + power
    weight = (inten - measured[...]) * 0.125
    sum_r = sum_i = None
    for m in range(modes):
        r, i = inv(weight * far[m, 0], weight * far[m, 1], t)
        pr, pi = psi[m, 0], psi[m, 1]
        part_r, part_i = pr * r + pi * i, pr * i - pi * r
        sum_r = part_r if sum_r is None else sum_r + part_r
        sum_i = part_i if sum_i is None else sum_i + part_i
        adj[m, 0] = obj_r * r + obj_i * i
        adj[m, 1] = obj_r * i - obj_i * r
    g1[0] = sum_r.astype(BF)
    g1[1] = sum_i.astype(BF)


def back_kernel(adj, g1, probe, kern, t, g0, mine, other):
    depth, _, _ = indices()
    sum_r = sum_i = None
    for m in range(probe.shape[0]):
        r, i = fwd(adj[m, 0], adj[m, 1], t)
        kr, ki = kern[0], kern[1]
        r, i = inv(kr * r + ki * i, kr * i - ki * r, t)
        pr, pi = probe[m, 0].astype(F32), probe[m, 1].astype(F32)
        part_r, part_i = pr * r + pi * i, pr * i - pi * r
        sum_r = part_r if sum_r is None else sum_r + part_r
        sum_i = part_i if sum_i is None else sum_i + part_i
    for c, total in enumerate((sum_r, sum_i)):
        first = total.astype(BF)
        second = g1[c]
        g0[c] = first
        a, b = first.astype(F32), second.astype(F32)
        mine[c] = jnp.where(depth == 0, a, b).astype(BF)
        other[c] = jnp.where(depth == 0, b, a).astype(BF)


def gather_kernel(pos_ref, mine, other, spill_a0, spill_b0, spill_b1, spill_a1, out, acc):
    _, _, height, frame = out.shape
    depth, pos, left = indices()
    acc[...] = jnp.zeros_like(acc)

    def add(piece, j, spill):
        base, row_shift, col_shift = place(pos_ref, j, height, frame)

        def kept(x):
            keep = columns(x.shape) < col_shift if spill else columns(x.shape) >= col_shift
            return jnp.where(keep, x.astype(F32), 0.0)

        for c in range(2):
            head = kept(piece[c, 0:ROWS])
            below = rows(head.shape) >= row_shift
            acc[c, pl.ds(base, ROWS)] += jnp.where(below, head, 0.0)
            acc[c, pl.ds(base + frame, ROWS)] += jnp.where(below, 0.0, head)
            acc[c, pl.ds(base + ROWS, frame - ROWS)] += kept(piece[c, ROWS:frame])

    add(mine, 2 * pos + depth, False)
    add(other, 2 * pos + 1 - depth, False)

    @pl.when(jnp.logical_and(pos > 0, depth == 0))
    def _():
        add(spill_a0, 2 * left, True)
        add(spill_b0, 2 * left + 1, True)

    @pl.when(jnp.logical_and(pos > 0, depth != 0))
    def _():
        add(spill_a1, 2 * left, True)
        add(spill_b1, 2 * left + 1, True)

    for c in range(2):
        out[0, c] = acc[c].astype(BF)


def local(n_pos, object_field, probe, prop_phase, measured, positions):
    modes, _, frame, _ = probe.shape
    height = object_field.shape[2]
    both = ("depth", "pos")
    tables = jnp.asarray(split_tables(frame))
    order = jnp.asarray(order_table(frame))
    window = jax.ShapeDtypeStruct((2, frame, frame), BF)
    fields = jax.ShapeDtypeStruct((modes, 2, frame, frame), F32)
    smem = pl.BlockSpec(memory_space=pltpu.SMEM)
    vmem = pl.BlockSpec(memory_space=pltpu.VMEM)
    hbm = pl.BlockSpec(memory_space=pl.ANY)

    def call(body, name, ins, outs, scratch=(), flops=0):
        return pl.pallas_call(
            body,
            name=name,
            in_specs=ins,
            out_specs=jax.tree.map(lambda _: vmem, outs),
            out_shape=outs,
            scratch_shapes=scratch,
            compiler_params=pltpu.CompilerParams(vmem_limit_bytes=VMEM_BYTES),
            cost_estimate=pl.CostEstimate(flops=flops, bytes_accessed=4 << 20, transcendentals=0),
        )

    def dev(d, p):
        return d * n_pos + p

    def leftward(to_of):
        return [(dev(d, p + 1), dev(to, p)) for d, to in to_of for p in range(n_pos - 1)]

    def rightward(to_of):
        return [(dev(d, p), dev(to, p + 1)) for d, to in to_of for p in range(n_pos - 1)]

    swap = [(dev(d, p), dev(1 - d, p)) for d in range(2) for p in range(n_pos)]

    left_a, left_b, mine, other = call(
        extract_kernel,
        "extract",
        [smem, hbm],
        (window,) * 4,
        [
            pltpu.VMEM((4, 2, ROWS, frame), BF),
            pltpu.VMEM((4, 2, ROWS, frame), BF),
            pltpu.SemaphoreType.DMA((4, 3)),
        ],
    )(positions, object_field)

    first_a = lax.ppermute(left_a, both, leftward([(0, 0)]))
    first_b = lax.ppermute(left_b, both, leftward([(0, 1)]))
    next_a = lax.ppermute(left_a, both, swap)
    next_b = lax.ppermute(left_b, both, swap)
    partner = lax.ppermute(other, both, swap)
    second_a = lax.ppermute(next_a, both, leftward([(0, 0)]))
    second_b = lax.ppermute(next_b, both, leftward([(0, 1)]))
    depth = lax.axis_index("depth")

    probe_at, kern, measured_at = call(
        functools.partial(prep_body, height),
        "prepare",
        [smem] + [vmem] * 4,
        (
            jax.ShapeDtypeStruct(probe.shape, BF),
            jax.ShapeDtypeStruct((2, frame, frame), F32),
            jax.ShapeDtypeStruct((frame, frame), F32),
        ),
    )(positions, probe, prop_phase, measured, order)

    halo_0 = jnp.where(depth == 0, first_a, first_b)
    halo_1 = jnp.where(depth == 0, second_a, second_b)
    work = 32 * 2 * frame**3 * 2
    psi = call(front_kernel, "front", [smem] + [vmem] * 6, fields, flops=work)(
        positions, mine, partner, halo_0, probe_at, kern, tables
    )
    g1, adj = call(
        tail_kernel,
        "tail",
        [smem] + [vmem] * 6,
        (window, fields),
        [pltpu.VMEM(fields.shape, F32)],
        flops=work,
    )(positions, partner, mine, halo_1, psi, measured_at, tables)
    side_1 = lax.ppermute(g1, both, rightward([(0, 0), (1, 1)]))
    g0, keep, give = call(back_kernel, "back", [vmem] * 5, (window,) * 3, flops=work)(
        adj, g1, probe_at, kern, tables
    )
    spill_b0 = lax.ppermute(g0, both, rightward([(1, 0)]))
    spill_a0 = lax.ppermute(g0, both, rightward([(0, 0)]))
    given = lax.ppermute(give, both, swap)
    spill_a1 = lax.ppermute(side_1, both, swap)
    return call(
        gather_kernel,
        "gather",
        [smem] + [vmem] * 6,
        jax.ShapeDtypeStruct(object_field.shape, BF),
        [pltpu.VMEM((2, height, frame), F32)],
    )(positions, keep, given, spill_a0, spill_b0, side_1, spill_a1)


def solution(mesh):
    placed = (P("depth", None, None, "pos"), P(), P(), P("pos", None, None), P())
    return jax.shard_map(
        functools.partial(local, mesh.shape["pos"]),
        mesh=mesh,
        in_specs=placed,
        out_specs=P("depth", None, None, "pos"),
        check_vma=False,
    )
```

time: 145 us -> 49.8 us (0.34)
  local copies, waits for them, and re-layouts: 44 us -> 2.37 us
  waiting for transfers between devices: 47.8 us -> 9.03 us
  Pallas kernels: 0 us -> 18.3 us
  matrix products: 15 us -> 0 us
  other arithmetic: 13.5 us -> 0.07 us
  between operations: 11.6 us -> 0.18 us
  starting transfers between devices: 12 us -> 19.6 us
    ppermute x4 -> x12, waiting for transfers between devices: 47.8 us -> 9.03 us  [the longest x1 4.55 us: local(): spill_b0 = lax.ppermute(g0, both, rightward([(1, 0)]))]
    dynamic_update_slice x6 -> x0, local copies, waits for them, and re-layouts: 21.4 us -> none  [the longest x2 7.37 us: local(): lax.dynamic_update_slice(padded, grads[:, which_pos], (0, 0, cols_mine[wh...]
    pallas_call x0 -> x6, Pallas kernels: none -> 18.3 us  [the longest x1 3.71 us: local(): call(front_kernel, 'front', [smem] + [vmem] * 6, fields, flops=work)]
    dot_general x16 -> x0, matrix products: 15 us -> none  [the longest x8 9.9 us: right_mult(): jnp.einsum('nmab,bc->nmac', values, table, preferred_element_type=jnp.flo...]
    another operation x10 -> x0, local copies, waits for them, and re-layouts: 8.02 us -> none
    ppermute x4 -> x12, starting transfers between devices: 12 us -> 19.6 us  [the longest x1 4.23 us: local(): first_a = lax.ppermute(left_a, both, leftward([(0, 0)]))]
    cond x6 -> x0, local copies, waits for them, and re-layouts: 6.66 us -> none  [the longest x1 4.3 us: local(): lax.cond(section_idx == 1, end_pass, lambda: (spec_zeros(count), grad_zer...]
    convert_element_type x5 -> x0, other arithmetic: 4.64 us -> none  [the longest x1 1.38 us: forward_front(): probe_r = probe[:, 0].astype(jnp.float32)[None]]
  transfers between devices with their start and end apart: 4 -> 12, of which waited for: 4 -> 5; matrix products, arithmetic and copies ran while one was open for 4% -> 0% of each run, Pallas kernels for 0% -> 20%
where the time goes in v1:
time: 49.8 us; the launch traced here: 49.6 us
  starting transfers between devices  19.6 us (39%)
  Pallas kernels  18.3 us (37%)
  waiting for transfers between devices  9.03 us (18%)
  local copies, waits for them, and re-layouts  2.37 us (5%)
    ppermute x1, waiting for transfers between devices, local(): spill_b0 = lax.ppermute(g0, both, rightward([(1, 0)]))  4.55 us
    ppermute x1, starting transfers between devices, local(): first_a = lax.ppermute(left_a, both, leftward([(0, 0)]))  4.23 us
    pallas_call x1, Pallas kernels, local(): call(front_kernel, 'front', [smem] + [vmem] * 6, fields, flops=work)  3.71 us
    pallas_call x1, Pallas kernels, local(): call(tail_kernel, 'tail', [smem] + [vmem] * 6, (window, fields), [pltpu.V...  3.6 us
    pallas_call x1, Pallas kernels, local(): call(functools.partial(prep_body, height), 'prepare', [smem] + [vmem] * 4...  3.45 us
    ppermute x1, starting transfers between devices, local(): side_1 = lax.ppermute(g1, both, rightward([(0, 0), (1, 1)]))  3.41 us
    ppermute x1, starting transfers between devices, local(): spill_a0 = lax.ppermute(g0, both, rightward([(0, 0)]))  3.36 us
    pallas_call x1, Pallas kernels, local(): call(back_kernel, 'back', [vmem] * 5, (window,) * 3, flops=work)  2.91 us
  transfers between devices with their start and end apart: 12, of which 5 were waited for; matrix products, arithmetic and copies ran while one was open for 0% of the time, Pallas kernels for 20%

profile of v1, /device:TPU:24, one launch (start us, length us, event | category | flops | bytes accessed | tf_op | source)
XLA Modules:
  0.0 49.6 jit_solution(2851157883076435538)
XLA Ops:
  0.0 0.8 %copy.12.pos_ref = s32[32,2]{1,0:T(8,128)S(1)} copy(s32[32,2]{0,1:T(2,128)} %param.11) | data formatting | bytes 512 | tf_op args[4]
  0.8 0.0 copy-start
  0.8 1.6 %copy-done = bf16[1,2,2048,256]{3,2,1,0:T(8,128)(2,1)S(1)} copy-done((bf16[1,2,2048,256]{3,2,1,0:T(8,128)(2,1)S(1)}, bf16[1,2,2048,256]{3,2,1,0:T(8,128)(2,1)}, u32[]{:S(2)}) %copy-start) | copy-done | bytes 2097176
  2.4 0.0 copy-start.1
  2.4 0.0 copy-start.2
  2.4 0.0 copy-start.3
  2.4 0.0 copy-start.4
  2.4 1.7 %extract.1 = (bf16[2,256,256]{2,1,0:T(8,128)(2,1)S(1)}, bf16[2,256,256]{2,1,0:T(8,128)(2,1)S(1)}, bf16[2,256,256]{2,1,0:T(8,128)(2,1)S(1)}, bf16[2,256,256]{2,1,0:T(8,128)(2,1)S(1)}) custom-call(s32[32,2]{1,0:T(8,128)S(1)} %copy.12.pos_ref, bf16[1,2,2048,256]{3,2,1,0:T(8,128)(2,1)S(1)} %copy-done), custom_call_target="tpu_custom_call" | custom-call | bytes 4194304 | tf_op jit(solution)/shard_map/extract/pallas_call | solution.py:303
  4.1 0.1 collective-permute-start.1
  4.2 0.5 %collective-permute-start.3 = (bf16[2,256,256]{2,1,0:T(8,128)(2,1)S(1)}, bf16[2,256,256]{2,1,0:T(8,128)(2,1)}, u32[]{:S(2)}, u32[]{:S(2)}) collective-permute-start(bf16[2,256,256]{2,1,0:T(8,128)(2,1)S(1)} %get-tuple-element.20), channel_id=1, source_target_pairs={{0,16},{1,17},{2,18},{3,19},{4,20},{5,21},{6,22},{7,23},{8,24},{9,... | collective-permute-start | bytes 786440 | tf_op jit(solution)/shard_map/ppermute | solution.py:318
  4.7 4.2 %collective-permute-start.5 = (bf16[2,256,256]{2,1,0:T(8,128)(2,1)S(1)}, bf16[2,256,256]{2,1,0:T(8,128)(2,1)S(1)}, u32[]{:S(2)}, u32[]{:S(2)}) collective-permute-start(bf16[2,256,256]{2,1,0:T(8,128)(2,1)S(1)} %get-tuple-element.19), channel_id=1, source_target_pairs={{1,0},{2,1},{3,2},{4,3},{5,4},{6,5},{7,6},{8,7},{9,8},{10,9},{11,1... | collective-permute-start | bytes 786440 | tf_op jit(solution)/shard_map/ppermute | solution.py:315
  8.9 2.0 %collective-permute-start.6 = (bf16[2,256,256]{2,1,0:T(8,128)(2,1)S(1)}, bf16[2,256,256]{2,1,0:T(8,128)(2,1)}, u32[]{:S(2)}, u32[]{:S(2)}) collective-permute-start(bf16[2,256,256]{2,1,0:T(8,128)(2,1)S(1)} %get-tuple-element.20), channel_id=1, source_target_pairs={{1,16},{2,17},{3,18},{4,19},{5,20},{6,21},{7,22},{8,23},{9,24},{10... | collective-permute-start | bytes 786440 | tf_op jit(solution)/shard_map/ppermute | solution.py:316
  10.9 0.0 collective-permute-start
  10.9 0.0 copy-done.1
  10.9 0.0 copy-done.2
  10.9 0.0 copy-done.3
  10.9 0.0 copy-done.4
  10.9 0.0 copy-start.5
  10.9 3.4 %prepare.1 = (bf16[4,2,256,256]{3,2,1,0:T(8,128)(2,1)S(1)}, f32[2,256,256]{2,1,0:T(8,128)S(1)}, f32[256,256]{1,0:T(8,128)S(1)}) custom-call(s32[32,2]{1,0:T(8,128)S(1)} %copy.12.pos_ref, bf16[4,2,256,256]{3,2,1,0:T(8,128)(2,1)S(1)} %copy-done.1, f32[256,256]{1,0:T(8,128)S(1)} %copy-done.3, f32[2,256,256]{2,1,0:T(8,128)S(1)} %copy-done.2, ...), custom_call_target="tpu_custom_call" | custom-call | bytes 4194304 | tf_op jit(solution)/shard_map/prepare/pallas_call | solution.py:324
  14.4 0.0 collective-permute-done.1
  14.4 2.4 %collective-permute-start.2 = (bf16[2,256,256]{2,1,0:T(8,128)(2,1)}, bf16[2,256,256]{2,1,0:T(8,128)(2,1)S(1)}, u32[]{:S(2)}, u32[]{:S(2)}) collective-permute-start(bf16[2,256,256]{2,1,0:T(8,128)(2,1)} %collective-permute-done.1), channel_id=1, source_target_pairs={{1,0},{2,1},{3,2},{4,3},{5,4},{6,5},{7,6},{8,7},{9,8},{10,9},{11,1... | collective-permute-start | bytes 786440 | tf_op jit(solution)/shard_map/ppermute | solution.py:320
  16.9 0.0 collective-permute-done.3
  16.9 1.3 %collective-permute-start.4 = (bf16[2,256,256]{2,1,0:T(8,128)(2,1)}, bf16[2,256,256]{2,1,0:T(8,128)(2,1)S(1)}, u32[]{:S(2)}, u32[]{:S(2)}) collective-permute-start(bf16[2,256,256]{2,1,0:T(8,128)(2,1)} %collective-permute-done.3), channel_id=1, source_target_pairs={{1,16},{2,17},{3,18},{4,19},{5,20},{6,21},{7,22},{8,23},{9,24},{10... | collective-permute-start | bytes 786440 | tf_op jit(solution)/shard_map/ppermute | solution.py:321
  18.2 0.0 collective-permute-done.5
  18.2 0.0 collective-permute-done.6
  18.2 0.0 collective-permute-done.own_1.own_0
  18.3 0.0 copy-done.5
  18.3 3.7 %front.1.psi = f32[4,2,256,256]{3,2,1,0:T(8,128)S(1)} custom-call(s32[32,2]{1,0:T(8,128)S(1)} %copy.12.pos_ref, bf16[2,256,256]{2,1,0:T(8,128)(2,1)S(1)} %get-tuple-element.18.own_0.own_1, bf16[2,256,256]{2,1,0:T(8,128)(2,1)S(1)} %collective-permute-done.own_1.own_0, bf16[2,256,256]{2,1,0:T(8,128)(2,1)S(1)} %broadcast_select_fusion.halo, ...), custom_call_target="tpu_custom_call" | custom-call | flops 2147483648 | bytes 4194304 | tf_op jit(solution)/shard_map/front/pallas_call | solution.py:338
  22.0 0.9 %collective-permute-done.2 = bf16[2,256,256]{2,1,0:T(8,128)(2,1)S(1)} collective-permute-done((bf16[2,256,256]{2,1,0:T(8,128)(2,1)}, bf16[2,256,256]{2,1,0:T(8,128)(2,1)S(1)}, u32[]{:S(2)}, u32[]{:S(2)}) %collective-permute-start.2) | collective-permute-done | bytes 262176 | tf_op jit(solution)/shard_map/ppermute | solution.py:320
  22.9 1.0 %collective-permute-done.4 = bf16[2,256,256]{2,1,0:T(8,128)(2,1)S(1)} collective-permute-done((bf16[2,256,256]{2,1,0:T(8,128)(2,1)}, bf16[2,256,256]{2,1,0:T(8,128)(2,1)S(1)}, u32[]{:S(2)}, u32[]{:S(2)}) %collective-permute-start.4) | collective-permute-done | bytes 262176 | tf_op jit(solution)/shard_map/ppermute | solution.py:321
  23.9 3.6 %tail.1 = (bf16[2,256,256]{2,1,0:T(8,128)(2,1)S(1)}, f32[4,2,256,256]{3,2,1,0:T(8,128)S(1)}) custom-call(s32[32,2]{1,0:T(8,128)S(1)} %copy.12.pos_ref, bf16[2,256,256]{2,1,0:T(8,128)(2,1)S(1)} %collective-permute-done.own_1.own_0, bf16[2,256,256]{2,1,0:T(8,128)(2,1)S(1)} %get-tuple-element.18.own_0.own_1, ...), custom_call_target="tpu_custom_call" | custom-call | flops 2147483648 | bytes 4194304 | tf_op jit(solution)/shard_map/tail/pallas_call | solution.py:341
  27.5 3.4 %collective-permute-start.10 = (bf16[2,256,256]{2,1,0:T(8,128)(2,1)S(1)}, bf16[2,256,256]{2,1,0:T(8,128)(2,1)S(1)}, u32[]{:S(2)}, u32[]{:S(2)}) collective-permute-start(bf16[2,256,256]{2,1,0:T(8,128)(2,1)S(1)} %get-tuple-element.25.g1), channel_id=1, source_target_pairs={{0,1},{1,2},{2,3},{3,4},{4,5},{5,6},{6,7},{7,8},{8,9},{9,10},{10,1... | collective-permute-start | bytes 786440 | tf_op jit(solution)/shard_map/ppermute | solution.py:349
  30.9 2.9 %back.1 = (bf16[2,256,256]{2,1,0:T(8,128)(2,1)S(1)}, bf16[2,256,256]{2,1,0:T(8,128)(2,1)S(1)}, bf16[2,256,256]{2,1,0:T(8,128)(2,1)S(1)}) custom-call(f32[4,2,256,256]{3,2,1,0:T(8,128)S(1)} %get-tuple-element.24.adj, bf16[2,256,256]{2,1,0:T(8,128)(2,1)S(1)} %get-tuple-element.25.g1, bf16[4,2,256,256]{3,2,1,0:T(8,128)(2,1)S(1)} %get-tuple-element.21.probe, ...), custom_call_target="tpu_custom_call" | custom-call | flops 2147483648 | bytes 4194304 | tf_op jit(solution)/shard_map/back/pallas_call | solution.py:350
  33.8 0.6 %collective-permute-start.7 = (bf16[2,256,256]{2,1,0:T(8,128)(2,1)S(1)}, bf16[2,256,256]{2,1,0:T(8,128)(2,1)S(1)}, u32[]{:S(2)}, u32[]{:S(2)}) collective-permute-start(bf16[2,256,256]{2,1,0:T(8,128)(2,1)S(1)} %get-tuple-element.27), channel_id=1, source_target_pairs={{0,16},{1,17},{2,18},{3,19},{4,20},{5,21},{6,22},{7,23},{8,24},{9,... | collective-permute-start | bytes 786440 | tf_op jit(solution)/shard_map/ppermute | solution.py:355
  34.4 1.3 %collective-permute-start.9 = (bf16[2,256,256]{2,1,0:T(8,128)(2,1)S(1)}, bf16[2,256,256]{2,1,0:T(8,128)(2,1)S(1)}, u32[]{:S(2)}, u32[]{:S(2)}) collective-permute-start(bf16[2,256,256]{2,1,0:T(8,128)(2,1)S(1)} %get-tuple-element.28), channel_id=1, source_target_pairs={{16,1},{17,2},{18,3},{19,4},{20,5},{21,6},{22,7},{23,8},{24,9},{25... | collective-permute-start | bytes 786440 | tf_op jit(solution)/shard_map/ppermute | solution.py:353
  35.7 3.4 %collective-permute-start.8 = (bf16[2,256,256]{2,1,0:T(8,128)(2,1)S(1)}, bf16[2,256,256]{2,1,0:T(8,128)(2,1)S(1)}, u32[]{:S(2)}, u32[]{:S(2)}) collective-permute-start(bf16[2,256,256]{2,1,0:T(8,128)(2,1)S(1)} %get-tuple-element.28), channel_id=1, source_target_pairs={{0,1},{1,2},{2,3},{3,4},{4,5},{5,6},{6,7},{7,8},{8,9},{9,10},{10,1... | collective-permute-start | bytes 786440 | tf_op jit(solution)/shard_map/ppermute | solution.py:354
  39.1 0.7 %collective-permute-done.10.spill_b1 = bf16[2,256,256]{2,1,0:T(8,128)(2,1)S(1)} collective-permute-done((bf16[2,256,256]{2,1,0:T(8,128)(2,1)S(1)}, bf16[2,256,256]{2,1,0:T(8,128)(2,1)S(1)}, u32[]{:S(2)}, u32[]{:S(2)}) %collective-permute-start.10) | collective-permute-done | bytes 262176 | tf_op jit(solution)/shard_map/ppermute | solution.py:349
  39.7 0.5 collective-permute-start.11
  40.2 0.0 collective-permute-done.7.other
  40.2 4.6 %collective-permute-done.9.spill_b0 = bf16[2,256,256]{2,1,0:T(8,128)(2,1)S(1)} collective-permute-done((bf16[2,256,256]{2,1,0:T(8,128)(2,1)S(1)}, bf16[2,256,256]{2,1,0:T(8,128)(2,1)S(1)}, u32[]{:S(2)}, u32[]{:S(2)}) %collective-permute-start.9) | collective-permute-done | bytes 262176 | tf_op jit(solution)/shard_map/ppermute | solution.py:353
  44.7 1.9 %collective-permute-done.8.spill_a0 = bf16[2,256,256]{2,1,0:T(8,128)(2,1)S(1)} collective-permute-done((bf16[2,256,256]{2,1,0:T(8,128)(2,1)S(1)}, bf16[2,256,256]{2,1,0:T(8,128)(2,1)S(1)}, u32[]{:S(2)}, u32[]{:S(2)}) %collective-permute-start.8) | collective-permute-done | bytes 262176 | tf_op jit(solution)/shard_map/ppermute | solution.py:354
  46.7 0.0 collective-permute-done.11.spill_a1
  46.7 2.9 %gather.1 = bf16[1,2,2048,256]{3,2,1,0:T(8,128)(2,1)} custom-call(s32[32,2]{1,0:T(8,128)S(1)} %copy.12.pos_ref, bf16[2,256,256]{2,1,0:T(8,128)(2,1)S(1)} %get-tuple-element.26.mine, bf16[2,256,256]{2,1,0:T(8,128)(2,1)S(1)} %collective-permute-done.7.other, bf16[2,256,256]{2,1,0:T(8,128)(2,1)S(1)} %collective-permute-done.8.spill_a0, ...), custom_call_target="tpu_custom_call" | custom-call | bytes 4194304 | tf_op jit(solution)/shard_map/gather/pallas_call | solution.py:357
  (2 shorter events, 0.1 us)
Async XLA Ops:
  0.8 1.6 %copy-start = (bf16[1,2,2048,256]{3,2,1,0:T(8,128)(2,1)S(1)}, bf16[1,2,2048,256]{3,2,1,0:T(8,128)(2,1)}, u32[]{:S(2)}) copy-start(bf16[1,2,2048,256]{3,2,1,0:T(8,128)(2,1)} %obj_ref.1) | copy-start | bytes 6291460
  2.4 8.6 %copy-start.1 = (bf16[4,2,256,256]{3,2,1,0:T(8,128)(2,1)S(1)}, bf16[4,2,256,256]{3,2,1,0:T(8,128)(2,1)}, u32[]{:S(2)}) copy-start(bf16[4,2,256,256]{3,2,1,0:T(8,128)(2,1)} %probe_ref.1) | copy-start | bytes 3145732
  2.4 8.6 %copy-start.2 = (f32[2,256,256]{2,1,0:T(8,128)S(1)}, f32[2,256,256]{2,1,0:T(8,128)}, u32[]{:S(2)}) copy-start(f32[2,256,256]{2,1,0:T(8,128)} %measured_ref.1) | copy-start | bytes 1572868
  2.4 8.6 %copy-start.3 = (f32[256,256]{1,0:T(8,128)S(1)}, f32[256,256]{1,0:T(8,128)}, u32[]{:S(2)}) copy-start(f32[256,256]{1,0:T(8,128)} %phase_ref.1) | copy-start | bytes 786436
  2.4 8.6 %copy-start.4 = (bf16[256,256]{1,0:T(8,128)(2,1)S(1)}, bf16[256,256]{1,0:T(8,128)(2,1)}, u32[]{:S(2)}) copy-start(bf16[256,256]{1,0:T(8,128)(2,1)} %constant.13.clone.order_ref) | copy-start | bytes 393220
  4.1 10.3 %collective-permute-start.1 = (bf16[2,256,256]{2,1,0:T(8,128)(2,1)S(1)}, bf16[2,256,256]{2,1,0:T(8,128)(2,1)}, u32[]{:S(2)}, u32[]{:S(2)}) collective-permute-start(bf16[2,256,256]{2,1,0:T(8,128)(2,1)S(1)} %get-tuple-element.19), channel_id=1, source_target_pairs={{0,16},{1,17},{2,18},{3,19},{4,20},{5,21},{6,22},{7,23},{8,24},{9,... | collective-permute-start | bytes 786440 | tf_op jit(solution)/shard_map/ppermute | solution.py:317
  4.2 12.7 %collective-permute-start.3 = (bf16[2,256,256]{2,1,0:T(8,128)(2,1)S(1)}, bf16[2,256,256]{2,1,0:T(8,128)(2,1)}, u32[]{:S(2)}, u32[]{:S(2)}) collective-permute-start(bf16[2,256,256]{2,1,0:T(8,128)(2,1)S(1)} %get-tuple-element.20), channel_id=1, source_target_pairs={{0,16},{1,17},{2,18},{3,19},{4,20},{5,21},{6,22},{7,23},{8,24},{9,... | collective-permute-start | bytes 786440 | tf_op jit(solution)/shard_map/ppermute | solution.py:318
  4.7 13.5 %collective-permute-start.5 = (bf16[2,256,256]{2,1,0:T(8,128)(2,1)S(1)}, bf16[2,256,256]{2,1,0:T(8,128)(2,1)S(1)}, u32[]{:S(2)}, u32[]{:S(2)}) collective-permute-start(bf16[2,256,256]{2,1,0:T(8,128)(2,1)S(1)} %get-tuple-element.19), channel_id=1, source_target_pairs={{1,0},{2,1},{3,2},{4,3},{5,4},{6,5},{7,6},{8,7},{9,8},{10,9},{11,1... | collective-permute-start | bytes 786440 | tf_op jit(solution)/shard_map/ppermute | solution.py:315
  8.9 9.3 %collective-permute-start.6 = (bf16[2,256,256]{2,1,0:T(8,128)(2,1)S(1)}, bf16[2,256,256]{2,1,0:T(8,128)(2,1)}, u32[]{:S(2)}, u32[]{:S(2)}) collective-permute-start(bf16[2,256,256]{2,1,0:T(8,128)(2,1)S(1)} %get-tuple-element.20), channel_id=1, source_target_pairs={{1,16},{2,17},{3,18},{4,19},{5,20},{6,21},{7,22},{8,23},{9,24},{10... | collective-permute-start | bytes 786440 | tf_op jit(solution)/shard_map/ppermute | solution.py:316
  10.9 7.3 %collective-permute-start = (bf16[2,256,256]{2,1,0:T(8,128)(2,1)S(1)}, bf16[2,256,256]{2,1,0:T(8,128)(2,1)S(1)}, u32[]{:S(2)}, u32[]{:S(2)}) collective-permute-start(bf16[2,256,256]{2,1,0:T(8,128)(2,1)S(1)} %get-tuple-element.17), channel_id=1, source_target_pairs={{0,16},{1,17},{2,18},{3,19},{4,20},{5,21},{6,22},{7,23},{8,24},{9,... | collective-permute-start | bytes 786440 | tf_op jit(solution)/shard_map/ppermute | solution.py:319
  10.9 7.3 %copy-start.5 = (bf16[4,256,256]{2,1,0:T(8,128)(2,1)S(1)}, bf16[4,256,256]{2,1,0:T(8,128)(2,1)}, u32[]{:S(2)}) copy-start(bf16[4,256,256]{2,1,0:T(8,128)(2,1)} %constant.12.clone.t) | copy-start | bytes 1572868
  14.4 8.5 %collective-permute-start.2 = (bf16[2,256,256]{2,1,0:T(8,128)(2,1)}, bf16[2,256,256]{2,1,0:T(8,128)(2,1)S(1)}, u32[]{:S(2)}, u32[]{:S(2)}) collective-permute-start(bf16[2,256,256]{2,1,0:T(8,128)(2,1)} %collective-permute-done.1), channel_id=1, source_target_pairs={{1,0},{2,1},{3,2},{4,3},{5,4},{6,5},{7,6},{8,7},{9,8},{10,9},{11,1... | collective-permute-start | bytes 786440 | tf_op jit(solution)/shard_map/ppermute | solution.py:320
  16.9 7.0 %collective-permute-start.4 = (bf16[2,256,256]{2,1,0:T(8,128)(2,1)}, bf16[2,256,256]{2,1,0:T(8,128)(2,1)S(1)}, u32[]{:S(2)}, u32[]{:S(2)}) collective-permute-start(bf16[2,256,256]{2,1,0:T(8,128)(2,1)} %collective-permute-done.3), channel_id=1, source_target_pairs={{1,16},{2,17},{3,18},{4,19},{5,20},{6,21},{7,22},{8,23},{9,24},{10... | collective-permute-start | bytes 786440 | tf_op jit(solution)/shard_map/ppermute | solution.py:321
  27.5 12.2 %collective-permute-start.10 = (bf16[2,256,256]{2,1,0:T(8,128)(2,1)S(1)}, bf16[2,256,256]{2,1,0:T(8,128)(2,1)S(1)}, u32[]{:S(2)}, u32[]{:S(2)}) collective-permute-start(bf16[2,256,256]{2,1,0:T(8,128)(2,1)S(1)} %get-tuple-element.25.g1), channel_id=1, source_target_pairs={{0,1},{1,2},{2,3},{3,4},{4,5},{5,6},{6,7},{7,8},{8,9},{9,10},{10,1... | collective-permute-start | bytes 786440 | tf_op jit(solution)/shard_map/ppermute | solution.py:349
  33.8 6.4 %collective-permute-start.7 = (bf16[2,256,256]{2,1,0:T(8,128)(2,1)S(1)}, bf16[2,256,256]{2,1,0:T(8,128)(2,1)S(1)}, u32[]{:S(2)}, u32[]{:S(2)}) collective-permute-start(bf16[2,256,256]{2,1,0:T(8,128)(2,1)S(1)} %get-tuple-element.27), channel_id=1, source_target_pairs={{0,16},{1,17},{2,18},{3,19},{4,20},{5,21},{6,22},{7,23},{8,24},{9,... | collective-permute-start | bytes 786440 | tf_op jit(solution)/shard_map/ppermute | solution.py:355
  34.4 10.3 %collective-permute-start.9 = (bf16[2,256,256]{2,1,0:T(8,128)(2,1)S(1)}, bf16[2,256,256]{2,1,0:T(8,128)(2,1)S(1)}, u32[]{:S(2)}, u32[]{:S(2)}) collective-permute-start(bf16[2,256,256]{2,1,0:T(8,128)(2,1)S(1)} %get-tuple-element.28), channel_id=1, source_target_pairs={{16,1},{17,2},{18,3},{19,4},{20,5},{21,6},{22,7},{23,8},{24,9},{25... | collective-permute-start | bytes 786440 | tf_op jit(solution)/shard_map/ppermute | solution.py:353
  35.7 11.0 %collective-permute-start.8 = (bf16[2,256,256]{2,1,0:T(8,128)(2,1)S(1)}, bf16[2,256,256]{2,1,0:T(8,128)(2,1)S(1)}, u32[]{:S(2)}, u32[]{:S(2)}) collective-permute-start(bf16[2,256,256]{2,1,0:T(8,128)(2,1)S(1)} %get-tuple-element.28), channel_id=1, source_target_pairs={{0,1},{1,2},{2,3},{3,4},{4,5},{5,6},{6,7},{7,8},{8,9},{9,10},{10,1... | collective-permute-start | bytes 786440 | tf_op jit(solution)/shard_map/ppermute | solution.py:354
  39.7 7.0 %collective-permute-start.11 = (bf16[2,256,256]{2,1,0:T(8,128)(2,1)S(1)}, bf16[2,256,256]{2,1,0:T(8,128)(2,1)S(1)}, u32[]{:S(2)}, u32[]{:S(2)}) collective-permute-start(bf16[2,256,256]{2,1,0:T(8,128)(2,1)S(1)} %collective-permute-done.10.spill_b1), channel_id=1, source_target_pairs={{0,16},{1,17},{2,18},{3,19},{4,20},{5,21},{6,22},{7,23},{8,24},{9,... | collective-permute-start | bytes 786440 | tf_op jit(solution)/shard_map/ppermute | solution.py:356

commit v2 on v1

v2 whole, which is shorter than its diff:
```python
import functools
import math

import jax
import jax.numpy as jnp
import ml_dtypes
import numpy as np
from jax import lax
from jax.experimental import pallas as pl
from jax.experimental.pallas import tpu as pltpu
from jax.sharding import PartitionSpec as P

BF = jnp.bfloat16
F32 = jnp.float32
ROWS = 16
VMEM_BYTES = 20 << 20
LIGHT, HEAVY = 1000, 4 << 30
EXTRACT_BYTES = 52 << 20


def split_tables(frame):
    half = frame // 2
    n = np.arange(half)[:, None]
    k = np.arange(half)[None, :]
    factor = 1.0 / math.sqrt(frame)
    mats = []
    for odd in (0, 1):
        angle = (n * (2 * k + odd) % frame) * (2.0 * math.pi / frame)
        re = (np.cos(angle) * factor).astype(ml_dtypes.bfloat16)
        im = (-np.sin(angle) * factor).astype(ml_dtypes.bfloat16)
        mats.append(np.block([[re, im], [-im, re]]))
    return np.stack([mats[0], mats[1], mats[0].T, mats[1].T])


def dot(a, b):
    return jnp.dot(a, b, preferred_element_type=F32)


def load_f32(ref, *index):
    return ref[index].astype(F32)


def store_sums(u, m, lanes, low, high):
    h = low[0].shape[0]
    for c in range(2):
        u[m, 0, c * h : (c + 1) * h, lanes] = (low[c] + high[c]).astype(BF)
        u[m, 1, c * h : (c + 1) * h, lanes] = (low[c] - high[c]).astype(BF)


def rows_fwd(u, v, m, t):
    h = t.shape[-1] // 2
    for k in range(2):
        x = dot(t[2 + k], u[m, k])
        at = pl.ds(k * h, h)
        for c in range(2):
            low, high = x[c * h : (c + 1) * h, :h], x[c * h : (c + 1) * h, h:]
            v[m, at, c * h : (c + 1) * h] = (low + high).astype(BF)
            v[m, at, (2 + c) * h : (3 + c) * h] = (low - high).astype(BF)


def rows_inv(u, v, m, t):
    h = t.shape[-1] // 2
    e, o = dot(t[0], u[m, 0]), dot(t[1], u[m, 1])
    for k, x in enumerate((e + o, e - o)):
        at = pl.ds(k * h, h)
        for c in range(2):
            v[m, at, c * h : (c + 1) * h] = x[c * h : (c + 1) * h, :h].astype(BF)
            v[m, at, (2 + c) * h : (3 + c) * h] = x[c * h : (c + 1) * h, h:].astype(BF)


def cols(v, m, t, inverse, sink):
    h = t.shape[-1] // 2
    k = 2 if inverse else 0
    e, o = dot(v[m, :, : 2 * h], t[k]), dot(v[m, :, 2 * h :], t[k + 1])
    if inverse:
        e, o = e + o, e - o
    for b, x in enumerate((e, o)):
        sink(m, b, (x[:h, :h], x[:h, h:]), (x[h:, :h], x[h:, h:]))


def block(h, a):
    return slice(a * h, (a + 1) * h)


def store_spectrum(u, m, a, b, r, i):
    h = r.shape[0]
    u[m, a, 0:h, block(h, b)] = r.astype(BF)
    u[m, a, h : 2 * h, block(h, b)] = i.astype(BF)


def place(pos_ref, j, height, frame):
    y = pos_ref[0, j]
    base = jnp.minimum((y >> 4) << 4, height - frame - ROWS)
    return pl.multiple_of(base, ROWS), y - base, pos_ref[1, j] & (frame - 1)


def indices():
    depth, pos = lax.axis_index("depth"), lax.axis_index("pos")
    left = jnp.maximum(pos - 1, 0)
    return depth, pos, left


def columns(shape):
    return lax.broadcasted_iota(jnp.int32, shape, len(shape) - 1)


def rows(shape):
    return lax.broadcasted_iota(jnp.int32, shape, len(shape) - 2)


def extract_kernel(pos_ref, obj_ref, left_a, left_b, mine, other, ends, sems):
    _, _, height, frame = obj_ref.shape
    depth, pos, left = indices()
    src = obj_ref.at[0]
    jobs = []
    for w, (out, j) in enumerate(
        [
            (left_a, 2 * left),
            (left_b, 2 * left + 1),
            (mine, 2 * pos + depth),
            (other, 2 * pos + 1 - depth),
        ]
    ):
        base, shift, _ = place(pos_ref, j, height, frame)
        body = pltpu.make_async_copy(src.at[:, pl.ds(base, frame)], out, sems.at[w, 0])
        end = pltpu.make_async_copy(src.at[:, pl.ds(base + frame, ROWS)], ends.at[w], sems.at[w, 1])
        end.start()
        body.start()
        jobs.append((out, body, end, shift))
    for w, (out, body, end, shift) in enumerate(jobs):
        end.wait()
        body.wait()
        upper, lower = out[:, 0:ROWS].astype(F32), ends[w].astype(F32)
        out[:, 0:ROWS] = jnp.where(rows(upper.shape) >= shift, upper, lower).astype(BF)


def cos_sin(x):
    x = x - jnp.floor(x * (0.5 / math.pi) + 0.5) * (2.0 * math.pi)
    t = 0.5 * x
    z = t * t
    sine = t * (1.0 + z * (-1 / 6 + z * (1 / 120 + z * (-1 / 5040 + z * (1 / 362880 - z / 39916800)))))
    cosine = 1.0 + z * (
        -1 / 2 + z * (1 / 24 + z * (-1 / 720 + z * (1 / 40320 + z * (-1 / 3628800 + z / 479001600))))
    )
    return 1.0 - 2.0 * sine * sine, 2.0 * sine * cosine


def prepare_kernel(height, pos_ref, probe_ref, phase_ref, measured_ref, probe_out, kern_out, measured_out, shift_out):
    modes, _, frame, _ = probe_ref.shape
    depth, pos, _ = indices()
    half = frame // 2
    _, row_shift, col_shift = place(pos_ref, 2 * pos + depth, height, frame)
    shift_out[...] = jnp.full(shift_out.shape, col_shift, jnp.int32)
    down = lax.broadcasted_iota(jnp.int32, (frame, frame), 0)
    across = lax.broadcasted_iota(jnp.int32, (frame, frame), 1)

    def chosen(where):
        return jnp.where(where, 1.0, 0.0).astype(BF)

    def even_odd(n):
        return jnp.where(n < half, 2 * n, 2 * (n - half) + 1)

    order, order_t = chosen(across == even_odd(down)), chosen(down == even_odd(across))
    turn = chosen(across == ((down - row_shift) & (frame - 1)))

    def reorder(x):
        for axis in (0, 1):
            high = x.astype(BF)
            low = (x - high.astype(F32)).astype(BF)
            if axis == 0:
                x = dot(order, high) + dot(order, low)
            else:
                x = dot(high, order_t) + dot(low, order_t)
        return x

    kern_out[0], kern_out[1] = cos_sin(reorder(phase_ref[...]))
    for m in range(modes):
        for c in range(2):
            plane = pltpu.roll(probe_ref[m, c].astype(F32), col_shift, 1).astype(BF)
            probe_out[m, c] = dot(turn, plane).astype(BF)
    measured_out[...] = reorder(measured_ref[depth])


def join(shift, obj, own, halo):
    for c in range(2):
        near = own[c].astype(F32)
        obj[c] = jnp.where(columns(near.shape) >= shift[0:1], near, halo[c].astype(F32))


def front_steps(obj, probe, kern, t, psi, u, v):
    h = t.shape[-1] // 2
    modes = range(probe.shape[0])
    for m in modes:
        halves = []
        for a in range(2):
            at = block(h, a)
            pr, pi = load_f32(probe, m, 0, at), load_f32(probe, m, 1, at)
            qr, qi = obj[0, at], obj[1, at]
            halves.append((pr * qr - pi * qi, pr * qi + pi * qr))
        store_sums(u, m, slice(None), *halves)
    for m in modes:
        rows_fwd(u, v, m, t)

    def spectrum(m, b, *halves):
        for a, (r, i) in enumerate(halves):
            kr, ki = kern[0, block(h, a), block(h, b)], kern[1, block(h, a), block(h, b)]
            store_spectrum(u, m, a, b, r * kr - i * ki, r * ki + i * kr)

    def wave(m, b, *halves):
        for a, (r, i) in enumerate(halves):
            psi[m, 0, block(h, a), block(h, b)] = r
            psi[m, 1, block(h, a), block(h, b)] = i

    for m in modes:
        cols(v, m, t, False, spectrum)
    for m in modes:
        rows_inv(u, v, m, t)
    for m in modes:
        cols(v, m, t, True, wave)


def tail_steps(obj, psi, measured, t, g1, adj, far, inten, total, u, v):
    h = t.shape[-1] // 2
    modes = range(psi.shape[0])
    for m in modes:
        halves = []
        for a in range(2):
            at = block(h, a)
            pr, pi, qr, qi = psi[m, 0, at], psi[m, 1, at], obj[0, at], obj[1, at]
            halves.append((pr * qr - pi * qi, pr * qi + pi * qr))
        store_sums(u, m, slice(None), *halves)
    for m in modes:
        rows_fwd(u, v, m, t)

    def detect(m, b, *halves):
        for a, (r, i) in enumerate(halves):
            at = (block(h, a), block(h, b))
            far[(m, 0) + at] = r
            far[(m, 1) + at] = i
            power = r * r + i * i
            inten[at] = power if m == 0 else inten[at] + power

    for m in modes:
        cols(v, m, t, False, detect)
    for a in range(2):
        for b in range(2):
            at = (block(h, a), block(h, b))
            weight = (inten[at] - measured[at].astype(F32)) * 0.125
            for m in modes:
                store_spectrum(u, m, a, b, weight * far[(m, 0) + at], weight * far[(m, 1) + at])
    for m in modes:
        rows_inv(u, v, m, t)
    last = psi.shape[0] - 1

    def back(m, b, *halves):
        adjoint = []
        for a, (r, i) in enumerate(halves):
            at = (block(h, a), block(h, b))
            pr, pi = psi[(m, 0) + at], psi[(m, 1) + at]
            add_up(g1, total, at, m == 0, m == last, pr * r + pi * i, pr * i - pi * r)
            qr, qi = obj[(0,) + at], obj[(1,) + at]
            adjoint.append((qr * r + qi * i, qr * i - qi * r))
        store_sums(adj, m, block(h, b), *adjoint)

    for m in modes:
        cols(v, m, t, True, back)


def back_steps(adj, probe, kern, t, g0, total, u, v):
    h = t.shape[-1] // 2
    modes = range(probe.shape[0])
    for m in modes:
        rows_fwd(adj, v, m, t)

    def spectrum(m, b, *halves):
        for a, (r, i) in enumerate(halves):
            kr, ki = kern[0, block(h, a), block(h, b)], kern[1, block(h, a), block(h, b)]
            store_spectrum(u, m, a, b, kr * r + ki * i, kr * i - ki * r)

    for m in modes:
        cols(v, m, t, False, spectrum)
    for m in modes:
        rows_inv(u, v, m, t)
    last = probe.shape[0] - 1

    def back(m, b, *halves):
        for a, (r, i) in enumerate(halves):
            at = (block(h, a), block(h, b))
            pr, pi = load_f32(probe, m, 0, *at), load_f32(probe, m, 1, *at)
            add_up(g0, total, at, m == 0, m == last, pr * r + pi * i, pr * i - pi * r)

    for m in modes:
        cols(v, m, t, True, back)


def add_up(out, total, at, first, last, *parts):
    for c, part in enumerate(parts):
        if not first:
            part = part + total[(c,) + at]
        if last:
            out[(c,) + at] = part.astype(BF)
        else:
            total[(c,) + at] = part


def front_kernel(core, shift, own, halo, probe, kern, t, psi, obj, u, v):
    @pl.when(lax.axis_index("depth") == core)
    def _():
        join(shift, obj, own, halo)
        front_steps(obj, probe, kern, t, psi, u, v)


def tail_kernel(core, shift, own, halo, psi, measured, t, g1, adj, obj, far, inten, total, u, v):
    @pl.when(lax.axis_index("depth") == core)
    def _():
        join(shift, obj, own, halo)
        tail_steps(obj, psi, measured, t, g1, adj, far, inten, total, u, v)


def back_a_kernel(adj, probe, kern, t, g0, total, u, v):
    depth, _, _ = indices()

    @pl.when(depth == 0)
    def _():
        back_steps(adj, probe, kern, t, g0, total, u, v)


def back_b_kernel(adj, g1_a, probe, kern, t, give, total, u, v):
    depth, _, _ = indices()

    @pl.when(depth == 0)
    def _():
        give[...] = g1_a[...]

    @pl.when(depth != 0)
    def _():
        back_steps(adj, probe, kern, t, give, total, u, v)


def add_window(acc, pos_ref, piece, j, spill):
    _, height, frame = acc.shape
    base, row_shift, col_shift = place(pos_ref, j, height, frame)

    def kept(x):
        keep = columns(x.shape) < col_shift if spill else columns(x.shape) >= col_shift
        return jnp.where(keep, x.astype(F32), 0.0)

    for c in range(2):
        part = piece[c] if isinstance(piece, tuple) else piece.at[c]
        head = kept(part[0:ROWS])
        below = rows(head.shape) >= row_shift
        acc[c, pl.ds(base, ROWS)] += jnp.where(below, head, 0.0)
        acc[c, pl.ds(base + frame, ROWS)] += jnp.where(below, 0.0, head)
        acc[c, pl.ds(base + ROWS, frame - ROWS)] += kept(part[ROWS:frame])


def begin_kernel(pos_ref, g0_a, g1_b, acc):
    depth, pos, _ = indices()
    acc[...] = jnp.zeros_like(acc)
    for d, own in ((0, g0_a), (1, g1_b)):

        @pl.when(depth == d)
        def _():
            add_window(acc, pos_ref, own, 2 * pos + d, False)


def add_kernel(pos_ref, acc_in, spill_0, spill_1, acc):
    del acc_in
    depth, pos, left = indices()
    for d, spill in ((0, spill_0), (1, spill_1)):

        @pl.when(jnp.logical_and(pos > 0, depth == d))
        def _():
            add_window(acc, pos_ref, spill, 2 * left + d, True)


def gather_kernel(pos_ref, acc_in, spill_0, spill_1, given, out, acc, stage, sems):
    del acc_in
    _, height, frame = acc.shape
    depth, pos, left = indices()
    add_window(acc, pos_ref, given, 2 * pos + 1 - depth, False)
    for d, spill in ((0, spill_0), (1, spill_1)):

        @pl.when(jnp.logical_and(pos > 0, depth == d))
        def _():
            add_window(acc, pos_ref, spill, 2 * left + 1 - d, True)

    copies = []
    for c in range(2):
        for n, first in enumerate(range(0, height, frame)):
            at = slice(first, first + frame)
            stage[c, at] = acc[c, at].astype(BF)
            copy = pltpu.make_async_copy(stage.at[c, at], out.at[0, c, at], sems.at[c, n])
            copy.start()
            copies.append(copy)
    for copy in copies:
        copy.wait()


def local(n_pos, object_field, probe, prop_phase, measured, positions):
    modes, _, frame, _ = probe.shape
    height = object_field.shape[2]
    both = ("depth", "pos")
    tables = jnp.asarray(split_tables(frame))
    window = jax.ShapeDtypeStruct((2, frame, frame), BF)
    fields = jax.ShapeDtypeStruct((modes, 2, frame, frame), F32)
    smem = pl.BlockSpec(memory_space=pltpu.SMEM)
    vmem = pl.BlockSpec(memory_space=pltpu.VMEM)
    hbm = pl.BlockSpec(memory_space=pltpu.HBM)

    def call(body, name, ins, outs, scratch=(), cost=LIGHT, out_specs=None, aliases=None, vmem_bytes=VMEM_BYTES):
        return pl.pallas_call(
            body,
            name=name,
            in_specs=ins,
            out_specs=jax.tree.map(lambda _: vmem, outs) if out_specs is None else out_specs,
            out_shape=outs,
            input_output_aliases=aliases or {},
            scratch_shapes=scratch,
            compiler_params=pltpu.CompilerParams(vmem_limit_bytes=vmem_bytes),
            cost_estimate=pl.CostEstimate(flops=cost, bytes_accessed=1000, transcendentals=0),
        )

    def dev(d, p):
        return d * n_pos + p

    def leftward(to_of):
        return [(dev(d, p + 1), dev(to, p)) for d, to in to_of for p in range(n_pos - 1)]

    def rightward(to_of):
        return [(dev(d, p), dev(to, p + 1)) for d, to in to_of for p in range(n_pos - 1)]

    positions = positions.T
    def send(name, x, pairs):
        with jax.named_scope(name):
            return lax.ppermute(x, both, pairs)

    swap = [(dev(d, p), dev(1 - d, p)) for d in range(2) for p in range(n_pos)]

    left_a, left_b, mine, other = call(
        extract_kernel,
        "extract",
        [smem, hbm],
        (window,) * 4,
        [pltpu.VMEM((4, 2, ROWS, frame), BF), pltpu.SemaphoreType.DMA((4, 2))],
        vmem_bytes=EXTRACT_BYTES,
    )(positions, object_field)
    first_a = send("first_a", left_a, leftward([(0, 0)]))
    second_a = send("second_a", left_a, leftward([(1, 0)]))
    partner = send("partner", other, swap)
    left_b, partner = lax.optimization_barrier((left_b, partner))
    first_b = send("first_b", left_b, leftward([(0, 1)]))
    second_b = send("second_b", left_b, leftward([(1, 1)]))
    probe_at, kern, measured_at, shift = call(
        functools.partial(prepare_kernel, height),
        "prepare",
        [smem] + [vmem] * 3,
        (
            jax.ShapeDtypeStruct(probe.shape, BF),
            jax.ShapeDtypeStruct((2, frame, frame), F32),
            jax.ShapeDtypeStruct((frame, frame), F32),
            jax.ShapeDtypeStruct((8, frame), jnp.int32),
        ),
    )(positions, probe, prop_phase, measured)

    packed = [pltpu.VMEM((modes, 2, frame, frame), BF), pltpu.VMEM((modes, frame, 2 * frame), BF)]
    sums_of = jax.ShapeDtypeStruct((modes, 2, frame, frame), BF)
    pair = pltpu.VMEM((2, frame, frame), F32)
    deep = [pair, pltpu.VMEM(fields.shape, F32), pltpu.VMEM((frame, frame), F32), pair] + packed
    def front(core, own, halo):
        body = functools.partial(front_kernel, core)
        return call(body, "front" + "ab"[core], [vmem] * 6, fields, [pair] + packed)(
            shift, own, halo, probe_at, kern, tables
        )

    def tail(core, own, halo, psi):
        body = functools.partial(tail_kernel, core)
        return call(body, "tail" + "ab"[core], [vmem] * 6, (window, sums_of), deep)(
            shift, own, halo, psi, measured_at, tables
        )

    barrier = lax.optimization_barrier
    psi_a = front(0, mine, first_a)
    first_b, psi_a = barrier((first_b, psi_a))
    psi_b = front(1, partner, first_b)
    psi_a, psi_b = barrier((psi_a, psi_b))
    g1_a, adj_a = tail(0, partner, second_a, psi_a)
    side_a = send("side_a", g1_a, rightward([(0, 0)]))
    psi_b, g1_a = barrier((psi_b, g1_a))
    g1_b, adj_b = tail(1, mine, second_b, psi_b)
    spill_b1 = send("spill_b1", g1_b, rightward([(1, 1)]))
    adj_a, g1_b = barrier((adj_a, g1_b))
    g0_a = call(back_a_kernel, "backa", [vmem] * 4, window, [pair] + packed)(
        adj_a, probe_at, kern, tables
    )
    spill_a0 = send("spill_a0", g0_a, rightward([(0, 0)]))
    adj_b, g0_a = barrier((adj_b, g0_a))
    give = call(back_b_kernel, "backb", [vmem] * 5, window, [pair] + packed)(
        adj_b, g1_a, probe_at, kern, tables
    )
    spill_b0 = send("spill_b0", give, rightward([(1, 0)]))
    sums = jax.ShapeDtypeStruct((2, height, frame), F32)
    total = call(begin_kernel, "begin", [smem] + [vmem] * 2, sums)(positions, g0_a, g1_b)
    total, give, side_a = barrier((total, give, side_a))
    given = send("given", give, swap)
    spill_a1 = send("spill_a1", side_a, swap)
    total = call(add_kernel, "add", [smem] + [vmem] * 3, sums, aliases={1: 0}, cost=HEAVY)(
        positions, total, spill_a0, spill_b1
    )
    out, _ = call(
        gather_kernel,
        "gather",
        [smem] + [vmem] * 4,
        (jax.ShapeDtypeStruct(object_field.shape, BF), sums),
        [pltpu.VMEM((2, height, frame), BF), pltpu.SemaphoreType.DMA((2, height // frame))],
        out_specs=(hbm, vmem),
        aliases={1: 1},
    )(positions, total, spill_b0, spill_a1, given)
    return out


def solution(mesh):
    placed = (P("depth", None, None, "pos"), P(), P(), P("pos", None, None), P())
    return jax.shard_map(
        functools.partial(local, mesh.shape["pos"]),
        mesh=mesh,
        in_specs=placed,
        out_specs=P("depth", None, None, "pos"),
        check_vma=False,
    )
```

time: 49.8 us -> 40.8 us (0.82)
  Pallas kernels: 18.3 us -> 13.4 us
  starting transfers between devices: 19.6 us -> 17.4 us
  waiting for transfers between devices: 9.03 us -> 7.42 us
  local copies, waits for them, and re-layouts: 2.37 us -> 1.78 us
    pallas_call x5 -> x10, Pallas kernels: 16.6 us -> 11.6 us  [the longest x2 2.6 us: tail(): call(body, 'tail' + 'ab'[core], [vmem] * 6, (window, sums_of), deep)]
    ppermute x12 -> x11, starting transfers between devices: 19.6 us -> 17.4 us  [send(): return lax.ppermute(x, both, pairs)]
    ppermute x12 -> x11, waiting for transfers between devices: 9.03 us -> 7.42 us  [send(): return lax.ppermute(x, both, pairs)]
    unnamed x13 -> x10, local copies, waits for them, and re-layouts: 2.37 us -> 1.78 us
  transfers between devices with their start and end apart: 12 -> 11, of which waited for: 5 -> 4; matrix products, arithmetic and copies ran while one was open for 0% -> 0% of each run, Pallas kernels for 20% -> 23%
where the time goes in v2:
time: 40.8 us; the launch traced here: 40.5 us
  starting transfers between devices  17.4 us (43%)
  Pallas kernels  13.4 us (33%)
  waiting for transfers between devices  7.42 us (18%)
  local copies, waits for them, and re-layouts  1.78 us (4%)
    ppermute x11, starting transfers between devices, send(): return lax.ppermute(x, both, pairs)  17.4 us
    ppermute x11, waiting for transfers between devices, send(): return lax.ppermute(x, both, pairs)  7.42 us
    pallas_call x2, Pallas kernels, tail(): call(body, 'tail' + 'ab'[core], [vmem] * 6, (window, sums_of), deep)  2.6 us
    pallas_call x1, Pallas kernels, local(): call(gather_kernel, 'gather', [smem] + [vmem] * 4, (jax.ShapeDtypeStruct(...  2.16 us
    pallas_call x1, Pallas kernels, local(): call(extract_kernel, 'extract', [smem, hbm], (window,) * 4, [pltpu.VMEM((...  1.89 us
    pallas_call x2, Pallas kernels, front(): call(body, 'front' + 'ab'[core], [vmem] * 6, fields, [pair] + packed)  1.86 us
    pallas_call x1, Pallas kernels, local(): call(functools.partial(prepare_kernel, height), 'prepare', [smem] + [vmem...  1.78 us
    unnamed x10, local copies, waits for them, and re-layouts  1.78 us
  transfers between devices with their start and end apart: 11, of which 4 were waited for; matrix products, arithmetic and copies ran while one was open for 0% of the time, Pallas kernels for 23%

profile of v2, /device:TPU:24, one launch (start us, length us, event | category | flops | bytes accessed | tf_op | source)
XLA Modules:
  0.0 40.5 jit_solution(10588711294251356601)
XLA Ops:
  0.0 0.0 copy-start
  0.0 0.0 copy-start.2
  0.0 0.0 copy-start.1
  0.0 0.0 copy-start.4
  0.0 0.8 %copy-done.4 = s32[32,2]{0,1:T(2,128)S(1)} copy-done((s32[32,2]{0,1:T(2,128)S(1)}, s32[32,2]{0,1:T(2,128)}, u32[]{:S(2)}) %copy-start.4) | copy-done | bytes 280
  0.8 1.9 %extract.1 = (bf16[2,256,256]{2,1,0:T(8,128)(2,1)S(1)}, bf16[2,256,256]{2,1,0:T(8,128)(2,1)S(1)}, bf16[2,256,256]{2,1,0:T(8,128)(2,1)S(1)}, bf16[2,256,256]{2,1,0:T(8,128)(2,1)S(1)}) custom-call(s32[2,32]{1,0:T(2,128)S(1)} %bitcast.1, bf16[1,2,2048,256]{3,2,1,0:T(8,128)(2,1)} %obj_ref.1), custom_call_target="tpu_custom_call" | custom-call | flops 1000 | bytes 1000 | tf_op jit(solution)/shard_map/extract/pallas_call | solution.py:440
  2.7 0.1 collective-permute-start
  2.8 4.2 %collective-permute-start.3 = (bf16[2,256,256]{2,1,0:T(8,128)(2,1)S(1)}, bf16[2,256,256]{2,1,0:T(8,128)(2,1)S(1)}, u32[]{:S(2)}, u32[]{:S(2)}) collective-permute-start(bf16[2,256,256]{2,1,0:T(8,128)(2,1)S(1)} %get-tuple-element.38), channel_id=1, source_target_pairs={{1,0},{2,1},{3,2},{4,3},{5,4},{6,5},{7,6},{8,7},{9,8},{10,9},{11,1... | collective-permute-start | bytes 786440 | tf_op jit(solution)/shard_map/first_a/ppermute | solution.py:436
  7.1 0.0 collective-permute-done.own
  7.1 1.3 %collective-permute-start.2 = (bf16[2,256,256]{2,1,0:T(8,128)(2,1)S(1)}, bf16[2,256,256]{2,1,0:T(8,128)(2,1)S(1)}, u32[]{:S(2)}, u32[]{:S(2)}) collective-permute-start(bf16[2,256,256]{2,1,0:T(8,128)(2,1)S(1)} %get-tuple-element.37), channel_id=1, source_target_pairs={{1,16},{2,17},{3,18},{4,19},{5,20},{6,21},{7,22},{8,23},{9,24},{10... | collective-permute-start | bytes 786440 | tf_op jit(solution)/shard_map/first_b/ppermute | solution.py:436
  8.4 1.3 %collective-permute-start.4 = (bf16[2,256,256]{2,1,0:T(8,128)(2,1)S(1)}, bf16[2,256,256]{2,1,0:T(8,128)(2,1)S(1)}, u32[]{:S(2)}, u32[]{:S(2)}) collective-permute-start(bf16[2,256,256]{2,1,0:T(8,128)(2,1)S(1)} %get-tuple-element.38), channel_id=1, source_target_pairs={{17,0},{18,1},{19,2},{20,3},{21,4},{22,5},{23,6},{24,7},{25,8},{26... | collective-permute-start | bytes 786440 | tf_op jit(solution)/shard_map/second_a/ppermute | solution.py:436
  9.7 0.7 %collective-permute-start.1 = (bf16[2,256,256]{2,1,0:T(8,128)(2,1)S(1)}, bf16[2,256,256]{2,1,0:T(8,128)(2,1)S(1)}, u32[]{:S(2)}, u32[]{:S(2)}) collective-permute-start(bf16[2,256,256]{2,1,0:T(8,128)(2,1)S(1)} %get-tuple-element.37), channel_id=1, source_target_pairs={{17,16},{18,17},{19,18},{20,19},{21,20},{22,21},{23,22},{24,23},{2... | collective-permute-start | bytes 786440 | tf_op jit(solution)/shard_map/second_b/ppermute | solution.py:436
  10.4 0.0 copy-done.2
  10.4 0.0 copy-done.1
  10.4 0.0 copy-start.3
  10.4 0.9 %copy-done.3 = f32[256,256]{1,0:T(8,128)S(1)} copy-done((f32[256,256]{1,0:T(8,128)S(1)}, f32[256,256]{1,0:T(8,128)}, u32[]{:S(2)}) %copy-start.3) | copy-done | bytes 262168
  11.3 1.8 %prepare.1 = (bf16[4,2,256,256]{3,2,1,0:T(8,128)(2,1)S(1)}, f32[2,256,256]{2,1,0:T(8,128)S(1)}, f32[256,256]{1,0:T(8,128)S(1)}, s32[8,256]{1,0:T(8,128)S(1)}) custom-call(s32[2,32]{1,0:T(2,128)S(1)} %bitcast.2, bf16[4,2,256,256]{3,2,1,0:T(8,128)(2,1)S(1)} %copy-done.1, f32[256,256]{1,0:T(8,128)S(1)} %copy-done.3, f32[2,256,256]{2,1,0:T(8,128)S(1)} %copy-done.2), custom_call_target="tpu_custom_call" | custom-call | flops 1000 | bytes 1000 | tf_op jit(solution)/shard_map/prepare/pallas_call | solution.py:454
  13.1 0.0 collective-permute-done.3.halo
  13.1 0.0 copy-done
  13.2 1.9 %fronta.1.psi = f32[4,2,256,256]{3,2,1,0:T(8,128)S(1)} custom-call(s32[8,256]{1,0:T(8,128)S(1)} %get-tuple-element.33.shift, bf16[2,256,256]{2,1,0:T(8,128)(2,1)S(1)} %get-tuple-element.34.own, bf16[2,256,256]{2,1,0:T(8,128)(2,1)S(1)} %collective-permute-done.3.halo, bf16[4,2,256,256]{3,2,1,0:T(8,128)(2,1)S(1)} %get-tuple-element.39.probe, ...), custom_call_target="tpu_custom_call" | custom-call | flops 1000 | bytes 1000 | tf_op jit(solution)/shard_map/fronta/pallas_call | solution.py:472
  15.0 1.1 %collective-permute-done.2.halo = bf16[2,256,256]{2,1,0:T(8,128)(2,1)S(1)} collective-permute-done((bf16[2,256,256]{2,1,0:T(8,128)(2,1)S(1)}, bf16[2,256,256]{2,1,0:T(8,128)(2,1)S(1)}, u32[]{:S(2)}, u32[]{:S(2)}) %collective-permute-start.2) | collective-permute-done | bytes 262176 | tf_op jit(solution)/shard_map/first_b/ppermute | solution.py:436
  16.1 0.6 %collective-permute-done.4.halo = bf16[2,256,256]{2,1,0:T(8,128)(2,1)S(1)} collective-permute-done((bf16[2,256,256]{2,1,0:T(8,128)(2,1)S(1)}, bf16[2,256,256]{2,1,0:T(8,128)(2,1)S(1)}, u32[]{:S(2)}, u32[]{:S(2)}) %collective-permute-start.4) | collective-permute-done | bytes 262176 | tf_op jit(solution)/shard_map/second_a/ppermute | solution.py:436
  16.7 2.6 %taila.1 = (bf16[2,256,256]{2,1,0:T(8,128)(2,1)S(1)}, bf16[4,2,256,256]{3,2,1,0:T(8,128)(2,1)S(1)}) custom-call(s32[8,256]{1,0:T(8,128)S(1)} %get-tuple-element.33.shift, bf16[2,256,256]{2,1,0:T(8,128)(2,1)S(1)} %collective-permute-done.own, bf16[2,256,256]{2,1,0:T(8,128)(2,1)S(1)} %collective-permute-done.4.halo, f32[4,2,256,256]{3,2,1,0:T(8,128)S(1)} %fronta.1.psi, ...), custom_call_target="tpu_custom_call" | custom-call | flops 1000 | bytes 1000 | tf_op jit(solution)/shard_map/taila/pallas_call | solution.py:478
  19.3 4.3 %collective-permute-start.5 = (bf16[2,256,256]{2,1,0:T(8,128)(2,1)S(1)}, bf16[2,256,256]{2,1,0:T(8,128)(2,1)S(1)}, u32[]{:S(2)}, u32[]{:S(2)}) collective-permute-start(bf16[2,256,256]{2,1,0:T(8,128)(2,1)S(1)} %get-tuple-element.56.g1_a), channel_id=1, source_target_pairs={{0,1},{1,2},{2,3},{3,4},{4,5},{5,6},{6,7},{7,8},{8,9},{9,10},{10,1... | collective-permute-start | bytes 786440 | tf_op jit(solution)/shard_map/side_a/ppermute | solution.py:436
  23.6 0.0 collective-permute-done.1.halo
  23.6 1.6 %backa.1.g0_a = bf16[2,256,256]{2,1,0:T(8,128)(2,1)S(1)} custom-call(bf16[4,2,256,256]{3,2,1,0:T(8,128)(2,1)S(1)} %get-tuple-element.52.adj, bf16[4,2,256,256]{3,2,1,0:T(8,128)(2,1)S(1)} %get-tuple-element.39.probe, f32[2,256,256]{2,1,0:T(8,128)S(1)} %get-tuple-element.40.kern, bf16[4,256,256]{2,1,0:T(8,128)(2,1)S(1)} %copy-done), custom_call_target="tpu_custom_call" | custom-call | flops 1000 | bytes 1000 | tf_op jit(solution)/shard_map/backa/pallas_call | solution.py:493
  25.2 2.5 %collective-permute-start.6 = (bf16[2,256,256]{2,1,0:T(8,128)(2,1)S(1)}, bf16[2,256,256]{2,1,0:T(8,128)(2,1)S(1)}, u32[]{:S(2)}, u32[]{:S(2)}) collective-permute-start(bf16[2,256,256]{2,1,0:T(8,128)(2,1)S(1)} %backa.1.g0_a), channel_id=1, source_target_pairs={{0,1},{1,2},{2,3},{3,4},{4,5},{5,6},{6,7},{7,8},{8,9},{9,10},{10,1... | collective-permute-start | bytes 786440 | tf_op jit(solution)/shard_map/spill_a0/ppermute | solution.py:436
  27.7 0.9 %collective-permute-start.7 = (bf16[2,256,256]{2,1,0:T(8,128)(2,1)S(1)}, bf16[2,256,256]{2,1,0:T(8,128)(2,1)S(1)}, u32[]{:S(2)}, u32[]{:S(2)}) collective-permute-start(bf16[2,256,256]{2,1,0:T(8,128)(2,1)S(1)} %get-tuple-element.54.g1_b), channel_id=1, source_target_pairs={{16,17},{17,18},{18,19},{19,20},{20,21},{21,22},{22,23},{23,24},{2... | collective-permute-start | bytes 786440 | tf_op jit(solution)/shard_map/spill_b1/ppermute | solution.py:436
  28.6 1.3 %collective-permute-start.8 = (bf16[2,256,256]{2,1,0:T(8,128)(2,1)S(1)}, bf16[2,256,256]{2,1,0:T(8,128)(2,1)S(1)}, u32[]{:S(2)}, u32[]{:S(2)}) collective-permute-start(bf16[2,256,256]{2,1,0:T(8,128)(2,1)S(1)} %backb.1), channel_id=1, source_target_pairs={{16,1},{17,2},{18,3},{19,4},{20,5},{21,6},{22,7},{23,8},{24,9},{25... | collective-permute-start | bytes 786440 | tf_op jit(solution)/shard_map/spill_b0/ppermute | solution.py:436
  29.9 0.9 %begin.1.acc_in = f32[2,2048,256]{2,1,0:T(8,128)S(1)} custom-call(s32[2,32]{1,0:T(2,128)S(1)} %bitcast.3, bf16[2,256,256]{2,1,0:T(8,128)(2,1)S(1)} %backa.1.g0_a, bf16[2,256,256]{2,1,0:T(8,128)(2,1)S(1)} %get-tuple-element.54.g1_b), custom_call_target="tpu_custom_call" | custom-call | flops 1000 | bytes 1000 | tf_op jit(solution)/shard_map/begin/pallas_call | solution.py:503
  30.8 0.0 collective-permute-done.5
  30.9 0.8 %collective-permute-start.9 = (bf16[2,256,256]{2,1,0:T(8,128)(2,1)S(1)}, bf16[2,256,256]{2,1,0:T(8,128)(2,1)S(1)}, u32[]{:S(2)}, u32[]{:S(2)}) collective-permute-start(bf16[2,256,256]{2,1,0:T(8,128)(2,1)S(1)} %collective-permute-done.5), channel_id=1, source_target_pairs={{0,16},{1,17},{2,18},{3,19},{4,20},{5,21},{6,22},{7,23},{8,24},{9,... | collective-permute-start | bytes 786440 | tf_op jit(solution)/shard_map/spill_a1/ppermute | solution.py:436
  31.7 0.1 collective-permute-start.10
  31.7 3.5 %collective-permute-done.6.spill_0 = bf16[2,256,256]{2,1,0:T(8,128)(2,1)S(1)} collective-permute-done((bf16[2,256,256]{2,1,0:T(8,128)(2,1)S(1)}, bf16[2,256,256]{2,1,0:T(8,128)(2,1)S(1)}, u32[]{:S(2)}, u32[]{:S(2)}) %collective-permute-start.6) | collective-permute-done | bytes 262176 | tf_op jit(solution)/shard_map/spill_a0/ppermute | solution.py:436
  35.3 0.0 collective-permute-done.7.spill_1
  35.3 0.6 %add.1.acc_in = f32[2,2048,256]{2,1,0:T(8,128)S(1)} custom-call(s32[2,32]{1,0:T(2,128)S(1)} %bitcast.4, f32[2,2048,256]{2,1,0:T(8,128)S(1)} %begin.1.acc_in, bf16[2,256,256]{2,1,0:T(8,128)(2,1)S(1)} %collective-permute-done.6.spill_0, bf16[2,256,256]{2,1,0:T(8,128)(2,1)S(1)} %collective-permute-done.7.spill_1), custom_call_target="tpu_custom_call", output_to_operand_aliasing={{}: (1, {})} | custom-call | flops 4294967296 | bytes 1000 | tf_op jit(solution)/shard_map/add/pallas_call | solution.py:507
  35.9 2.2 %collective-permute-done.8.spill_0 = bf16[2,256,256]{2,1,0:T(8,128)(2,1)S(1)} collective-permute-done((bf16[2,256,256]{2,1,0:T(8,128)(2,1)S(1)}, bf16[2,256,256]{2,1,0:T(8,128)(2,1)S(1)}, u32[]{:S(2)}, u32[]{:S(2)}) %collective-permute-start.8) | collective-permute-done | bytes 262176 | tf_op jit(solution)/shard_map/spill_b0/ppermute | solution.py:436
  38.1 0.0 collective-permute-done.9.spill_1
  38.1 0.0 collective-permute-done.10.given
  38.1 2.2 %gather.1 = (bf16[1,2,2048,256]{3,2,1,0:T(8,128)(2,1)}, f32[2,2048,256]{2,1,0:T(8,128)S(1)}) custom-call(s32[2,32]{1,0:T(2,128)S(1)} %bitcast.5, f32[2,2048,256]{2,1,0:T(8,128)S(1)} %add.1.acc_in, bf16[2,256,256]{2,1,0:T(8,128)(2,1)S(1)} %collective-permute-done.8.spill_0, ...), custom_call_target="tpu_custom_call", output_to_operand_aliasing={{1}: (1, {})} | custom-call | flops 1000 | bytes 1000 | tf_op jit(solution)/shard_map/gather/pallas_call | solution.py:510
  (3 shorter events, 0.1 us)
Async XLA Ops:
  0.0 13.2 %copy-start = (bf16[4,256,256]{2,1,0:T(8,128)(2,1)S(1)}, bf16[4,256,256]{2,1,0:T(8,128)(2,1)}, u32[]{:S(2)}) copy-start(bf16[4,256,256]{2,1,0:T(8,128)(2,1)} %constant.2.clone.t) | copy-start | bytes 1572868
  0.0 10.4 %copy-start.2 = (f32[2,256,256]{2,1,0:T(8,128)S(1)}, f32[2,256,256]{2,1,0:T(8,128)}, u32[]{:S(2)}) copy-start(f32[2,256,256]{2,1,0:T(8,128)} %measured_ref.1) | copy-start | bytes 1572868
  0.0 10.4 %copy-start.1 = (bf16[4,2,256,256]{3,2,1,0:T(8,128)(2,1)S(1)}, bf16[4,2,256,256]{3,2,1,0:T(8,128)(2,1)}, u32[]{:S(2)}) copy-start(bf16[4,2,256,256]{3,2,1,0:T(8,128)(2,1)} %probe_ref.1) | copy-start | bytes 3145732
  0.0 0.8 %copy-start.4 = (s32[32,2]{0,1:T(2,128)S(1)}, s32[32,2]{0,1:T(2,128)}, u32[]{:S(2)}) copy-start(s32[32,2]{0,1:T(2,128)} %param.10) | copy-start | bytes 772
  2.7 4.3 %collective-permute-start = (bf16[2,256,256]{2,1,0:T(8,128)(2,1)S(1)}, bf16[2,256,256]{2,1,0:T(8,128)(2,1)S(1)}, u32[]{:S(2)}, u32[]{:S(2)}) collective-permute-start(bf16[2,256,256]{2,1,0:T(8,128)(2,1)S(1)} %get-tuple-element.36), channel_id=1, source_target_pairs={{0,16},{1,17},{2,18},{3,19},{4,20},{5,21},{6,22},{7,23},{8,24},{9,... | collective-permute-start | bytes 786440 | tf_op jit(solution)/shard_map/partner/ppermute | solution.py:436
  2.8 10.3 %collective-permute-start.3 = (bf16[2,256,256]{2,1,0:T(8,128)(2,1)S(1)}, bf16[2,256,256]{2,1,0:T(8,128)(2,1)S(1)}, u32[]{:S(2)}, u32[]{:S(2)}) collective-permute-start(bf16[2,256,256]{2,1,0:T(8,128)(2,1)S(1)} %get-tuple-element.38), channel_id=1, source_target_pairs={{1,0},{2,1},{3,2},{4,3},{5,4},{6,5},{7,6},{8,7},{9,8},{10,9},{11,1... | collective-permute-start | bytes 786440 | tf_op jit(solution)/shard_map/first_a/ppermute | solution.py:436
  7.1 9.0 %collective-permute-start.2 = (bf16[2,256,256]{2,1,0:T(8,128)(2,1)S(1)}, bf16[2,256,256]{2,1,0:T(8,128)(2,1)S(1)}, u32[]{:S(2)}, u32[]{:S(2)}) collective-permute-start(bf16[2,256,256]{2,1,0:T(8,128)(2,1)S(1)} %get-tuple-element.37), channel_id=1, source_target_pairs={{1,16},{2,17},{3,18},{4,19},{5,20},{6,21},{7,22},{8,23},{9,24},{10... | collective-permute-start | bytes 786440 | tf_op jit(solution)/shard_map/first_b/ppermute | solution.py:436
  8.4 8.3 %collective-permute-start.4 = (bf16[2,256,256]{2,1,0:T(8,128)(2,1)S(1)}, bf16[2,256,256]{2,1,0:T(8,128)(2,1)S(1)}, u32[]{:S(2)}, u32[]{:S(2)}) collective-permute-start(bf16[2,256,256]{2,1,0:T(8,128)(2,1)S(1)} %get-tuple-element.38), channel_id=1, source_target_pairs={{17,0},{18,1},{19,2},{20,3},{21,4},{22,5},{23,6},{24,7},{25,8},{26... | collective-permute-start | bytes 786440 | tf_op jit(solution)/shard_map/second_a/ppermute | solution.py:436
  9.7 13.9 %collective-permute-start.1 = (bf16[2,256,256]{2,1,0:T(8,128)(2,1)S(1)}, bf16[2,256,256]{2,1,0:T(8,128)(2,1)S(1)}, u32[]{:S(2)}, u32[]{:S(2)}) collective-permute-start(bf16[2,256,256]{2,1,0:T(8,128)(2,1)S(1)} %get-tuple-element.37), channel_id=1, source_target_pairs={{17,16},{18,17},{19,18},{20,19},{21,20},{22,21},{23,22},{24,23},{2... | collective-permute-start | bytes 786440 | tf_op jit(solution)/shard_map/second_b/ppermute | solution.py:436
  10.4 1.0 %copy-start.3 = (f32[256,256]{1,0:T(8,128)S(1)}, f32[256,256]{1,0:T(8,128)}, u32[]{:S(2)}) copy-start(f32[256,256]{1,0:T(8,128)} %phase_ref.1) | copy-start | bytes 786436
  19.3 11.5 %collective-permute-start.5 = (bf16[2,256,256]{2,1,0:T(8,128)(2,1)S(1)}, bf16[2,256,256]{2,1,0:T(8,128)(2,1)S(1)}, u32[]{:S(2)}, u32[]{:S(2)}) collective-permute-start(bf16[2,256,256]{2,1,0:T(8,128)(2,1)S(1)} %get-tuple-element.56.g1_a), channel_id=1, source_target_pairs={{0,1},{1,2},{2,3},{3,4},{4,5},{5,6},{6,7},{7,8},{8,9},{9,10},{10,1... | collective-permute-start | bytes 786440 | tf_op jit(solution)/shard_map/side_a/ppermute | solution.py:436
  25.2 10.1 %collective-permute-start.6 = (bf16[2,256,256]{2,1,0:T(8,128)(2,1)S(1)}, bf16[2,256,256]{2,1,0:T(8,128)(2,1)S(1)}, u32[]{:S(2)}, u32[]{:S(2)}) collective-permute-start(bf16[2,256,256]{2,1,0:T(8,128)(2,1)S(1)} %backa.1.g0_a), channel_id=1, source_target_pairs={{0,1},{1,2},{2,3},{3,4},{4,5},{5,6},{6,7},{7,8},{8,9},{9,10},{10,1... | collective-permute-start | bytes 786440 | tf_op jit(solution)/shard_map/spill_a0/ppermute | solution.py:436
  27.7 7.6 %collective-permute-start.7 = (bf16[2,256,256]{2,1,0:T(8,128)(2,1)S(1)}, bf16[2,256,256]{2,1,0:T(8,128)(2,1)S(1)}, u32[]{:S(2)}, u32[]{:S(2)}) collective-permute-start(bf16[2,256,256]{2,1,0:T(8,128)(2,1)S(1)} %get-tuple-element.54.g1_b), channel_id=1, source_target_pairs={{16,17},{17,18},{18,19},{19,20},{20,21},{21,22},{22,23},{23,24},{2... | collective-permute-start | bytes 786440 | tf_op jit(solution)/shard_map/spill_b1/ppermute | solution.py:436
  28.6 9.5 %collective-permute-start.8 = (bf16[2,256,256]{2,1,0:T(8,128)(2,1)S(1)}, bf16[2,256,256]{2,1,0:T(8,128)(2,1)S(1)}, u32[]{:S(2)}, u32[]{:S(2)}) collective-permute-start(bf16[2,256,256]{2,1,0:T(8,128)(2,1)S(1)} %backb.1), channel_id=1, source_target_pairs={{16,1},{17,2},{18,3},{19,4},{20,5},{21,6},{22,7},{23,8},{24,9},{25... | collective-permute-start | bytes 786440 | tf_op jit(solution)/shard_map/spill_b0/ppermute | solution.py:436
  30.9 7.3 %collective-permute-start.9 = (bf16[2,256,256]{2,1,0:T(8,128)(2,1)S(1)}, bf16[2,256,256]{2,1,0:T(8,128)(2,1)S(1)}, u32[]{:S(2)}, u32[]{:S(2)}) collective-permute-start(bf16[2,256,256]{2,1,0:T(8,128)(2,1)S(1)} %collective-permute-done.5), channel_id=1, source_target_pairs={{0,16},{1,17},{2,18},{3,19},{4,20},{5,21},{6,22},{7,23},{8,24},{9,... | collective-permute-start | bytes 786440 | tf_op jit(solution)/shard_map/spill_a1/ppermute | solution.py:436
  31.7 6.5 %collective-permute-start.10 = (bf16[2,256,256]{2,1,0:T(8,128)(2,1)S(1)}, bf16[2,256,256]{2,1,0:T(8,128)(2,1)S(1)}, u32[]{:S(2)}, u32[]{:S(2)}) collective-permute-start(bf16[2,256,256]{2,1,0:T(8,128)(2,1)S(1)} %backb.1), channel_id=1, source_target_pairs={{0,16},{1,17},{2,18},{3,19},{4,20},{5,21},{6,22},{7,23},{8,24},{9,... | collective-permute-start | bytes 786440 | tf_op jit(solution)/shard_map/given/ppermute | solution.py:436

commit v3 on v2

--- a/solution.py
+++ b/solution.py
@@ -88,10 +88,15 @@
     u[m, a, h : 2 * h, block(h, b)] = i.astype(BF)
 
 
+def pick(pos_ref, row, j):
+    x = pos_ref[row : row + 1].astype(F32)
+    return jnp.sum(jnp.where(columns(x.shape) == j, x, 0.0)).astype(jnp.int32)
+
+
 def place(pos_ref, j, height, frame):
-    y = pos_ref[0, j]
+    y = pick(pos_ref, 0, j)
     base = jnp.minimum((y >> 4) << 4, height - frame - ROWS)
-    return pl.multiple_of(base, ROWS), y - base, pos_ref[1, j] & (frame - 1)
+    return pl.multiple_of(base, ROWS), y - base, pick(pos_ref, 1, j) & (frame - 1)
 
 
 def indices():
@@ -108,30 +113,32 @@
     return lax.broadcasted_iota(jnp.int32, shape, len(shape) - 2)
 
 
-def extract_kernel(pos_ref, obj_ref, left_a, left_b, mine, other, ends, sems):
+def extract_kernel(pos_ref, obj_ref, left_a, left_b, mine, pair, ends, sems):
     _, _, height, frame = obj_ref.shape
     depth, pos, left = indices()
     src = obj_ref.at[0]
     jobs = []
-    for w, (out, j) in enumerate(
+    for w, (outs, j) in enumerate(
         [
-            (left_a, 2 * left),
-            (left_b, 2 * left + 1),
-            (mine, 2 * pos + depth),
-            (other, 2 * pos + 1 - depth),
+            ((left_a,), 2 * left),
+            ((left_b, pair.at[0]), 2 * left + 1),
+            ((pair.at[1],), 2 * pos + 1 - depth),
+            ((mine,), 2 * pos + depth),
         ]
     ):
         base, shift, _ = place(pos_ref, j, height, frame)
-        body = pltpu.make_async_copy(src.at[:, pl.ds(base, frame)], out, sems.at[w, 0])
+        body = pltpu.make_async_copy(src.at[:, pl.ds(base, frame)], outs[0], sems.at[w, 0])
         end = pltpu.make_async_copy(src.at[:, pl.ds(base + frame, ROWS)], ends.at[w], sems.at[w, 1])
         end.start()
         body.start()
-        jobs.append((out, body, end, shift))
-    for w, (out, body, end, shift) in enumerate(jobs):
+        jobs.append((outs, body, end, shift))
+    for w, (outs, body, end, shift) in enumerate(jobs):
         end.wait()
         body.wait()
-        upper, lower = out[:, 0:ROWS].astype(F32), ends[w].astype(F32)
-        out[:, 0:ROWS] = jnp.where(rows(upper.shape) >= shift, upper, lower).astype(BF)
+        upper, lower = outs[0][:, 0:ROWS].astype(F32), ends[w].astype(F32)
+        outs[0][:, 0:ROWS] = jnp.where(rows(upper.shape) >= shift, upper, lower).astype(BF)
+        for copy in outs[1:]:
+            copy[...] = outs[0][...]
 
 
 def cos_sin(x):
@@ -306,23 +313,22 @@
 def front_kernel(core, shift, own, halo, probe, kern, t, psi, obj, u, v):
     @pl.when(lax.axis_index("depth") == core)
     def _():
-        join(shift, obj, own, halo)
+        join(shift, obj, own if core == 0 else own.at[1], halo)
         front_steps(obj, probe, kern, t, psi, u, v)
 
 
 def tail_kernel(core, shift, own, halo, psi, measured, t, g1, adj, obj, far, inten, total, u, v):
     @pl.when(lax.axis_index("depth") == core)
     def _():
-        join(shift, obj, own, halo)
+        join(shift, obj, own if core == 1 else own.at[1], halo)
         tail_steps(obj, psi, measured, t, g1, adj, far, inten, total, u, v)
 
 
-def back_a_kernel(adj, probe, kern, t, g0, total, u, v):
-    depth, _, _ = indices()
-
-    @pl.when(depth == 0)
-    def _():
-        back_steps(adj, probe, kern, t, g0, total, u, v)
+def back_a_kernel(adj, g1, probe, kern, t, out, total, u, v):
+    @pl.when(lax.axis_index("depth") == 0)
+    def _():
+        back_steps(adj, probe, kern, t, out.at[0], total, u, v)
+        out[1] = g1[...]
 
 
 def back_b_kernel(adj, g1_a, probe, kern, t, give, total, u, v):
@@ -354,36 +360,39 @@
         acc[c, pl.ds(base + ROWS, frame - ROWS)] += kept(part[ROWS:frame])
 
 
-def begin_kernel(pos_ref, g0_a, g1_b, acc):
+def begin_kernel(pos_ref, grads_a, g1_b, acc):
     depth, pos, _ = indices()
     acc[...] = jnp.zeros_like(acc)
-    for d, own in ((0, g0_a), (1, g1_b)):
+    for d, own in ((0, grads_a.at[0]), (1, g1_b)):
 
         @pl.when(depth == d)
         def _():
             add_window(acc, pos_ref, own, 2 * pos + d, False)
 
 
-def add_kernel(pos_ref, acc_in, spill_0, spill_1, acc):
+def add_kernel(pos_ref, acc_in, spill_a, acc):
     del acc_in
     depth, pos, left = indices()
-    for d, spill in ((0, spill_0), (1, spill_1)):
-
-        @pl.when(jnp.logical_and(pos > 0, depth == d))
-        def _():
-            add_window(acc, pos_ref, spill, 2 * left + d, True)
-
-
-def gather_kernel(pos_ref, acc_in, spill_0, spill_1, given, out, acc, stage, sems):
+
+    @pl.when(jnp.logical_and(pos > 0, depth != 0))
+    def _():
+        add_window(acc, pos_ref, spill_a.at[1], 2 * left, True)
+
+
+def gather_kernel(pos_ref, acc_in, spill_b0, spill_b1, spill_a0, given, out, acc, stage, sems):
     del acc_in
     _, height, frame = acc.shape
     depth, pos, left = indices()
     add_window(acc, pos_ref, given, 2 * pos + 1 - depth, False)
-    for d, spill in ((0, spill_0), (1, spill_1)):
-
-        @pl.when(jnp.logical_and(pos > 0, depth == d))
-        def _():
-            add_window(acc, pos_ref, spill, 2 * left + 1 - d, True)
+
+    @pl.when(jnp.logical_and(pos > 0, depth == 0))
+    def _():
+        add_window(acc, pos_ref, spill_a0, 2 * left, True)
+        add_window(acc, pos_ref, spill_b0, 2 * left + 1, True)
+
+    @pl.when(jnp.logical_and(pos > 0, depth != 0))
+    def _():
+        add_window(acc, pos_ref, spill_b1, 2 * left + 1, True)
 
     copies = []
     for c in range(2):
@@ -404,7 +413,6 @@
     tables = jnp.asarray(split_tables(frame))
     window = jax.ShapeDtypeStruct((2, frame, frame), BF)
     fields = jax.ShapeDtypeStruct((modes, 2, frame, frame), F32)
-    smem = pl.BlockSpec(memory_space=pltpu.SMEM)
     vmem = pl.BlockSpec(memory_space=pltpu.VMEM)
     hbm = pl.BlockSpec(memory_space=pltpu.HBM)
 
@@ -437,24 +445,25 @@
 
     swap = [(dev(d, p), dev(1 - d, p)) for d in range(2) for p in range(n_pos)]
 
-    left_a, left_b, mine, other = call(
+    two = jax.ShapeDtypeStruct((2, 2, frame, frame), BF)
+    left_a, left_b, mine, pairs = call(
         extract_kernel,
         "extract",
-        [smem, hbm],
-        (window,) * 4,
+        [vmem, hbm],
+        (window, window, window, two),
         [pltpu.VMEM((4, 2, ROWS, frame), BF), pltpu.SemaphoreType.DMA((4, 2))],
         vmem_bytes=EXTRACT_BYTES,
     )(positions, object_field)
     first_a = send("first_a", left_a, leftward([(0, 0)]))
     second_a = send("second_a", left_a, leftward([(1, 0)]))
-    partner = send("partner", other, swap)
-    left_b, partner = lax.optimization_barrier((left_b, partner))
-    first_b = send("first_b", left_b, leftward([(0, 1)]))
+    swapped = send("swapped", pairs, swap)
+    left_b, swapped = lax.optimization_barrier((left_b, swapped))
+    first_b = send("first_b", swapped[0], leftward([(1, 1)]))
     second_b = send("second_b", left_b, leftward([(1, 1)]))
     probe_at, kern, measured_at, shift = call(
         functools.partial(prepare_kernel, height),
         "prepare",
-        [smem] + [vmem] * 3,
+        [vmem] * 4,
         (
             jax.ShapeDtypeStruct(probe.shape, BF),
             jax.ShapeDtypeStruct((2, frame, frame), F32),
@@ -481,41 +490,37 @@
 
     barrier = lax.optimization_barrier
     psi_a = front(0, mine, first_a)
-    first_b, psi_a = barrier((first_b, psi_a))
-    psi_b = front(1, partner, first_b)
-    psi_a, psi_b = barrier((psi_a, psi_b))
-    g1_a, adj_a = tail(0, partner, second_a, psi_a)
-    side_a = send("side_a", g1_a, rightward([(0, 0)]))
-    psi_b, g1_a = barrier((psi_b, g1_a))
+    g1_a, adj_a = tail(0, swapped, second_a, psi_a)
+    grads_a = call(back_a_kernel, "backa", [vmem] * 5, two, [pair] + packed)(
+        adj_a, g1_a, probe_at, kern, tables
+    )
+    spill_a = send("spill_a", grads_a, rightward([(0, 1)]))
+    first_b, grads_a = barrier((first_b, grads_a))
+    psi_b = front(1, swapped, first_b)
     g1_b, adj_b = tail(1, mine, second_b, psi_b)
-    spill_b1 = send("spill_b1", g1_b, rightward([(1, 1)]))
-    adj_a, g1_b = barrier((adj_a, g1_b))
-    g0_a = call(back_a_kernel, "backa", [vmem] * 4, window, [pair] + packed)(
-        adj_a, probe_at, kern, tables
-    )
-    spill_a0 = send("spill_a0", g0_a, rightward([(0, 0)]))
-    adj_b, g0_a = barrier((adj_b, g0_a))
     give = call(back_b_kernel, "backb", [vmem] * 5, window, [pair] + packed)(
         adj_b, g1_a, probe_at, kern, tables
     )
     spill_b0 = send("spill_b0", give, rightward([(1, 0)]))
+    g1_b, give = barrier((g1_b, give))
+    spill_b1 = send("spill_b1", g1_b, rightward([(1, 1)]))
     sums = jax.ShapeDtypeStruct((2, height, frame), F32)
-    total = call(begin_kernel, "begin", [smem] + [vmem] * 2, sums)(positions, g0_a, g1_b)
-    total, give, side_a = barrier((total, give, side_a))
+    total = call(begin_kernel, "begin", [vmem] * 3, sums, cost=HEAVY)(positions, grads_a, g1_b)
+    total, give, spill_a = barrier((total, give, spill_a))
     given = send("given", give, swap)
-    spill_a1 = send("spill_a1", side_a, swap)
-    total = call(add_kernel, "add", [smem] + [vmem] * 3, sums, aliases={1: 0}, cost=HEAVY)(
-        positions, total, spill_a0, spill_b1
+    spill_a0 = send("spill_a0", spill_a[0], swap)
+    total = call(add_kernel, "add", [vmem] * 3, sums, aliases={1: 0}, cost=HEAVY)(
+        positions, total, spill_a
     )
     out, _ = call(
         gather_kernel,
         "gather",
-        [smem] + [vmem] * 4,
+        [vmem] * 6,
         (jax.ShapeDtypeStruct(object_field.shape, BF), sums),
         [pltpu.VMEM((2, height, frame), BF), pltpu.SemaphoreType.DMA((2, height // frame))],
         out_specs=(hbm, vmem),
         aliases={1: 1},
-    )(positions, total, spill_b0, spill_a1, given)
+    )(positions, total, spill_b0, spill_b1, spill_a0, given)
     return out
 
 

time: 40.8 us -> 38.1 us (0.934)
  the two profiles are of different devices: /device:TPU:24 before, /device:TPU:25 now
where the time goes in v3:
time: 38.1 us; the launch traced here: 37.9 us
  starting transfers between devices  18.9 us (50%)
  Pallas kernels  11.7 us (31%)
  waiting for transfers between devices  6.02 us (16%)
  local copies, waits for them, and re-layouts  0.86 us (2%)
  between operations  0.4 us (1%)
    ppermute x10, starting transfers between devices, send(): return lax.ppermute(x, both, pairs)  18.9 us
    ppermute x10, waiting for transfers between devices, send(): return lax.ppermute(x, both, pairs)  6.02 us
    pallas_call x2, Pallas kernels, tail(): call(body, 'tail' + 'ab'[core], [vmem] * 6, (window, sums_of), deep)  2.78 us
    pallas_call x2, Pallas kernels, front(): call(body, 'front' + 'ab'[core], [vmem] * 6, fields, [pair] + packed)  1.88 us
    pallas_call x1, Pallas kernels, local(): call(gather_kernel, 'gather', [vmem] * 6, (jax.ShapeDtypeStruct(object_fi...  1.86 us
    pallas_call x1, Pallas kernels, local(): call(back_b_kernel, 'backb', [vmem] * 5, window, [pair] + packed)  1.58 us
    pallas_call x1, Pallas kernels, local(): call(extract_kernel, 'extract', [vmem, hbm], (window, window, window, two...  1.49 us
    pallas_call x1, Pallas kernels, local(): call(functools.partial(prepare_kernel, height), 'prepare', [vmem] * 4, (j...  1.46 us
  transfers between devices with their start and end apart: 10, of which 3 were waited for; matrix products, arithmetic and copies ran while one was open for 0% of the time, Pallas kernels for 22%

profile of v3, /device:TPU:25, one launch (start us, length us, event | category | flops | bytes accessed | tf_op | source)
XLA Modules:
  0.0 37.9 jit_solution(5069389207975418685)
XLA Ops:
  0.0 0.0 copy-start.2
  0.0 0.0 copy-start.3
  0.0 0.0 copy-start.1
  0.0 0.0 copy-start.4
  0.0 0.8 %copy-done.4 = s32[32,2]{0,1:T(2,128)S(1)} copy-done((s32[32,2]{0,1:T(2,128)S(1)}, s32[32,2]{0,1:T(2,128)}, u32[]{:S(2)}) %copy-start.4) | copy-done | bytes 280
  0.8 0.0 copy-start
  0.8 1.5 %extract.1 = (bf16[2,256,256]{2,1,0:T(8,128)(2,1)S(1)}, bf16[2,256,256]{2,1,0:T(8,128)(2,1)S(1)}, bf16[2,256,256]{2,1,0:T(8,128)(2,1)S(1)}, bf16[2,2,256,256]{3,2,1,0:T(8,128)(2,1)S(1)}) custom-call(s32[2,32]{1,0:T(2,128)S(1)} %bitcast.5, bf16[1,2,2048,256]{3,2,1,0:T(8,128)(2,1)} %obj_ref.1), custom_call_target="tpu_custom_call" | custom-call | flops 1000 | bytes 1000 | tf_op jit(solution)/shard_map/extract/pallas_call | solution.py:449
  2.3 0.7 %collective-permute-start = (bf16[2,2,256,256]{3,2,1,0:T(8,128)(2,1)S(1)}, bf16[2,2,256,256]{3,2,1,0:T(8,128)(2,1)S(1)}, u32[]{:S(2)}, u32[]{:S(2)}) collective-permute-start(bf16[2,2,256,256]{3,2,1,0:T(8,128)(2,1)S(1)} %get-tuple-element.28), channel_id=1, source_target_pairs={{0,16},{1,17},{2,18},{3,19},{4,20},{5,21},{6,22},{7,23},{8,24},{9,... | collective-permute-start | bytes 1572872 | tf_op jit(solution)/shard_map/swapped/ppermute | solution.py:444
  3.1 0.7 %collective-permute-start.3 = (bf16[2,256,256]{2,1,0:T(8,128)(2,1)S(1)}, bf16[2,256,256]{2,1,0:T(8,128)(2,1)S(1)}, u32[]{:S(2)}, u32[]{:S(2)}) collective-permute-start(bf16[2,256,256]{2,1,0:T(8,128)(2,1)S(1)} %get-tuple-element.31), channel_id=1, source_target_pairs={{1,0},{2,1},{3,2},{4,3},{5,4},{6,5},{7,6},{8,7},{9,8},{10,9},{11,1... | collective-permute-start | bytes 786440 | tf_op jit(solution)/shard_map/first_a/ppermute | solution.py:444
  3.7 5.6 %collective-permute-start.2 = (bf16[2,256,256]{2,1,0:T(8,128)(2,1)S(1)}, bf16[2,256,256]{2,1,0:T(8,128)(2,1)S(1)}, u32[]{:S(2)}, u32[]{:S(2)}) collective-permute-start(bf16[2,256,256]{2,1,0:T(8,128)(2,1)S(1)} %get-tuple-element.31), channel_id=1, source_target_pairs={{17,0},{18,1},{19,2},{20,3},{21,4},{22,5},{23,6},{24,7},{25,8},{26... | collective-permute-start | bytes 786440 | tf_op jit(solution)/shard_map/second_a/ppermute | solution.py:444
  9.4 0.0 collective-permute-done.own
  9.4 3.1 %collective-permute-start.1 = (bf16[2,256,256]{2,1,0:T(8,128)(2,1)S(1)}, bf16[2,256,256]{2,1,0:T(8,128)(2,1)S(1)}, u32[]{:S(2)}, u32[]{:S(2)}) collective-permute-start(bf16[2,256,256]{2,1,0:T(8,128)(2,1)S(1)} %slice_bitcast_fusion.1), channel_id=1, source_target_pairs={{17,16},{18,17},{19,18},{20,19},{21,20},{22,21},{23,22},{24,23},{2... | collective-permute-start | bytes 786440 | tf_op jit(solution)/shard_map/first_b/ppermute | solution.py:444
  12.5 2.2 %collective-permute-start.4 = (bf16[2,256,256]{2,1,0:T(8,128)(2,1)S(1)}, bf16[2,256,256]{2,1,0:T(8,128)(2,1)S(1)}, u32[]{:S(2)}, u32[]{:S(2)}) collective-permute-start(bf16[2,256,256]{2,1,0:T(8,128)(2,1)S(1)} %get-tuple-element.39), channel_id=1, source_target_pairs={{17,16},{18,17},{19,18},{20,19},{21,20},{22,21},{23,22},{24,23},{2... | collective-permute-start | bytes 786440 | tf_op jit(solution)/shard_map/second_b/ppermute | solution.py:444
  14.7 0.0 copy-done.2
  14.7 0.0 copy-done.3
  14.7 0.0 copy-done.1
  14.7 1.5 %prepare.1 = (bf16[4,2,256,256]{3,2,1,0:T(8,128)(2,1)S(1)}, f32[2,256,256]{2,1,0:T(8,128)S(1)}, f32[256,256]{1,0:T(8,128)S(1)}, s32[8,256]{1,0:T(8,128)S(1)}) custom-call(s32[2,32]{1,0:T(2,128)S(1)} %bitcast.6, bf16[4,2,256,256]{3,2,1,0:T(8,128)(2,1)S(1)} %copy-done.1, f32[256,256]{1,0:T(8,128)S(1)} %copy-done.3, f32[2,256,256]{2,1,0:T(8,128)S(1)} %copy-done.2), custom_call_target="tpu_custom_call" | custom-call | flops 1000 | bytes 1000 | tf_op jit(solution)/shard_map/prepare/pallas_call | solution.py:463
  16.2 0.0 collective-permute-done.3.halo
  16.2 0.0 copy-done
  16.2 0.0 collective-permute-done.2.halo
  16.3 1.3 %collective-permute-start.5 = (bf16[2,2,256,256]{3,2,1,0:T(8,128)(2,1)S(1)}, bf16[2,2,256,256]{3,2,1,0:T(8,128)(2,1)S(1)}, u32[]{:S(2)}, u32[]{:S(2)}) collective-permute-start(bf16[2,2,256,256]{3,2,1,0:T(8,128)(2,1)S(1)} %backa.1.grads_a), channel_id=1, source_target_pairs={{0,17},{1,18},{2,19},{3,20},{4,21},{5,22},{6,23},{7,24},{8,25},{9,... | collective-permute-start | bytes 1572872 | tf_op jit(solution)/shard_map/spill_a/ppermute | solution.py:444
  17.6 0.0 collective-permute-done.1.halo
  17.6 1.9 %frontb.1.psi = f32[4,2,256,256]{3,2,1,0:T(8,128)S(1)} custom-call(s32[8,256]{1,0:T(8,128)S(1)} %get-tuple-element.30.shift, bf16[2,2,256,256]{3,2,1,0:T(8,128)(2,1)S(1)} %collective-permute-done.own, bf16[2,256,256]{2,1,0:T(8,128)(2,1)S(1)} %collective-permute-done.1.halo, bf16[4,2,256,256]{3,2,1,0:T(8,128)(2,1)S(1)} %get-tuple-element.33.probe, ...), custom_call_target="tpu_custom_call" | custom-call | flops 1000 | bytes 1000 | tf_op jit(solution)/shard_map/frontb/pallas_call | solution.py:481
  19.5 0.5 %collective-permute-done.4.halo = bf16[2,256,256]{2,1,0:T(8,128)(2,1)S(1)} collective-permute-done((bf16[2,256,256]{2,1,0:T(8,128)(2,1)S(1)}, bf16[2,256,256]{2,1,0:T(8,128)(2,1)S(1)}, u32[]{:S(2)}, u32[]{:S(2)}) %collective-permute-start.4) | collective-permute-done | bytes 262176 | tf_op jit(solution)/shard_map/second_b/ppermute | solution.py:444
  19.9 2.8 %tailb.1 = (bf16[2,256,256]{2,1,0:T(8,128)(2,1)S(1)}, bf16[4,2,256,256]{3,2,1,0:T(8,128)(2,1)S(1)}) custom-call(s32[8,256]{1,0:T(8,128)S(1)} %get-tuple-element.30.shift, bf16[2,256,256]{2,1,0:T(8,128)(2,1)S(1)} %get-tuple-element.32.own, bf16[2,256,256]{2,1,0:T(8,128)(2,1)S(1)} %collective-permute-done.4.halo, f32[4,2,256,256]{3,2,1,0:T(8,128)S(1)} %frontb.1.psi, ...), custom_call_target="tpu_custom_call" | custom-call | flops 1000 | bytes 1000 | tf_op jit(solution)/shard_map/tailb/pallas_call | solution.py:487
  22.7 1.6 %backb.1 = bf16[2,256,256]{2,1,0:T(8,128)(2,1)S(1)} custom-call(bf16[4,2,256,256]{3,2,1,0:T(8,128)(2,1)S(1)} %get-tuple-element.42.adj, bf16[2,256,256]{2,1,0:T(8,128)(2,1)S(1)} %get-tuple-element.37.g1.g1_a, bf16[4,2,256,256]{3,2,1,0:T(8,128)(2,1)S(1)} %get-tuple-element.33.probe, f32[2,256,256]{2,1,0:T(8,128)S(1)} %get-tuple-element.34.kern, ...), custom_call_target="tpu_custom_call" | custom-call | flops 1000 | bytes 1000 | tf_op jit(solution)/shard_map/backb/pallas_call | solution.py:501
  24.3 1.3 %collective-permute-start.6 = (bf16[2,256,256]{2,1,0:T(8,128)(2,1)S(1)}, bf16[2,256,256]{2,1,0:T(8,128)(2,1)S(1)}, u32[]{:S(2)}, u32[]{:S(2)}) collective-permute-start(bf16[2,256,256]{2,1,0:T(8,128)(2,1)S(1)} %backb.1), channel_id=1, source_target_pairs={{16,1},{17,2},{18,3},{19,4},{20,5},{21,6},{22,7},{23,8},{24,9},{25... | collective-permute-start | bytes 786440 | tf_op jit(solution)/shard_map/spill_b0/ppermute | solution.py:444
  25.6 3.4 %collective-permute-start.7 = (bf16[2,256,256]{2,1,0:T(8,128)(2,1)S(1)}, bf16[2,256,256]{2,1,0:T(8,128)(2,1)S(1)}, u32[]{:S(2)}, u32[]{:S(2)}) collective-permute-start(bf16[2,256,256]{2,1,0:T(8,128)(2,1)S(1)} %get-tuple-element.43.g1_b), channel_id=1, source_target_pairs={{16,17},{17,18},{18,19},{19,20},{20,21},{21,22},{22,23},{23,24},{2... | collective-permute-start | bytes 786440 | tf_op jit(solution)/shard_map/spill_b1/ppermute | solution.py:444
  29.1 0.5 %begin.1.acc_in = f32[2,2048,256]{2,1,0:T(8,128)S(1)} custom-call(s32[2,32]{1,0:T(2,128)S(1)} %bitcast.7, bf16[2,2,256,256]{3,2,1,0:T(8,128)(2,1)S(1)} %backa.1.grads_a, bf16[2,256,256]{2,1,0:T(8,128)(2,1)S(1)} %get-tuple-element.43.g1_b), custom_call_target="tpu_custom_call" | custom-call | flops 4294967296 | bytes 1000 | tf_op jit(solution)/shard_map/begin/pallas_call | solution.py:508
  29.5 1.6 %collective-permute-done.5.spill_a = bf16[2,2,256,256]{3,2,1,0:T(8,128)(2,1)S(1)} collective-permute-done((bf16[2,2,256,256]{3,2,1,0:T(8,128)(2,1)S(1)}, bf16[2,2,256,256]{3,2,1,0:T(8,128)(2,1)S(1)}, u32[]{:S(2)}, u32[]{:S(2)}) %collective-permute-start.5) | collective-permute-done | bytes 524320 | tf_op jit(solution)/shard_map/spill_a/ppermute | solution.py:444
  31.1 0.1 collective-permute-start.8
  31.2 0.5 %collective-permute-start.9 = (bf16[2,256,256]{2,1,0:T(8,128)(2,1)S(1)}, bf16[2,256,256]{2,1,0:T(8,128)(2,1)S(1)}, u32[]{:S(2)}, u32[]{:S(2)}) collective-permute-start(bf16[2,256,256]{2,1,0:T(8,128)(2,1)S(1)} %backb.1), channel_id=1, source_target_pairs={{0,16},{1,17},{2,18},{3,19},{4,20},{5,21},{6,22},{7,23},{8,24},{9,... | collective-permute-start | bytes 786440 | tf_op jit(solution)/shard_map/given/ppermute | solution.py:444
  31.7 0.2 add.1.acc_in
  31.9 3.9 %collective-permute-done.7.spill_b1 = bf16[2,256,256]{2,1,0:T(8,128)(2,1)S(1)} collective-permute-done((bf16[2,256,256]{2,1,0:T(8,128)(2,1)S(1)}, bf16[2,256,256]{2,1,0:T(8,128)(2,1)S(1)}, u32[]{:S(2)}, u32[]{:S(2)}) %collective-permute-start.7) | collective-permute-done | bytes 262176 | tf_op jit(solution)/shard_map/spill_b1/ppermute | solution.py:444
  35.8 0.0 collective-permute-done.6.spill_b0
  35.8 0.0 collective-permute-done.8.spill_a0
  35.8 0.0 collective-permute-done.9.given
  35.8 1.9 %gather.1 = (bf16[1,2,2048,256]{3,2,1,0:T(8,128)(2,1)}, f32[2,2048,256]{2,1,0:T(8,128)S(1)}) custom-call(s32[2,32]{1,0:T(2,128)S(1)} %bitcast.9, f32[2,2048,256]{2,1,0:T(8,128)S(1)} %add.1.acc_in, bf16[2,256,256]{2,1,0:T(8,128)(2,1)S(1)} %collective-permute-done.6.spill_b0, ...), custom_call_target="tpu_custom_call", output_to_operand_aliasing={{1}: (1, {})} | custom-call | flops 1000 | bytes 1000 | tf_op jit(solution)/shard_map/gather/pallas_call | solution.py:515
  (5 shorter events, 0.1 us)
Async XLA Ops:
  0.0 14.7 %copy-start.2 = (f32[2,256,256]{2,1,0:T(8,128)S(1)}, f32[2,256,256]{2,1,0:T(8,128)}, u32[]{:S(2)}) copy-start(f32[2,256,256]{2,1,0:T(8,128)} %measured_ref.1) | copy-start | bytes 1572868
  0.0 14.7 %copy-start.3 = (f32[256,256]{1,0:T(8,128)S(1)}, f32[256,256]{1,0:T(8,128)}, u32[]{:S(2)}) copy-start(f32[256,256]{1,0:T(8,128)} %phase_ref.1) | copy-start | bytes 786436
  0.0 14.7 %copy-start.1 = (bf16[4,2,256,256]{3,2,1,0:T(8,128)(2,1)S(1)}, bf16[4,2,256,256]{3,2,1,0:T(8,128)(2,1)}, u32[]{:S(2)}) copy-start(bf16[4,2,256,256]{3,2,1,0:T(8,128)(2,1)} %probe_ref.1) | copy-start | bytes 3145732
  0.0 0.8 %copy-start.4 = (s32[32,2]{0,1:T(2,128)S(1)}, s32[32,2]{0,1:T(2,128)}, u32[]{:S(2)}) copy-start(s32[32,2]{0,1:T(2,128)} %param.10) | copy-start | bytes 772
  0.8 15.4 %copy-start = (bf16[4,256,256]{2,1,0:T(8,128)(2,1)S(1)}, bf16[4,256,256]{2,1,0:T(8,128)(2,1)}, u32[]{:S(2)}) copy-start(bf16[4,256,256]{2,1,0:T(8,128)(2,1)} %constant.2.clone.t) | copy-start | bytes 1572868
  2.3 7.1 %collective-permute-start = (bf16[2,2,256,256]{3,2,1,0:T(8,128)(2,1)S(1)}, bf16[2,2,256,256]{3,2,1,0:T(8,128)(2,1)S(1)}, u32[]{:S(2)}, u32[]{:S(2)}) collective-permute-start(bf16[2,2,256,256]{3,2,1,0:T(8,128)(2,1)S(1)} %get-tuple-element.28), channel_id=1, source_target_pairs={{0,16},{1,17},{2,18},{3,19},{4,20},{5,21},{6,22},{7,23},{8,24},{9,... | collective-permute-start | bytes 1572872 | tf_op jit(solution)/shard_map/swapped/ppermute | solution.py:444
  3.1 13.1 %collective-permute-start.3 = (bf16[2,256,256]{2,1,0:T(8,128)(2,1)S(1)}, bf16[2,256,256]{2,1,0:T(8,128)(2,1)S(1)}, u32[]{:S(2)}, u32[]{:S(2)}) collective-permute-start(bf16[2,256,256]{2,1,0:T(8,128)(2,1)S(1)} %get-tuple-element.31), channel_id=1, source_target_pairs={{1,0},{2,1},{3,2},{4,3},{5,4},{6,5},{7,6},{8,7},{9,8},{10,9},{11,1... | collective-permute-start | bytes 786440 | tf_op jit(solution)/shard_map/first_a/ppermute | solution.py:444
  3.7 12.5 %collective-permute-start.2 = (bf16[2,256,256]{2,1,0:T(8,128)(2,1)S(1)}, bf16[2,256,256]{2,1,0:T(8,128)(2,1)S(1)}, u32[]{:S(2)}, u32[]{:S(2)}) collective-permute-start(bf16[2,256,256]{2,1,0:T(8,128)(2,1)S(1)} %get-tuple-element.31), channel_id=1, source_target_pairs={{17,0},{18,1},{19,2},{20,3},{21,4},{22,5},{23,6},{24,7},{25,8},{26... | collective-permute-start | bytes 786440 | tf_op jit(solution)/shard_map/second_a/ppermute | solution.py:444
  9.4 8.1 %collective-permute-start.1 = (bf16[2,256,256]{2,1,0:T(8,128)(2,1)S(1)}, bf16[2,256,256]{2,1,0:T(8,128)(2,1)S(1)}, u32[]{:S(2)}, u32[]{:S(2)}) collective-permute-start(bf16[2,256,256]{2,1,0:T(8,128)(2,1)S(1)} %slice_bitcast_fusion.1), channel_id=1, source_target_pairs={{17,16},{18,17},{19,18},{20,19},{21,20},{22,21},{23,22},{24,23},{2... | collective-permute-start | bytes 786440 | tf_op jit(solution)/shard_map/first_b/ppermute | solution.py:444
  12.5 7.4 %collective-permute-start.4 = (bf16[2,256,256]{2,1,0:T(8,128)(2,1)S(1)}, bf16[2,256,256]{2,1,0:T(8,128)(2,1)S(1)}, u32[]{:S(2)}, u32[]{:S(2)}) collective-permute-start(bf16[2,256,256]{2,1,0:T(8,128)(2,1)S(1)} %get-tuple-element.39), channel_id=1, source_target_pairs={{17,16},{18,17},{19,18},{20,19},{21,20},{22,21},{23,22},{24,23},{2... | collective-permute-start | bytes 786440 | tf_op jit(solution)/shard_map/second_b/ppermute | solution.py:444
  16.3 14.8 %collective-permute-start.5 = (bf16[2,2,256,256]{3,2,1,0:T(8,128)(2,1)S(1)}, bf16[2,2,256,256]{3,2,1,0:T(8,128)(2,1)S(1)}, u32[]{:S(2)}, u32[]{:S(2)}) collective-permute-start(bf16[2,2,256,256]{3,2,1,0:T(8,128)(2,1)S(1)} %backa.1.grads_a), channel_id=1, source_target_pairs={{0,17},{1,18},{2,19},{3,20},{4,21},{5,22},{6,23},{7,24},{8,25},{9,... | collective-permute-start | bytes 1572872 | tf_op jit(solution)/shard_map/spill_a/ppermute | solution.py:444
  24.3 11.5 %collective-permute-start.6 = (bf16[2,256,256]{2,1,0:T(8,128)(2,1)S(1)}, bf16[2,256,256]{2,1,0:T(8,128)(2,1)S(1)}, u32[]{:S(2)}, u32[]{:S(2)}) collective-permute-start(bf16[2,256,256]{2,1,0:T(8,128)(2,1)S(1)} %backb.1), channel_id=1, source_target_pairs={{16,1},{17,2},{18,3},{19,4},{20,5},{21,6},{22,7},{23,8},{24,9},{25... | collective-permute-start | bytes 786440 | tf_op jit(solution)/shard_map/spill_b0/ppermute | solution.py:444
  25.6 10.2 %collective-permute-start.7 = (bf16[2,256,256]{2,1,0:T(8,128)(2,1)S(1)}, bf16[2,256,256]{2,1,0:T(8,128)(2,1)S(1)}, u32[]{:S(2)}, u32[]{:S(2)}) collective-permute-start(bf16[2,256,256]{2,1,0:T(8,128)(2,1)S(1)} %get-tuple-element.43.g1_b), channel_id=1, source_target_pairs={{16,17},{17,18},{18,19},{19,20},{20,21},{21,22},{22,23},{23,24},{2... | collective-permute-start | bytes 786440 | tf_op jit(solution)/shard_map/spill_b1/ppermute | solution.py:444
  31.1 4.7 %collective-permute-start.8 = (bf16[2,256,256]{2,1,0:T(8,128)(2,1)S(1)}, bf16[2,256,256]{2,1,0:T(8,128)(2,1)S(1)}, u32[]{:S(2)}, u32[]{:S(2)}) collective-permute-start(bf16[2,256,256]{2,1,0:T(8,128)(2,1)S(1)} %slice_bitcast_fusion), channel_id=1, source_target_pairs={{0,16},{1,17},{2,18},{3,19},{4,20},{5,21},{6,22},{7,23},{8,24},{9,... | collective-permute-start | bytes 786440 | tf_op jit(solution)/shard_map/spill_a0/ppermute | solution.py:444
  31.2 4.6 %collective-permute-start.9 = (bf16[2,256,256]{2,1,0:T(8,128)(2,1)S(1)}, bf16[2,256,256]{2,1,0:T(8,128)(2,1)S(1)}, u32[]{:S(2)}, u32[]{:S(2)}) collective-permute-start(bf16[2,256,256]{2,1,0:T(8,128)(2,1)S(1)} %backb.1), channel_id=1, source_target_pairs={{0,16},{1,17},{2,18},{3,19},{4,20},{5,21},{6,22},{7,23},{8,24},{9,... | collective-permute-start | bytes 786440 | tf_op jit(solution)/shard_map/given/ppermute | solution.py:444

commit v4 on v3

--- a/solution.py
+++ b/solution.py
@@ -14,7 +14,7 @@
 F32 = jnp.float32
 ROWS = 16
 VMEM_BYTES = 20 << 20
-LIGHT, HEAVY = 1000, 4 << 30
+LIGHT, MEDIUM = 1000, 1 << 30
 EXTRACT_BYTES = 52 << 20
 
 
@@ -324,11 +324,10 @@
         tail_steps(obj, psi, measured, t, g1, adj, far, inten, total, u, v)
 
 
-def back_a_kernel(adj, g1, probe, kern, t, out, total, u, v):
+def back_a_kernel(adj, probe, kern, t, g0, total, u, v):
     @pl.when(lax.axis_index("depth") == 0)
     def _():
-        back_steps(adj, probe, kern, t, out.at[0], total, u, v)
-        out[1] = g1[...]
+        back_steps(adj, probe, kern, t, g0, total, u, v)
 
 
 def back_b_kernel(adj, g1_a, probe, kern, t, give, total, u, v):
@@ -360,39 +359,46 @@
         acc[c, pl.ds(base + ROWS, frame - ROWS)] += kept(part[ROWS:frame])
 
 
-def begin_kernel(pos_ref, grads_a, g1_b, acc):
+def begin_kernel(pos_ref, g0_a, g1_b, acc):
     depth, pos, _ = indices()
     acc[...] = jnp.zeros_like(acc)
-    for d, own in ((0, grads_a.at[0]), (1, g1_b)):
+    for d, own in ((0, g0_a), (1, g1_b)):
 
         @pl.when(depth == d)
         def _():
             add_window(acc, pos_ref, own, 2 * pos + d, False)
 
 
-def add_kernel(pos_ref, acc_in, spill_a, acc):
+def trade_kernel(spill_b1, spill_a0, out):
+    for d, spill in ((0, spill_b1), (1, spill_a0)):
+
+        @pl.when(lax.axis_index("depth") == d)
+        def _():
+            out[...] = spill[...]
+
+
+def add_kernel(pos_ref, acc_in, spill_a1, acc):
     del acc_in
     depth, pos, left = indices()
 
     @pl.when(jnp.logical_and(pos > 0, depth != 0))
     def _():
-        add_window(acc, pos_ref, spill_a.at[1], 2 * left, True)
-
-
-def gather_kernel(pos_ref, acc_in, spill_b0, spill_b1, spill_a0, given, out, acc, stage, sems):
+        add_window(acc, pos_ref, spill_a1, 2 * left, True)
+
+
+def gather_kernel(pos_ref, acc_in, spill_b0, traded, given, out, acc, stage, sems):
     del acc_in
     _, height, frame = acc.shape
     depth, pos, left = indices()
     add_window(acc, pos_ref, given, 2 * pos + 1 - depth, False)
 
+    @pl.when(pos > 0)
+    def _():
+        add_window(acc, pos_ref, traded, 2 * left + depth, True)
+
     @pl.when(jnp.logical_and(pos > 0, depth == 0))
     def _():
-        add_window(acc, pos_ref, spill_a0, 2 * left, True)
         add_window(acc, pos_ref, spill_b0, 2 * left + 1, True)
-
-    @pl.when(jnp.logical_and(pos > 0, depth != 0))
-    def _():
-        add_window(acc, pos_ref, spill_b1, 2 * left + 1, True)
 
     copies = []
     for c in range(2):
@@ -491,36 +497,38 @@
     barrier = lax.optimization_barrier
     psi_a = front(0, mine, first_a)
     g1_a, adj_a = tail(0, swapped, second_a, psi_a)
-    grads_a = call(back_a_kernel, "backa", [vmem] * 5, two, [pair] + packed)(
-        adj_a, g1_a, probe_at, kern, tables
+    spill_a1 = send("spill_a1", g1_a, rightward([(0, 1)]))
+    g0_a = call(back_a_kernel, "backa", [vmem] * 4, window, [pair] + packed)(
+        adj_a, probe_at, kern, tables
     )
-    spill_a = send("spill_a", grads_a, rightward([(0, 1)]))
-    first_b, grads_a = barrier((first_b, grads_a))
+    spill_a0 = send("spill_a0", g0_a, rightward([(0, 1)]))
+    first_b, g0_a = barrier((first_b, g0_a))
     psi_b = front(1, swapped, first_b)
     g1_b, adj_b = tail(1, mine, second_b, psi_b)
+    spill_b1 = send("spill_b1", g1_b, rightward([(1, 0)]))
     give = call(back_b_kernel, "backb", [vmem] * 5, window, [pair] + packed)(
         adj_b, g1_a, probe_at, kern, tables
     )
     spill_b0 = send("spill_b0", give, rightward([(1, 0)]))
-    g1_b, give = barrier((g1_b, give))
-    spill_b1 = send("spill_b1", g1_b, rightward([(1, 1)]))
     sums = jax.ShapeDtypeStruct((2, height, frame), F32)
-    total = call(begin_kernel, "begin", [vmem] * 3, sums, cost=HEAVY)(positions, grads_a, g1_b)
-    total, give, spill_a = barrier((total, give, spill_a))
+    total = call(begin_kernel, "begin", [vmem] * 3, sums)(positions, g0_a, g1_b)
+    total, give, spill_a1 = barrier((total, give, spill_a1))
+    total = call(add_kernel, "add", [vmem] * 3, sums, aliases={1: 0}, cost=MEDIUM)(
+        positions, total, spill_a1
+    )
+    total, give, spill_b1, spill_a0 = barrier((total, give, spill_b1, spill_a0))
     given = send("given", give, swap)
-    spill_a0 = send("spill_a0", spill_a[0], swap)
-    total = call(add_kernel, "add", [vmem] * 3, sums, aliases={1: 0}, cost=HEAVY)(
-        positions, total, spill_a
-    )
+    trade = call(trade_kernel, "trade", [vmem] * 2, window)(spill_b1, spill_a0)
+    traded = send("traded", trade, swap)
     out, _ = call(
         gather_kernel,
         "gather",
-        [vmem] * 6,
+        [vmem] * 5,
         (jax.ShapeDtypeStruct(object_field.shape, BF), sums),
         [pltpu.VMEM((2, height, frame), BF), pltpu.SemaphoreType.DMA((2, height // frame))],
         out_specs=(hbm, vmem),
         aliases={1: 1},
-    )(positions, total, spill_b0, spill_b1, spill_a0, given)
+    )(positions, total, spill_b0, traded, given)
     return out
 
 

time: 38.1 us -> 37.1 us (0.974)
  the two profiles are of different devices: /device:TPU:25 before, /device:TPU:24 now
where the time goes in v4:
time: 37.1 us; the launch traced here: 36.9 us
  starting transfers between devices  13.6 us (37%)
  Pallas kernels  11.7 us (32%)
  waiting for transfers between devices  10.3 us (28%)
  local copies, waits for them, and re-layouts  0.84 us (2%)
  between operations  0.41 us (1%)
    ppermute x11, starting transfers between devices, send(): return lax.ppermute(x, both, pairs)  13.6 us
    ppermute x11, waiting for transfers between devices, send(): return lax.ppermute(x, both, pairs)  10.3 us
    pallas_call x2, Pallas kernels, tail(): call(body, 'tail' + 'ab'[core], [vmem] * 6, (window, sums_of), deep)  2.78 us
    pallas_call x1, Pallas kernels, local(): call(gather_kernel, 'gather', [vmem] * 5, (jax.ShapeDtypeStruct(object_fi...  2.05 us
    pallas_call x2, Pallas kernels, front(): call(body, 'front' + 'ab'[core], [vmem] * 6, fields, [pair] + packed)  1.86 us
    pallas_call x1, Pallas kernels, local(): call(back_a_kernel, 'backa', [vmem] * 4, window, [pair] + packed)  1.57 us
    pallas_call x1, Pallas kernels, local(): call(extract_kernel, 'extract', [vmem, hbm], (window, window, window, two...  1.49 us
    pallas_call x1, Pallas kernels, local(): call(functools.partial(prepare_kernel, height), 'prepare', [vmem] * 4, (j...  1.45 us
  transfers between devices with their start and end apart: 11, of which 5 were waited for; matrix products, arithmetic and copies ran while one was open for 0% of the time, Pallas kernels for 22%

profile of v4, /device:TPU:24, one launch (start us, length us, event | category | flops | bytes accessed | tf_op | source)
XLA Modules:
  0.0 36.9 jit_solution(5268994122229214254)
XLA Ops:
  0.0 0.0 copy-start.2
  0.0 0.0 copy-start.3
  0.0 0.0 copy-start.1
  0.0 0.0 copy-start.4
  0.0 0.8 %copy-done.4 = s32[32,2]{0,1:T(2,128)S(1)} copy-done((s32[32,2]{0,1:T(2,128)S(1)}, s32[32,2]{0,1:T(2,128)}, u32[]{:S(2)}) %copy-start.4) | copy-done | bytes 280
  0.8 0.0 copy-start
  0.8 1.5 %extract.1 = (bf16[2,256,256]{2,1,0:T(8,128)(2,1)S(1)}, bf16[2,256,256]{2,1,0:T(8,128)(2,1)S(1)}, bf16[2,256,256]{2,1,0:T(8,128)(2,1)S(1)}, bf16[2,2,256,256]{3,2,1,0:T(8,128)(2,1)S(1)}) custom-call(s32[2,32]{1,0:T(2,128)S(1)} %bitcast.3, bf16[1,2,2048,256]{3,2,1,0:T(8,128)(2,1)} %obj_ref.1), custom_call_target="tpu_custom_call" | custom-call | flops 1000 | bytes 1000 | tf_op jit(solution)/shard_map/extract/pallas_call | solution.py:455
  2.3 0.1 collective-permute-start
  2.4 4.2 %collective-permute-start.3 = (bf16[2,256,256]{2,1,0:T(8,128)(2,1)S(1)}, bf16[2,256,256]{2,1,0:T(8,128)(2,1)S(1)}, u32[]{:S(2)}, u32[]{:S(2)}) collective-permute-start(bf16[2,256,256]{2,1,0:T(8,128)(2,1)S(1)} %get-tuple-element.33), channel_id=1, source_target_pairs={{1,0},{2,1},{3,2},{4,3},{5,4},{6,5},{7,6},{8,7},{9,8},{10,9},{11,1... | collective-permute-start | bytes 786440 | tf_op jit(solution)/shard_map/first_a/ppermute | solution.py:450
  6.7 1.3 %collective-permute-start.2 = (bf16[2,256,256]{2,1,0:T(8,128)(2,1)S(1)}, bf16[2,256,256]{2,1,0:T(8,128)(2,1)S(1)}, u32[]{:S(2)}, u32[]{:S(2)}) collective-permute-start(bf16[2,256,256]{2,1,0:T(8,128)(2,1)S(1)} %get-tuple-element.33), channel_id=1, source_target_pairs={{17,0},{18,1},{19,2},{20,3},{21,4},{22,5},{23,6},{24,7},{25,8},{26... | collective-permute-start | bytes 786440 | tf_op jit(solution)/shard_map/second_a/ppermute | solution.py:450
  8.0 0.0 collective-permute-done.own
  8.0 0.7 %collective-permute-start.1 = (bf16[2,256,256]{2,1,0:T(8,128)(2,1)S(1)}, bf16[2,256,256]{2,1,0:T(8,128)(2,1)S(1)}, u32[]{:S(2)}, u32[]{:S(2)}) collective-permute-start(bf16[2,256,256]{2,1,0:T(8,128)(2,1)S(1)} %slice_bitcast_fusion), channel_id=1, source_target_pairs={{17,16},{18,17},{19,18},{20,19},{21,20},{22,21},{23,22},{24,23},{2... | collective-permute-start | bytes 786440 | tf_op jit(solution)/shard_map/first_b/ppermute | solution.py:450
  8.7 0.7 %collective-permute-start.4 = (bf16[2,256,256]{2,1,0:T(8,128)(2,1)S(1)}, bf16[2,256,256]{2,1,0:T(8,128)(2,1)S(1)}, u32[]{:S(2)}, u32[]{:S(2)}) collective-permute-start(bf16[2,256,256]{2,1,0:T(8,128)(2,1)S(1)} %get-tuple-element.40), channel_id=1, source_target_pairs={{17,16},{18,17},{19,18},{20,19},{21,20},{22,21},{23,22},{24,23},{2... | collective-permute-start | bytes 786440 | tf_op jit(solution)/shard_map/second_b/ppermute | solution.py:450
  9.4 0.0 copy-done.2
  9.4 0.0 copy-done.3
  9.4 0.0 copy-done.1
  9.4 1.5 %prepare.1 = (bf16[4,2,256,256]{3,2,1,0:T(8,128)(2,1)S(1)}, f32[2,256,256]{2,1,0:T(8,128)S(1)}, f32[256,256]{1,0:T(8,128)S(1)}, s32[8,256]{1,0:T(8,128)S(1)}) custom-call(s32[2,32]{1,0:T(2,128)S(1)} %bitcast.4, bf16[4,2,256,256]{3,2,1,0:T(8,128)(2,1)S(1)} %copy-done.1, f32[256,256]{1,0:T(8,128)S(1)} %copy-done.3, f32[2,256,256]{2,1,0:T(8,128)S(1)} %copy-done.2), custom_call_target="tpu_custom_call" | custom-call | flops 1000 | bytes 1000 | tf_op jit(solution)/shard_map/prepare/pallas_call | solution.py:469
  10.9 0.5 %collective-permute-done.3.halo = bf16[2,256,256]{2,1,0:T(8,128)(2,1)S(1)} collective-permute-done((bf16[2,256,256]{2,1,0:T(8,128)(2,1)S(1)}, bf16[2,256,256]{2,1,0:T(8,128)(2,1)S(1)}, u32[]{:S(2)}, u32[]{:S(2)}) %collective-permute-start.3) | collective-permute-done | bytes 262176 | tf_op jit(solution)/shard_map/first_a/ppermute | solution.py:450
  11.4 0.0 copy-done
  11.4 1.8 %fronta.1.psi = f32[4,2,256,256]{3,2,1,0:T(8,128)S(1)} custom-call(s32[8,256]{1,0:T(8,128)S(1)} %get-tuple-element.32.shift, bf16[2,256,256]{2,1,0:T(8,128)(2,1)S(1)} %get-tuple-element.34.own, bf16[2,256,256]{2,1,0:T(8,128)(2,1)S(1)} %collective-permute-done.3.halo, bf16[4,2,256,256]{3,2,1,0:T(8,128)(2,1)S(1)} %get-tuple-element.35.probe, ...), custom_call_target="tpu_custom_call" | custom-call | flops 1000 | bytes 1000 | tf_op jit(solution)/shard_map/fronta/pallas_call | solution.py:487
  13.2 1.1 %collective-permute-done.2.halo = bf16[2,256,256]{2,1,0:T(8,128)(2,1)S(1)} collective-permute-done((bf16[2,256,256]{2,1,0:T(8,128)(2,1)S(1)}, bf16[2,256,256]{2,1,0:T(8,128)(2,1)S(1)}, u32[]{:S(2)}, u32[]{:S(2)}) %collective-permute-start.2) | collective-permute-done | bytes 262176 | tf_op jit(solution)/shard_map/second_a/ppermute | solution.py:450
  14.3 2.6 %taila.1 = (bf16[2,256,256]{2,1,0:T(8,128)(2,1)S(1)}, bf16[4,2,256,256]{3,2,1,0:T(8,128)(2,1)S(1)}) custom-call(s32[8,256]{1,0:T(8,128)S(1)} %get-tuple-element.32.shift, bf16[2,2,256,256]{3,2,1,0:T(8,128)(2,1)S(1)} %collective-permute-done.own, bf16[2,256,256]{2,1,0:T(8,128)(2,1)S(1)} %collective-permute-done.2.halo, f32[4,2,256,256]{3,2,1,0:T(8,128)S(1)} %fronta.1.psi, ...), custom_call_target="tpu_custom_call" | custom-call | flops 1000 | bytes 1000 | tf_op jit(solution)/shard_map/taila/pallas_call | solution.py:493
  16.9 2.2 %collective-permute-start.5 = (bf16[2,256,256]{2,1,0:T(8,128)(2,1)S(1)}, bf16[2,256,256]{2,1,0:T(8,128)(2,1)S(1)}, u32[]{:S(2)}, u32[]{:S(2)}) collective-permute-start(bf16[2,256,256]{2,1,0:T(8,128)(2,1)S(1)} %get-tuple-element.44.g1_a), channel_id=1, source_target_pairs={{0,17},{1,18},{2,19},{3,20},{4,21},{5,22},{6,23},{7,24},{8,25},{9,... | collective-permute-start | bytes 786440 | tf_op jit(solution)/shard_map/spill_a1/ppermute | solution.py:450
  19.1 1.6 %backa.1.g0_a = bf16[2,256,256]{2,1,0:T(8,128)(2,1)S(1)} custom-call(bf16[4,2,256,256]{3,2,1,0:T(8,128)(2,1)S(1)} %get-tuple-element.38.adj, bf16[4,2,256,256]{3,2,1,0:T(8,128)(2,1)S(1)} %get-tuple-element.35.probe, f32[2,256,256]{2,1,0:T(8,128)S(1)} %get-tuple-element.36.kern, bf16[4,256,256]{2,1,0:T(8,128)(2,1)S(1)} %copy-done), custom_call_target="tpu_custom_call" | custom-call | flops 1000 | bytes 1000 | tf_op jit(solution)/shard_map/backa/pallas_call | solution.py:501
  20.7 1.3 %collective-permute-start.7 = (bf16[2,256,256]{2,1,0:T(8,128)(2,1)S(1)}, bf16[2,256,256]{2,1,0:T(8,128)(2,1)S(1)}, u32[]{:S(2)}, u32[]{:S(2)}) collective-permute-start(bf16[2,256,256]{2,1,0:T(8,128)(2,1)S(1)} %backa.1.g0_a), channel_id=1, source_target_pairs={{0,17},{1,18},{2,19},{3,20},{4,21},{5,22},{6,23},{7,24},{8,25},{9,... | collective-permute-start | bytes 786440 | tf_op jit(solution)/shard_map/spill_a0/ppermute | solution.py:450
  22.0 0.0 collective-permute-done.1.halo
  22.0 0.0 collective-permute-done.4.halo
  22.0 0.2 tailb.1
  22.3 1.3 %collective-permute-start.6 = (bf16[2,256,256]{2,1,0:T(8,128)(2,1)S(1)}, bf16[2,256,256]{2,1,0:T(8,128)(2,1)S(1)}, u32[]{:S(2)}, u32[]{:S(2)}) collective-permute-start(bf16[2,256,256]{2,1,0:T(8,128)(2,1)S(1)} %get-tuple-element.42.g1_b), channel_id=1, source_target_pairs={{16,1},{17,2},{18,3},{19,4},{20,5},{21,6},{22,7},{23,8},{24,9},{25... | collective-permute-start | bytes 786440 | tf_op jit(solution)/shard_map/spill_b1/ppermute | solution.py:450
  23.6 1.3 %collective-permute-start.8 = (bf16[2,256,256]{2,1,0:T(8,128)(2,1)S(1)}, bf16[2,256,256]{2,1,0:T(8,128)(2,1)S(1)}, u32[]{:S(2)}, u32[]{:S(2)}) collective-permute-start(bf16[2,256,256]{2,1,0:T(8,128)(2,1)S(1)} %backb.1), channel_id=1, source_target_pairs={{16,1},{17,2},{18,3},{19,4},{20,5},{21,6},{22,7},{23,8},{24,9},{25... | collective-permute-start | bytes 786440 | tf_op jit(solution)/shard_map/spill_b0/ppermute | solution.py:450
  24.9 0.5 %begin.1.acc_in = f32[2,2048,256]{2,1,0:T(8,128)S(1)} custom-call(s32[2,32]{1,0:T(2,128)S(1)} %bitcast.5, bf16[2,256,256]{2,1,0:T(8,128)(2,1)S(1)} %backa.1.g0_a, bf16[2,256,256]{2,1,0:T(8,128)(2,1)S(1)} %get-tuple-element.42.g1_b), custom_call_target="tpu_custom_call" | custom-call | flops 1000 | bytes 1000 | tf_op jit(solution)/shard_map/begin/pallas_call | solution.py:514
  25.4 0.0 collective-permute-done.5.spill_a1
  25.4 0.5 %collective-permute-done.7.spill_a0 = bf16[2,256,256]{2,1,0:T(8,128)(2,1)S(1)} collective-permute-done((bf16[2,256,256]{2,1,0:T(8,128)(2,1)S(1)}, bf16[2,256,256]{2,1,0:T(8,128)(2,1)S(1)}, u32[]{:S(2)}, u32[]{:S(2)}) %collective-permute-start.7) | collective-permute-done | bytes 262176 | tf_op jit(solution)/shard_map/spill_a0/ppermute | solution.py:450
  25.9 5.9 %collective-permute-done.6.spill_b1 = bf16[2,256,256]{2,1,0:T(8,128)(2,1)S(1)} collective-permute-done((bf16[2,256,256]{2,1,0:T(8,128)(2,1)S(1)}, bf16[2,256,256]{2,1,0:T(8,128)(2,1)S(1)}, u32[]{:S(2)}, u32[]{:S(2)}) %collective-permute-start.6) | collective-permute-done | bytes 262176 | tf_op jit(solution)/shard_map/spill_b1/ppermute | solution.py:450
  31.8 0.1 collective-permute-start.9
  31.8 0.5 %collective-permute-start.10 = (bf16[2,256,256]{2,1,0:T(8,128)(2,1)S(1)}, bf16[2,256,256]{2,1,0:T(8,128)(2,1)S(1)}, u32[]{:S(2)}, u32[]{:S(2)}) collective-permute-start(bf16[2,256,256]{2,1,0:T(8,128)(2,1)S(1)} %backb.1), channel_id=1, source_target_pairs={{0,16},{1,17},{2,18},{3,19},{4,20},{5,21},{6,22},{7,23},{8,24},{9,... | collective-permute-start | bytes 786440 | tf_op jit(solution)/shard_map/given/ppermute | solution.py:450
  32.3 2.3 %collective-permute-done.8.spill_b0 = bf16[2,256,256]{2,1,0:T(8,128)(2,1)S(1)} collective-permute-done((bf16[2,256,256]{2,1,0:T(8,128)(2,1)S(1)}, bf16[2,256,256]{2,1,0:T(8,128)(2,1)S(1)}, u32[]{:S(2)}, u32[]{:S(2)}) %collective-permute-start.8) | collective-permute-done | bytes 262176 | tf_op jit(solution)/shard_map/spill_b0/ppermute | solution.py:450
  34.6 0.0 collective-permute-done.9.traded
  34.6 0.0 collective-permute-done.10.given
  34.6 2.0 %gather.1 = (bf16[1,2,2048,256]{3,2,1,0:T(8,128)(2,1)}, f32[2,2048,256]{2,1,0:T(8,128)S(1)}) custom-call(s32[2,32]{1,0:T(2,128)S(1)} %bitcast.7, f32[2,2048,256]{2,1,0:T(8,128)S(1)} %add.1.acc_in, bf16[2,256,256]{2,1,0:T(8,128)(2,1)S(1)} %collective-permute-done.8.spill_b0, ...), custom_call_target="tpu_custom_call", output_to_operand_aliasing={{1}: (1, {})} | custom-call | flops 1000 | bytes 1000 | tf_op jit(solution)/shard_map/gather/pallas_call | solution.py:523
  (5 shorter events, 0.1 us)
Async XLA Ops:
  0.0 9.4 %copy-start.2 = (f32[2,256,256]{2,1,0:T(8,128)S(1)}, f32[2,256,256]{2,1,0:T(8,128)}, u32[]{:S(2)}) copy-start(f32[2,256,256]{2,1,0:T(8,128)} %measured_ref.1) | copy-start | bytes 1572868
  0.0 9.4 %copy-start.3 = (f32[256,256]{1,0:T(8,128)S(1)}, f32[256,256]{1,0:T(8,128)}, u32[]{:S(2)}) copy-start(f32[256,256]{1,0:T(8,128)} %phase_ref.1) | copy-start | bytes 786436
  0.0 9.4 %copy-start.1 = (bf16[4,2,256,256]{3,2,1,0:T(8,128)(2,1)S(1)}, bf16[4,2,256,256]{3,2,1,0:T(8,128)(2,1)}, u32[]{:S(2)}) copy-start(bf16[4,2,256,256]{3,2,1,0:T(8,128)(2,1)} %probe_ref.1) | copy-start | bytes 3145732
  0.0 0.8 %copy-start.4 = (s32[32,2]{0,1:T(2,128)S(1)}, s32[32,2]{0,1:T(2,128)}, u32[]{:S(2)}) copy-start(s32[32,2]{0,1:T(2,128)} %param.10) | copy-start | bytes 772
  0.8 10.6 %copy-start = (bf16[4,256,256]{2,1,0:T(8,128)(2,1)S(1)}, bf16[4,256,256]{2,1,0:T(8,128)(2,1)}, u32[]{:S(2)}) copy-start(bf16[4,256,256]{2,1,0:T(8,128)(2,1)} %constant.2.clone.t) | copy-start | bytes 1572868
  2.3 5.6 %collective-permute-start = (bf16[2,2,256,256]{3,2,1,0:T(8,128)(2,1)S(1)}, bf16[2,2,256,256]{3,2,1,0:T(8,128)(2,1)S(1)}, u32[]{:S(2)}, u32[]{:S(2)}) collective-permute-start(bf16[2,2,256,256]{3,2,1,0:T(8,128)(2,1)S(1)} %get-tuple-element.30), channel_id=1, source_target_pairs={{0,16},{1,17},{2,18},{3,19},{4,20},{5,21},{6,22},{7,23},{8,24},{9,... | collective-permute-start | bytes 1572872 | tf_op jit(solution)/shard_map/swapped/ppermute | solution.py:450
  2.4 9.0 %collective-permute-start.3 = (bf16[2,256,256]{2,1,0:T(8,128)(2,1)S(1)}, bf16[2,256,256]{2,1,0:T(8,128)(2,1)S(1)}, u32[]{:S(2)}, u32[]{:S(2)}) collective-permute-start(bf16[2,256,256]{2,1,0:T(8,128)(2,1)S(1)} %get-tuple-element.33), channel_id=1, source_target_pairs={{1,0},{2,1},{3,2},{4,3},{5,4},{6,5},{7,6},{8,7},{9,8},{10,9},{11,1... | collective-permute-start | bytes 786440 | tf_op jit(solution)/shard_map/first_a/ppermute | solution.py:450
  6.7 7.7 %collective-permute-start.2 = (bf16[2,256,256]{2,1,0:T(8,128)(2,1)S(1)}, bf16[2,256,256]{2,1,0:T(8,128)(2,1)S(1)}, u32[]{:S(2)}, u32[]{:S(2)}) collective-permute-start(bf16[2,256,256]{2,1,0:T(8,128)(2,1)S(1)} %get-tuple-element.33), channel_id=1, source_target_pairs={{17,0},{18,1},{19,2},{20,3},{21,4},{22,5},{23,6},{24,7},{25,8},{26... | collective-permute-start | bytes 786440 | tf_op jit(solution)/shard_map/second_a/ppermute | solution.py:450
  8.0 14.0 %collective-permute-start.1 = (bf16[2,256,256]{2,1,0:T(8,128)(2,1)S(1)}, bf16[2,256,256]{2,1,0:T(8,128)(2,1)S(1)}, u32[]{:S(2)}, u32[]{:S(2)}) collective-permute-start(bf16[2,256,256]{2,1,0:T(8,128)(2,1)S(1)} %slice_bitcast_fusion), channel_id=1, source_target_pairs={{17,16},{18,17},{19,18},{20,19},{21,20},{22,21},{23,22},{24,23},{2... | collective-permute-start | bytes 786440 | tf_op jit(solution)/shard_map/first_b/ppermute | solution.py:450
  8.7 13.4 %collective-permute-start.4 = (bf16[2,256,256]{2,1,0:T(8,128)(2,1)S(1)}, bf16[2,256,256]{2,1,0:T(8,128)(2,1)S(1)}, u32[]{:S(2)}, u32[]{:S(2)}) collective-permute-start(bf16[2,256,256]{2,1,0:T(8,128)(2,1)S(1)} %get-tuple-element.40), channel_id=1, source_target_pairs={{17,16},{18,17},{19,18},{20,19},{21,20},{22,21},{23,22},{24,23},{2... | collective-permute-start | bytes 786440 | tf_op jit(solution)/shard_map/second_b/ppermute | solution.py:450
  16.9 8.4 %collective-permute-start.5 = (bf16[2,256,256]{2,1,0:T(8,128)(2,1)S(1)}, bf16[2,256,256]{2,1,0:T(8,128)(2,1)S(1)}, u32[]{:S(2)}, u32[]{:S(2)}) collective-permute-start(bf16[2,256,256]{2,1,0:T(8,128)(2,1)S(1)} %get-tuple-element.44.g1_a), channel_id=1, source_target_pairs={{0,17},{1,18},{2,19},{3,20},{4,21},{5,22},{6,23},{7,24},{8,25},{9,... | collective-permute-start | bytes 786440 | tf_op jit(solution)/shard_map/spill_a1/ppermute | solution.py:450
  20.7 5.2 %collective-permute-start.7 = (bf16[2,256,256]{2,1,0:T(8,128)(2,1)S(1)}, bf16[2,256,256]{2,1,0:T(8,128)(2,1)S(1)}, u32[]{:S(2)}, u32[]{:S(2)}) collective-permute-start(bf16[2,256,256]{2,1,0:T(8,128)(2,1)S(1)} %backa.1.g0_a), channel_id=1, source_target_pairs={{0,17},{1,18},{2,19},{3,20},{4,21},{5,22},{6,23},{7,24},{8,25},{9,... | collective-permute-start | bytes 786440 | tf_op jit(solution)/shard_map/spill_a0/ppermute | solution.py:450
  22.3 9.5 %collective-permute-start.6 = (bf16[2,256,256]{2,1,0:T(8,128)(2,1)S(1)}, bf16[2,256,256]{2,1,0:T(8,128)(2,1)S(1)}, u32[]{:S(2)}, u32[]{:S(2)}) collective-permute-start(bf16[2,256,256]{2,1,0:T(8,128)(2,1)S(1)} %get-tuple-element.42.g1_b), channel_id=1, source_target_pairs={{16,1},{17,2},{18,3},{19,4},{20,5},{21,6},{22,7},{23,8},{24,9},{25... | collective-permute-start | bytes 786440 | tf_op jit(solution)/shard_map/spill_b1/ppermute | solution.py:450
  23.6 11.0 %collective-permute-start.8 = (bf16[2,256,256]{2,1,0:T(8,128)(2,1)S(1)}, bf16[2,256,256]{2,1,0:T(8,128)(2,1)S(1)}, u32[]{:S(2)}, u32[]{:S(2)}) collective-permute-start(bf16[2,256,256]{2,1,0:T(8,128)(2,1)S(1)} %backb.1), channel_id=1, source_target_pairs={{16,1},{17,2},{18,3},{19,4},{20,5},{21,6},{22,7},{23,8},{24,9},{25... | collective-permute-start | bytes 786440 | tf_op jit(solution)/shard_map/spill_b0/ppermute | solution.py:450
  31.8 2.9 %collective-permute-start.9 = (bf16[2,256,256]{2,1,0:T(8,128)(2,1)S(1)}, bf16[2,256,256]{2,1,0:T(8,128)(2,1)S(1)}, u32[]{:S(2)}, u32[]{:S(2)}) collective-permute-start(bf16[2,256,256]{2,1,0:T(8,128)(2,1)S(1)} %trade.1), channel_id=1, source_target_pairs={{0,16},{1,17},{2,18},{3,19},{4,20},{5,21},{6,22},{7,23},{8,24},{9,... | collective-permute-start | bytes 786440 | tf_op jit(solution)/shard_map/traded/ppermute | solution.py:450
  31.8 2.8 %collective-permute-start.10 = (bf16[2,256,256]{2,1,0:T(8,128)(2,1)S(1)}, bf16[2,256,256]{2,1,0:T(8,128)(2,1)S(1)}, u32[]{:S(2)}, u32[]{:S(2)}) collective-permute-start(bf16[2,256,256]{2,1,0:T(8,128)(2,1)S(1)} %backb.1), channel_id=1, source_target_pairs={{0,16},{1,17},{2,18},{3,19},{4,20},{5,21},{6,22},{7,23},{8,24},{9,... | collective-permute-start | bytes 786440 | tf_op jit(solution)/shard_map/given/ppermute | solution.py:450

commit v5 on v4

--- a/solution.py
+++ b/solution.py
@@ -152,11 +152,13 @@
     return 1.0 - 2.0 * sine * sine, 2.0 * sine * cosine
 
 
-def prepare_kernel(height, pos_ref, probe_ref, phase_ref, measured_ref, probe_out, kern_out, measured_out, shift_out):
+def prepare_steps(
+    core, height, pos_ref, probe_ref, phase_ref, measured_ref, probe_out, kern_out, measured_out, shift_out
+):
     modes, _, frame, _ = probe_ref.shape
-    depth, pos, _ = indices()
+    _, pos, _ = indices()
     half = frame // 2
-    _, row_shift, col_shift = place(pos_ref, 2 * pos + depth, height, frame)
+    _, row_shift, col_shift = place(pos_ref, 2 * pos + core, height, frame)
     shift_out[...] = jnp.full(shift_out.shape, col_shift, jnp.int32)
     down = lax.broadcasted_iota(jnp.int32, (frame, frame), 0)
     across = lax.broadcasted_iota(jnp.int32, (frame, frame), 1)
@@ -185,7 +187,13 @@
         for c in range(2):
             plane = pltpu.roll(probe_ref[m, c].astype(F32), col_shift, 1).astype(BF)
             probe_out[m, c] = dot(turn, plane).astype(BF)
-    measured_out[...] = reorder(measured_ref[depth])
+    measured_out[...] = reorder(measured_ref[core])
+
+
+def prepare_kernel(core, *rest):
+    @pl.when(lax.axis_index("depth") == core)
+    def _():
+        prepare_steps(core, *rest)
 
 
 def join(shift, obj, own, halo):
@@ -466,17 +474,18 @@
     left_b, swapped = lax.optimization_barrier((left_b, swapped))
     first_b = send("first_b", swapped[0], leftward([(1, 1)]))
     second_b = send("second_b", left_b, leftward([(1, 1)]))
-    probe_at, kern, measured_at, shift = call(
-        functools.partial(prepare_kernel, height),
-        "prepare",
-        [vmem] * 4,
-        (
-            jax.ShapeDtypeStruct(probe.shape, BF),
-            jax.ShapeDtypeStruct((2, frame, frame), F32),
-            jax.ShapeDtypeStruct((frame, frame), F32),
-            jax.ShapeDtypeStruct((8, frame), jnp.int32),
-        ),
-    )(positions, probe, prop_phase, measured)
+    def prepare(core):
+        return call(
+            functools.partial(prepare_kernel, core, height),
+            "prepare" + "ab"[core],
+            [vmem] * 4,
+            (
+                jax.ShapeDtypeStruct(probe.shape, BF),
+                jax.ShapeDtypeStruct((2, frame, frame), F32),
+                jax.ShapeDtypeStruct((frame, frame), F32),
+                jax.ShapeDtypeStruct((8, frame), jnp.int32),
+            ),
+        )(positions, probe, prop_phase, measured)
 
     packed = [pltpu.VMEM((modes, 2, frame, frame), BF), pltpu.VMEM((modes, frame, 2 * frame), BF)]
     sums_of = jax.ShapeDtypeStruct((modes, 2, frame, frame), BF)
@@ -484,22 +493,25 @@
     deep = [pair, pltpu.VMEM(fields.shape, F32), pltpu.VMEM((frame, frame), F32), pair] + packed
     def front(core, own, halo):
         body = functools.partial(front_kernel, core)
+        probe_at, kern, _, shift = ready[core]
         return call(body, "front" + "ab"[core], [vmem] * 6, fields, [pair] + packed)(
             shift, own, halo, probe_at, kern, tables
         )
 
     def tail(core, own, halo, psi):
         body = functools.partial(tail_kernel, core)
+        _, _, measured_at, shift = ready[core]
         return call(body, "tail" + "ab"[core], [vmem] * 6, (window, sums_of), deep)(
             shift, own, halo, psi, measured_at, tables
         )
 
     barrier = lax.optimization_barrier
+    ready = [prepare(0), prepare(1)]
     psi_a = front(0, mine, first_a)
     g1_a, adj_a = tail(0, swapped, second_a, psi_a)
     spill_a1 = send("spill_a1", g1_a, rightward([(0, 1)]))
     g0_a = call(back_a_kernel, "backa", [vmem] * 4, window, [pair] + packed)(
-        adj_a, probe_at, kern, tables
+        adj_a, *ready[0][:2], tables
     )
     spill_a0 = send("spill_a0", g0_a, rightward([(0, 1)]))
     first_b, g0_a = barrier((first_b, g0_a))
@@ -507,7 +519,7 @@
     g1_b, adj_b = tail(1, mine, second_b, psi_b)
     spill_b1 = send("spill_b1", g1_b, rightward([(1, 0)]))
     give = call(back_b_kernel, "backb", [vmem] * 5, window, [pair] + packed)(
-        adj_b, g1_a, probe_at, kern, tables
+        adj_b, g1_a, *ready[1][:2], tables
     )
     spill_b0 = send("spill_b0", give, rightward([(1, 0)]))
     sums = jax.ShapeDtypeStruct((2, height, frame), F32)

time: 37.1 us -> 36.8 us (level)
  starting transfers between devices: 13.6 us -> 12.7 us
  waiting for transfers between devices: 10.3 us -> 10.8 us
    ppermute x11, starting transfers between devices: 13.6 us -> 12.7 us  [send(): return lax.ppermute(x, both, pairs)]
    ppermute x11, waiting for transfers between devices: 10.3 us -> 10.8 us  [send(): return lax.ppermute(x, both, pairs)]
    pallas_call x1 -> x2, Pallas kernels: 1.45 us -> 1.48 us  [prepare(): call(functools.partial(prepare_kernel, core, height), 'prepare' + 'ab'[co...]
  transfers between devices with their start and end apart: 11 -> 11, of which waited for: 5 -> 5; matrix products, arithmetic and copies ran while one was open for 0% -> 0% of each run, Pallas kernels for 22% -> 23%
where the time goes in v5:
time: 36.8 us; the launch traced here: 36.6 us
  starting transfers between devices  12.7 us (35%)
  Pallas kernels  11.8 us (32%)
  waiting for transfers between devices  10.8 us (29%)
  local copies, waits for them, and re-layouts  0.84 us (2%)
  between operations  0.42 us (1%)
    ppermute x11, starting transfers between devices, send(): return lax.ppermute(x, both, pairs)  12.7 us
    ppermute x11, waiting for transfers between devices, send(): return lax.ppermute(x, both, pairs)  10.8 us
    pallas_call x2, Pallas kernels, tail(): call(body, 'tail' + 'ab'[core], [vmem] * 6, (window, sums_of), deep)  2.78 us
    pallas_call x1, Pallas kernels, local(): call(gather_kernel, 'gather', [vmem] * 5, (jax.ShapeDtypeStruct(object_fi...  2.05 us
    pallas_call x2, Pallas kernels, front(): call(body, 'front' + 'ab'[core], [vmem] * 6, fields, [pair] + packed)  1.86 us
    pallas_call x1, Pallas kernels, local(): call(back_a_kernel, 'backa', [vmem] * 4, window, [pair] + packed)  1.57 us
    pallas_call x1, Pallas kernels, local(): call(extract_kernel, 'extract', [vmem, hbm], (window, window, window, two...  1.49 us
    pallas_call x2, Pallas kernels, prepare(): call(functools.partial(prepare_kernel, core, height), 'prepare' + 'ab'[co...  1.48 us
  transfers between devices with their start and end apart: 11, of which 5 were waited for; matrix products, arithmetic and copies ran while one was open for 0% of the time, Pallas kernels for 23%

profile of v5, /device:TPU:24, one launch (start us, length us, event | category | flops | bytes accessed | tf_op | source)
XLA Modules:
  0.0 36.6 jit_solution(5890255663251611517)
XLA Ops:
  0.0 0.0 copy-start.2
  0.0 0.0 copy-start.3
  0.0 0.0 copy-start.1
  0.0 0.0 copy-start.4
  0.0 0.8 %copy-done.4 = s32[32,2]{0,1:T(2,128)S(1)} copy-done((s32[32,2]{0,1:T(2,128)S(1)}, s32[32,2]{0,1:T(2,128)}, u32[]{:S(2)}) %copy-start.4) | copy-done | bytes 280
  0.8 0.0 copy-start
  0.8 1.5 %extract.1 = (bf16[2,256,256]{2,1,0:T(8,128)(2,1)S(1)}, bf16[2,256,256]{2,1,0:T(8,128)(2,1)S(1)}, bf16[2,256,256]{2,1,0:T(8,128)(2,1)S(1)}, bf16[2,2,256,256]{3,2,1,0:T(8,128)(2,1)S(1)}) custom-call(s32[2,32]{1,0:T(2,128)S(1)} %bitcast.3, bf16[1,2,2048,256]{3,2,1,0:T(8,128)(2,1)} %obj_ref.1), custom_call_target="tpu_custom_call" | custom-call | flops 1000 | bytes 1000 | tf_op jit(solution)/shard_map/extract/pallas_call | solution.py:463
  2.3 0.1 collective-permute-start
  2.4 4.2 %collective-permute-start.3 = (bf16[2,256,256]{2,1,0:T(8,128)(2,1)S(1)}, bf16[2,256,256]{2,1,0:T(8,128)(2,1)S(1)}, u32[]{:S(2)}, u32[]{:S(2)}) collective-permute-start(bf16[2,256,256]{2,1,0:T(8,128)(2,1)S(1)} %get-tuple-element.37), channel_id=1, source_target_pairs={{1,0},{2,1},{3,2},{4,3},{5,4},{6,5},{7,6},{8,7},{9,8},{10,9},{11,1... | collective-permute-start | bytes 786440 | tf_op jit(solution)/shard_map/first_a/ppermute | solution.py:458
  6.7 1.3 %collective-permute-start.2 = (bf16[2,256,256]{2,1,0:T(8,128)(2,1)S(1)}, bf16[2,256,256]{2,1,0:T(8,128)(2,1)S(1)}, u32[]{:S(2)}, u32[]{:S(2)}) collective-permute-start(bf16[2,256,256]{2,1,0:T(8,128)(2,1)S(1)} %get-tuple-element.37), channel_id=1, source_target_pairs={{17,0},{18,1},{19,2},{20,3},{21,4},{22,5},{23,6},{24,7},{25,8},{26... | collective-permute-start | bytes 786440 | tf_op jit(solution)/shard_map/second_a/ppermute | solution.py:458
  8.0 0.0 collective-permute-done.own
  8.0 0.7 %collective-permute-start.1 = (bf16[2,256,256]{2,1,0:T(8,128)(2,1)S(1)}, bf16[2,256,256]{2,1,0:T(8,128)(2,1)S(1)}, u32[]{:S(2)}, u32[]{:S(2)}) collective-permute-start(bf16[2,256,256]{2,1,0:T(8,128)(2,1)S(1)} %slice_bitcast_fusion), channel_id=1, source_target_pairs={{17,16},{18,17},{19,18},{20,19},{21,20},{22,21},{23,22},{24,23},{2... | collective-permute-start | bytes 786440 | tf_op jit(solution)/shard_map/first_b/ppermute | solution.py:458
  8.7 0.7 %collective-permute-start.4 = (bf16[2,256,256]{2,1,0:T(8,128)(2,1)S(1)}, bf16[2,256,256]{2,1,0:T(8,128)(2,1)S(1)}, u32[]{:S(2)}, u32[]{:S(2)}) collective-permute-start(bf16[2,256,256]{2,1,0:T(8,128)(2,1)S(1)} %get-tuple-element.45), channel_id=1, source_target_pairs={{17,16},{18,17},{19,18},{20,19},{21,20},{22,21},{23,22},{24,23},{2... | collective-permute-start | bytes 786440 | tf_op jit(solution)/shard_map/second_b/ppermute | solution.py:458
  9.4 0.0 copy-done.2
  9.4 0.0 copy-done.3
  9.4 0.0 copy-done.1
  9.4 1.5 %preparea.1 = (bf16[4,2,256,256]{3,2,1,0:T(8,128)(2,1)S(1)}, f32[2,256,256]{2,1,0:T(8,128)S(1)}, f32[256,256]{1,0:T(8,128)S(1)}, s32[8,256]{1,0:T(8,128)S(1)}) custom-call(s32[2,32]{1,0:T(2,128)S(1)} %bitcast.4, bf16[4,2,256,256]{3,2,1,0:T(8,128)(2,1)S(1)} %copy-done.1, f32[256,256]{1,0:T(8,128)S(1)} %copy-done.3, f32[2,256,256]{2,1,0:T(8,128)S(1)} %copy-done.2), custom_call_target="tpu_custom_call" | custom-call | flops 1000 | bytes 1000 | tf_op jit(solution)/shard_map/preparea/pallas_call | solution.py:478
  10.9 0.5 %collective-permute-done.3.halo = bf16[2,256,256]{2,1,0:T(8,128)(2,1)S(1)} collective-permute-done((bf16[2,256,256]{2,1,0:T(8,128)(2,1)S(1)}, bf16[2,256,256]{2,1,0:T(8,128)(2,1)S(1)}, u32[]{:S(2)}, u32[]{:S(2)}) %collective-permute-start.3) | collective-permute-done | bytes 262176 | tf_op jit(solution)/shard_map/first_a/ppermute | solution.py:458
  11.4 0.0 copy-done
  11.4 1.8 %fronta.1.psi = f32[4,2,256,256]{3,2,1,0:T(8,128)S(1)} custom-call(s32[8,256]{1,0:T(8,128)S(1)} %get-tuple-element.36.shift, bf16[2,256,256]{2,1,0:T(8,128)(2,1)S(1)} %get-tuple-element.38.own, bf16[2,256,256]{2,1,0:T(8,128)(2,1)S(1)} %collective-permute-done.3.halo, bf16[4,2,256,256]{3,2,1,0:T(8,128)(2,1)S(1)} %get-tuple-element.39.probe, ...), custom_call_target="tpu_custom_call" | custom-call | flops 1000 | bytes 1000 | tf_op jit(solution)/shard_map/fronta/pallas_call | solution.py:497
  13.2 1.1 %collective-permute-done.2.halo = bf16[2,256,256]{2,1,0:T(8,128)(2,1)S(1)} collective-permute-done((bf16[2,256,256]{2,1,0:T(8,128)(2,1)S(1)}, bf16[2,256,256]{2,1,0:T(8,128)(2,1)S(1)}, u32[]{:S(2)}, u32[]{:S(2)}) %collective-permute-start.2) | collective-permute-done | bytes 262176 | tf_op jit(solution)/shard_map/second_a/ppermute | solution.py:458
  14.3 2.6 %taila.1 = (bf16[2,256,256]{2,1,0:T(8,128)(2,1)S(1)}, bf16[4,2,256,256]{3,2,1,0:T(8,128)(2,1)S(1)}) custom-call(s32[8,256]{1,0:T(8,128)S(1)} %get-tuple-element.36.shift, bf16[2,2,256,256]{3,2,1,0:T(8,128)(2,1)S(1)} %collective-permute-done.own, bf16[2,256,256]{2,1,0:T(8,128)(2,1)S(1)} %collective-permute-done.2.halo, f32[4,2,256,256]{3,2,1,0:T(8,128)S(1)} %fronta.1.psi, ...), custom_call_target="tpu_custom_call" | custom-call | flops 1000 | bytes 1000 | tf_op jit(solution)/shard_map/taila/pallas_call | solution.py:504
  16.9 1.3 %collective-permute-start.5 = (bf16[2,256,256]{2,1,0:T(8,128)(2,1)S(1)}, bf16[2,256,256]{2,1,0:T(8,128)(2,1)S(1)}, u32[]{:S(2)}, u32[]{:S(2)}) collective-permute-start(bf16[2,256,256]{2,1,0:T(8,128)(2,1)S(1)} %get-tuple-element.52.g1_a), channel_id=1, source_target_pairs={{0,17},{1,18},{2,19},{3,20},{4,21},{5,22},{6,23},{7,24},{8,25},{9,... | collective-permute-start | bytes 786440 | tf_op jit(solution)/shard_map/spill_a1/ppermute | solution.py:458
  18.3 1.6 %backa.1.g0_a = bf16[2,256,256]{2,1,0:T(8,128)(2,1)S(1)} custom-call(bf16[4,2,256,256]{3,2,1,0:T(8,128)(2,1)S(1)} %get-tuple-element.42.adj, bf16[4,2,256,256]{3,2,1,0:T(8,128)(2,1)S(1)} %get-tuple-element.39.probe, f32[2,256,256]{2,1,0:T(8,128)S(1)} %get-tuple-element.40.kern, bf16[4,256,256]{2,1,0:T(8,128)(2,1)S(1)} %copy-done), custom_call_target="tpu_custom_call" | custom-call | flops 1000 | bytes 1000 | tf_op jit(solution)/shard_map/backa/pallas_call | solution.py:513
  19.9 1.3 %collective-permute-start.7 = (bf16[2,256,256]{2,1,0:T(8,128)(2,1)S(1)}, bf16[2,256,256]{2,1,0:T(8,128)(2,1)S(1)}, u32[]{:S(2)}, u32[]{:S(2)}) collective-permute-start(bf16[2,256,256]{2,1,0:T(8,128)(2,1)S(1)} %backa.1.g0_a), channel_id=1, source_target_pairs={{0,17},{1,18},{2,19},{3,20},{4,21},{5,22},{6,23},{7,24},{8,25},{9,... | collective-permute-start | bytes 786440 | tf_op jit(solution)/shard_map/spill_a0/ppermute | solution.py:458
  21.2 0.0 collective-permute-done.1.halo
  21.2 0.0 collective-permute-done.4.halo
  21.2 0.2 tailb.1
  21.4 1.3 %collective-permute-start.6 = (bf16[2,256,256]{2,1,0:T(8,128)(2,1)S(1)}, bf16[2,256,256]{2,1,0:T(8,128)(2,1)S(1)}, u32[]{:S(2)}, u32[]{:S(2)}) collective-permute-start(bf16[2,256,256]{2,1,0:T(8,128)(2,1)S(1)} %get-tuple-element.50.g1_b), channel_id=1, source_target_pairs={{16,1},{17,2},{18,3},{19,4},{20,5},{21,6},{22,7},{23,8},{24,9},{25... | collective-permute-start | bytes 786440 | tf_op jit(solution)/shard_map/spill_b1/ppermute | solution.py:458
  22.8 1.3 %collective-permute-start.8 = (bf16[2,256,256]{2,1,0:T(8,128)(2,1)S(1)}, bf16[2,256,256]{2,1,0:T(8,128)(2,1)S(1)}, u32[]{:S(2)}, u32[]{:S(2)}) collective-permute-start(bf16[2,256,256]{2,1,0:T(8,128)(2,1)S(1)} %backb.1), channel_id=1, source_target_pairs={{16,1},{17,2},{18,3},{19,4},{20,5},{21,6},{22,7},{23,8},{24,9},{25... | collective-permute-start | bytes 786440 | tf_op jit(solution)/shard_map/spill_b0/ppermute | solution.py:458
  24.1 0.5 %begin.1.acc_in = f32[2,2048,256]{2,1,0:T(8,128)S(1)} custom-call(s32[2,32]{1,0:T(2,128)S(1)} %bitcast.6, bf16[2,256,256]{2,1,0:T(8,128)(2,1)S(1)} %backa.1.g0_a, bf16[2,256,256]{2,1,0:T(8,128)(2,1)S(1)} %get-tuple-element.50.g1_b), custom_call_target="tpu_custom_call" | custom-call | flops 1000 | bytes 1000 | tf_op jit(solution)/shard_map/begin/pallas_call | solution.py:526
  24.5 0.0 collective-permute-done.5.spill_a1
  24.6 0.5 %collective-permute-done.7.spill_a0 = bf16[2,256,256]{2,1,0:T(8,128)(2,1)S(1)} collective-permute-done((bf16[2,256,256]{2,1,0:T(8,128)(2,1)S(1)}, bf16[2,256,256]{2,1,0:T(8,128)(2,1)S(1)}, u32[]{:S(2)}, u32[]{:S(2)}) %collective-permute-start.7) | collective-permute-done | bytes 262176 | tf_op jit(solution)/shard_map/spill_a0/ppermute | solution.py:458
  25.0 6.5 %collective-permute-done.6.spill_b1 = bf16[2,256,256]{2,1,0:T(8,128)(2,1)S(1)} collective-permute-done((bf16[2,256,256]{2,1,0:T(8,128)(2,1)S(1)}, bf16[2,256,256]{2,1,0:T(8,128)(2,1)S(1)}, u32[]{:S(2)}, u32[]{:S(2)}) %collective-permute-start.6) | collective-permute-done | bytes 262176 | tf_op jit(solution)/shard_map/spill_b1/ppermute | solution.py:458
  31.6 0.1 collective-permute-start.9
  31.7 0.5 %collective-permute-start.10 = (bf16[2,256,256]{2,1,0:T(8,128)(2,1)S(1)}, bf16[2,256,256]{2,1,0:T(8,128)(2,1)S(1)}, u32[]{:S(2)}, u32[]{:S(2)}) collective-permute-start(bf16[2,256,256]{2,1,0:T(8,128)(2,1)S(1)} %backb.1), channel_id=1, source_target_pairs={{0,16},{1,17},{2,18},{3,19},{4,20},{5,21},{6,22},{7,23},{8,24},{9,... | collective-permute-start | bytes 786440 | tf_op jit(solution)/shard_map/given/ppermute | solution.py:458
  32.2 2.2 %collective-permute-done.8.spill_b0 = bf16[2,256,256]{2,1,0:T(8,128)(2,1)S(1)} collective-permute-done((bf16[2,256,256]{2,1,0:T(8,128)(2,1)S(1)}, bf16[2,256,256]{2,1,0:T(8,128)(2,1)S(1)}, u32[]{:S(2)}, u32[]{:S(2)}) %collective-permute-start.8) | collective-permute-done | bytes 262176 | tf_op jit(solution)/shard_map/spill_b0/ppermute | solution.py:458
  34.4 0.0 collective-permute-done.9.traded
  34.4 0.0 collective-permute-done.10.given
  34.4 2.0 %gather.1 = (bf16[1,2,2048,256]{3,2,1,0:T(8,128)(2,1)}, f32[2,2048,256]{2,1,0:T(8,128)S(1)}) custom-call(s32[2,32]{1,0:T(2,128)S(1)} %bitcast.8, f32[2,2048,256]{2,1,0:T(8,128)S(1)} %add.1.acc_in, bf16[2,256,256]{2,1,0:T(8,128)(2,1)S(1)} %collective-permute-done.8.spill_b0, ...), custom_call_target="tpu_custom_call", output_to_operand_aliasing={{1}: (1, {})} | custom-call | flops 1000 | bytes 1000 | tf_op jit(solution)/shard_map/gather/pallas_call | solution.py:535
  (6 shorter events, 0.1 us)
Async XLA Ops:
  0.0 9.4 %copy-start.2 = (f32[2,256,256]{2,1,0:T(8,128)S(1)}, f32[2,256,256]{2,1,0:T(8,128)}, u32[]{:S(2)}) copy-start(f32[2,256,256]{2,1,0:T(8,128)} %rest_3_.3) | copy-start | bytes 1572868
  0.0 9.4 %copy-start.3 = (f32[256,256]{1,0:T(8,128)S(1)}, f32[256,256]{1,0:T(8,128)}, u32[]{:S(2)}) copy-start(f32[256,256]{1,0:T(8,128)} %rest_2_.3) | copy-start | bytes 786436
  0.0 9.4 %copy-start.1 = (bf16[4,2,256,256]{3,2,1,0:T(8,128)(2,1)S(1)}, bf16[4,2,256,256]{3,2,1,0:T(8,128)(2,1)}, u32[]{:S(2)}) copy-start(bf16[4,2,256,256]{3,2,1,0:T(8,128)(2,1)} %rest_1_.3) | copy-start | bytes 3145732
  0.0 0.8 %copy-start.4 = (s32[32,2]{0,1:T(2,128)S(1)}, s32[32,2]{0,1:T(2,128)}, u32[]{:S(2)}) copy-start(s32[32,2]{0,1:T(2,128)} %param.10) | copy-start | bytes 772
  0.8 10.6 %copy-start = (bf16[4,256,256]{2,1,0:T(8,128)(2,1)S(1)}, bf16[4,256,256]{2,1,0:T(8,128)(2,1)}, u32[]{:S(2)}) copy-start(bf16[4,256,256]{2,1,0:T(8,128)(2,1)} %constant.2.clone.t) | copy-start | bytes 1572868
  2.3 5.6 %collective-permute-start = (bf16[2,2,256,256]{3,2,1,0:T(8,128)(2,1)S(1)}, bf16[2,2,256,256]{3,2,1,0:T(8,128)(2,1)S(1)}, u32[]{:S(2)}, u32[]{:S(2)}) collective-permute-start(bf16[2,2,256,256]{3,2,1,0:T(8,128)(2,1)S(1)} %get-tuple-element.34), channel_id=1, source_target_pairs={{0,16},{1,17},{2,18},{3,19},{4,20},{5,21},{6,22},{7,23},{8,24},{9,... | collective-permute-start | bytes 1572872 | tf_op jit(solution)/shard_map/swapped/ppermute | solution.py:458
  2.4 9.0 %collective-permute-start.3 = (bf16[2,256,256]{2,1,0:T(8,128)(2,1)S(1)}, bf16[2,256,256]{2,1,0:T(8,128)(2,1)S(1)}, u32[]{:S(2)}, u32[]{:S(2)}) collective-permute-start(bf16[2,256,256]{2,1,0:T(8,128)(2,1)S(1)} %get-tuple-element.37), channel_id=1, source_target_pairs={{1,0},{2,1},{3,2},{4,3},{5,4},{6,5},{7,6},{8,7},{9,8},{10,9},{11,1... | collective-permute-start | bytes 786440 | tf_op jit(solution)/shard_map/first_a/ppermute | solution.py:458
  6.7 7.7 %collective-permute-start.2 = (bf16[2,256,256]{2,1,0:T(8,128)(2,1)S(1)}, bf16[2,256,256]{2,1,0:T(8,128)(2,1)S(1)}, u32[]{:S(2)}, u32[]{:S(2)}) collective-permute-start(bf16[2,256,256]{2,1,0:T(8,128)(2,1)S(1)} %get-tuple-element.37), channel_id=1, source_target_pairs={{17,0},{18,1},{19,2},{20,3},{21,4},{22,5},{23,6},{24,7},{25,8},{26... | collective-permute-start | bytes 786440 | tf_op jit(solution)/shard_map/second_a/ppermute | solution.py:458
  8.0 13.2 %collective-permute-start.1 = (bf16[2,256,256]{2,1,0:T(8,128)(2,1)S(1)}, bf16[2,256,256]{2,1,0:T(8,128)(2,1)S(1)}, u32[]{:S(2)}, u32[]{:S(2)}) collective-permute-start(bf16[2,256,256]{2,1,0:T(8,128)(2,1)S(1)} %slice_bitcast_fusion), channel_id=1, source_target_pairs={{17,16},{18,17},{19,18},{20,19},{21,20},{22,21},{23,22},{24,23},{2... | collective-permute-start | bytes 786440 | tf_op jit(solution)/shard_map/first_b/ppermute | solution.py:458
  8.7 12.5 %collective-permute-start.4 = (bf16[2,256,256]{2,1,0:T(8,128)(2,1)S(1)}, bf16[2,256,256]{2,1,0:T(8,128)(2,1)S(1)}, u32[]{:S(2)}, u32[]{:S(2)}) collective-permute-start(bf16[2,256,256]{2,1,0:T(8,128)(2,1)S(1)} %get-tuple-element.45), channel_id=1, source_target_pairs={{17,16},{18,17},{19,18},{20,19},{21,20},{22,21},{23,22},{24,23},{2... | collective-permute-start | bytes 786440 | tf_op jit(solution)/shard_map/second_b/ppermute | solution.py:458
  16.9 7.6 %collective-permute-start.5 = (bf16[2,256,256]{2,1,0:T(8,128)(2,1)S(1)}, bf16[2,256,256]{2,1,0:T(8,128)(2,1)S(1)}, u32[]{:S(2)}, u32[]{:S(2)}) collective-permute-start(bf16[2,256,256]{2,1,0:T(8,128)(2,1)S(1)} %get-tuple-element.52.g1_a), channel_id=1, source_target_pairs={{0,17},{1,18},{2,19},{3,20},{4,21},{5,22},{6,23},{7,24},{8,25},{9,... | collective-permute-start | bytes 786440 | tf_op jit(solution)/shard_map/spill_a1/ppermute | solution.py:458
  19.9 5.2 %collective-permute-start.7 = (bf16[2,256,256]{2,1,0:T(8,128)(2,1)S(1)}, bf16[2,256,256]{2,1,0:T(8,128)(2,1)S(1)}, u32[]{:S(2)}, u32[]{:S(2)}) collective-permute-start(bf16[2,256,256]{2,1,0:T(8,128)(2,1)S(1)} %backa.1.g0_a), channel_id=1, source_target_pairs={{0,17},{1,18},{2,19},{3,20},{4,21},{5,22},{6,23},{7,24},{8,25},{9,... | collective-permute-start | bytes 786440 | tf_op jit(solution)/shard_map/spill_a0/ppermute | solution.py:458
  21.4 10.1 %collective-permute-start.6 = (bf16[2,256,256]{2,1,0:T(8,128)(2,1)S(1)}, bf16[2,256,256]{2,1,0:T(8,128)(2,1)S(1)}, u32[]{:S(2)}, u32[]{:S(2)}) collective-permute-start(bf16[2,256,256]{2,1,0:T(8,128)(2,1)S(1)} %get-tuple-element.50.g1_b), channel_id=1, source_target_pairs={{16,1},{17,2},{18,3},{19,4},{20,5},{21,6},{22,7},{23,8},{24,9},{25... | collective-permute-start | bytes 786440 | tf_op jit(solution)/shard_map/spill_b1/ppermute | solution.py:458
  22.8 11.6 %collective-permute-start.8 = (bf16[2,256,256]{2,1,0:T(8,128)(2,1)S(1)}, bf16[2,256,256]{2,1,0:T(8,128)(2,1)S(1)}, u32[]{:S(2)}, u32[]{:S(2)}) collective-permute-start(bf16[2,256,256]{2,1,0:T(8,128)(2,1)S(1)} %backb.1), channel_id=1, source_target_pairs={{16,1},{17,2},{18,3},{19,4},{20,5},{21,6},{22,7},{23,8},{24,9},{25... | collective-permute-start | bytes 786440 | tf_op jit(solution)/shard_map/spill_b0/ppermute | solution.py:458
  31.6 2.8 %collective-permute-start.9 = (bf16[2,256,256]{2,1,0:T(8,128)(2,1)S(1)}, bf16[2,256,256]{2,1,0:T(8,128)(2,1)S(1)}, u32[]{:S(2)}, u32[]{:S(2)}) collective-permute-start(bf16[2,256,256]{2,1,0:T(8,128)(2,1)S(1)} %trade.1), channel_id=1, source_target_pairs={{0,16},{1,17},{2,18},{3,19},{4,20},{5,21},{6,22},{7,23},{8,24},{9,... | collective-permute-start | bytes 786440 | tf_op jit(solution)/shard_map/traded/ppermute | solution.py:458
  31.7 2.7 %collective-permute-start.10 = (bf16[2,256,256]{2,1,0:T(8,128)(2,1)S(1)}, bf16[2,256,256]{2,1,0:T(8,128)(2,1)S(1)}, u32[]{:S(2)}, u32[]{:S(2)}) collective-permute-start(bf16[2,256,256]{2,1,0:T(8,128)(2,1)S(1)} %backb.1), channel_id=1, source_target_pairs={{0,16},{1,17},{2,18},{3,19},{4,20},{5,21},{6,22},{7,23},{8,24},{9,... | collective-permute-start | bytes 786440 | tf_op jit(solution)/shard_map/given/ppermute | solution.py:458
